TPU v7x, 32 devices: a whole 2x2x4 slice. The times are simulated.
32 devices in a mesh: rows: 16 (over z, y, x), sub: 2 (over core).
Axes of the slice: x: 2, y: 2, z: 4, core: 2. Of those that a mesh axis runs over, the one named last changes fastest.
Arguments:
- affinity: bfloat16 [256, 3, 256, 256], P(('rows', 'sub')), may hold values from 0.0099487305 to 1
- old_basis: bfloat16 [65536, 64], P(('rows', 'sub')), may hold values from -1500 to 1500, as said below
- degrees: int32 [65536], P(('rows', 'sub')), may hold values from 10 to 90
- column_blocks: int32 [256, 3], P(('rows', 'sub')), may hold values from 0 to 255, as said below
- reorder: int32 [256, 256], P(('rows', 'sub')), may hold values from 0 to 255, each once within a row
Outputs:
- targets: float32 [65536, 64], P(('rows', 'sub'))
Inputs may be any that keep to these rules, and one draw needn't show every extreme that they name: column_blocks[b, 0] = b; the other entries of row b are distinct, differ from b and lie within 2 of b; block row 0 names block 2. `old_basis`: entries of magnitude up to 1500.
All inputs are finite; a program needn't handle non-finite values.
Results may differ from a plain program's by a relative error of at most 0.0035.
Values may be sent and summed in bfloat16 or wider, within the bound.
No kernel may reach another device: no remote copies, remote signals or barrier semaphores. Data moves between devices by JAX's collectives and lax.ppermute only.
A program may use at most 64 MiB of HBM per device.

v0:
```python
import math

import jax
import jax.numpy as jnp
from jax import lax
from jax.sharding import PartitionSpec as P

REACH = 2


def with_halo(cells, sides, width):
    for axis, dim in sides:
        count = lax.axis_size(axis)
        ends = count - 1
        head = lax.slice_in_dim(cells, 0, width, axis=dim)
        tail = lax.slice_in_dim(cells, cells.shape[dim] - width, cells.shape[dim], axis=dim)
        cells = jnp.concatenate(
            [
                lax.ppermute(tail, axis, [(i, (i + 1) % count) for i in range(ends)]),
                cells,
                lax.ppermute(head, axis, [((i + 1) % count, i) for i in range(ends)]),
            ],
            axis=dim,
        )
    return cells


def body(affinity, old_basis, degrees, column_blocks, reorder):
    count = affinity.shape[0]
    block = affinity.shape[-1]
    rows_here = old_basis.shape[0]
    width = REACH * block
    inverse_root = lax.rsqrt(degrees.astype(jnp.float32))[:, None]
    scaled = (inverse_root * old_basis.astype(jnp.float32)).astype(jnp.bfloat16)
    extended = with_halo(scaled, ((("rows", "sub"), 0),), width)
    ext_blocks = extended.reshape(count + 2 * REACH, block, -1)
    first_local = lax.axis_index(("rows", "sub")) * count - REACH
    fetched = ext_blocks[column_blocks - first_local]
    product = jnp.einsum("bkij,bkjr->bir", affinity, fetched, preferred_element_type=jnp.float32)
    image_rows = product.reshape(rows_here, -1) * inverse_root
    gram_local = jnp.einsum(
        "ir,is->rs",
        image_rows,
        image_rows,
        precision=lax.Precision.HIGHEST,
        preferred_element_type=jnp.float32,
    )
    gram_whole = lax.psum(gram_local, ("rows", "sub"))
    lower_factor = jnp.linalg.cholesky(gram_whole)
    solved = lax.linalg.triangular_solve(lower_factor, image_rows.T, left_side=True, lower=True)
    total_items = rows_here * lax.axis_size("rows") * lax.axis_size("sub")
    clustered = (solved.T * math.sqrt(total_items)).reshape(count, block, -1)
    targets = jnp.take_along_axis(clustered, reorder[:, :, None], axis=1)
    return targets.reshape(rows_here, -1)


def solution(mesh):
    placed = (
        P(("rows", "sub"), None, None, None),
        P(("rows", "sub"), None),
        P(("rows", "sub")),
        P(("rows", "sub"), None),
        P(("rows", "sub"), None),
    )
    return jax.shard_map(
        body, mesh=mesh, in_specs=placed, out_specs=P(("rows", "sub"), None), check_vma=False
    )
```

profile of v0, /device:TPU:0, one launch (start us, length us, event | category | flops | bytes accessed | tf_op | source)
XLA Modules:
  0.0 115.6 jit_solution(14248737578041199506)
XLA Ops:
  0.0 0.0 copy-start
  0.0 0.9 convert_rsqrt_fusion
  0.9 1.1 multiply_convert_fusion
  2.0 0.7 fusion.6
  2.6 2.3 %collective-permute-start = (bf16[512,64]{0,1:T(8,128)(2,1)}, bf16[512,64]{0,1:T(8,128)(2,1)S(1)}, u32[]{:S(2)}, u32[]{:S(2)}) collective-permute-start(bf16[512,64]{0,1:T(8,128)(2,1)} %get-tuple-element.5), channel_id=1, source_target_pairs={{0,1},{1,2},{2,3},{3,4},{4,5},{5,6},{6,7},{7,8},{8,9},{9,10},{10,1... | collective-permute-start | bytes 196616 | tf_op jit(solution)/shard_map/ppermute | solution.py:19
  5.0 1.3 %collective-permute-start.1 = (bf16[512,64]{0,1:T(8,128)(2,1)}, bf16[512,64]{0,1:T(8,128)(2,1)S(1)}, u32[]{:S(2)}, u32[]{:S(2)}) collective-permute-start(bf16[512,64]{0,1:T(8,128)(2,1)} %get-tuple-element.6), channel_id=1, source_target_pairs={{1,0},{2,1},{3,2},{4,3},{5,4},{6,5},{7,6},{8,7},{9,8},{10,9},{11,1... | collective-permute-start | bytes 196616 | tf_op jit(solution)/shard_map/ppermute | solution.py:21
  6.3 1.3 %fusion.5 = s32[1,2,8,128]{3,2,1,0:T(8,128)} fusion(s32[8,256]{1,0:T(8,128)} %param.9), kind=kLoop, calls=%fused_computation.21 | loop fusion | flops 16384 | bytes 16384
  7.6 1.3 %compare_and_fusion = pred[8,256]{1,0:T(8,128)(4,1)} fusion(s32[8,256]{1,0:T(8,128)} %param.9), kind=kLoop, calls=%fused_computation.23 | loop fusion | flops 12288 | bytes 10240 | tf_op jit(solution)/shard_map/jit(take_along_axis)/and | solution.py:53
  8.9 0.7 compare_select_fusion.1
  9.5 0.1 copy.12
  9.6 0.6 reshape.48
  10.2 0.7 copy.25
  10.9 1.3 %broadcast_in_dim.17 = pred[2048]{0:T(1024)(128)(4,1)} reshape(pred[8,256]{1,0:T(8,128)(4,1)} %compare_and_fusion) | data formatting | bytes 4096 | tf_op jit(solution)/shard_map/jit(take_along_axis)/broadcast_in_dim | solution.py:53
  12.2 1.2 %pad_clamp_fusion = s32[1024]{0:T(1024)} fusion(s32[24]{0:T(128)} %reshape.48), kind=kLoop, calls=%fused_computation.25 | loop fusion | flops 1024 | bytes 4192 | tf_op jit(solution)/shard_map/gather | solution.py:38
  13.4 0.0 collective-permute-done
  13.4 0.0 collective-permute-done.1
  13.5 1.6 %gather_fusion = bf16[24,256,64]{1,2,0:T(8,128)(2,1)} fusion(bf16[12,256,64]{1,2,0:T(8,128)(2,1)S(1)} %bitcast.40, s32[1024]{0:T(1024)} %pad_clamp_fusion), kind=kCustom, calls=%fused_computation | custom fusion | bytes 1572960 | tf_op jit(solution)/shard_map/gather | solution.py:38
  15.1 0.0 copy-done
  15.1 2.2 %fusion = f32[8,64,256]{2,1,0:T(8,128)S(1)} fusion(bf16[8,3,256,64]{2,3,1,0:T(8,128)(2,1)} %bitcast.41, bf16[8,3,256,256]{3,2,1,0:T(8,128)(2,1)S(1)} %copy-done, f32[8,256]{1,0:T(8,128)S(1)} %mul.42), kind=kOutput, calls=%fused_computation.4 | convolution fusion | flops 201457664 | bytes 4464640 | tf_op jit(solution)/shard_map/bkij,bkjr->bir/dot_general | solution.py:39
  17.3 0.0 copy-start.1
  17.3 0.8 copy-done.1
  18.1 0.6 convolution_bitcast_fusion.1
  18.6 44.8 %psum.7 = f32[64,64]{0,1:T(8,128)S(1)} all-reduce(f32[64,64]{0,1:T(8,128)S(1)} %convolution_bitcast_fusion.1), channel_id=1, replica_groups=mesh['rows'=16,'sub'=2] {'rows','sub'}, use_global_device_ids=true, to_apply=%region_0.0 | all-reduce | flops 4096 | bytes 32768 | tf_op jit(solution)/shard_map/psum | solution.py:48
  63.5 0.1 copy.16
  63.6 5.8 %cholesky.16 = f32[64,64]{1,0:T(8,128)S(1)} custom-call(f32[64,64]{1,0:T(8,128)S(1)} %fusion.4), custom_call_target="Cholesky" | custom-call | tf_op jit(solution)/shard_map/jit(cholesky)/cholesky | solution.py:49
  69.4 0.7 compare_reduce_fusion
  70.2 0.7 fusion.2
  70.9 4.9 %custom-call.6 = f32[1,64,64]{1,2,0:T(8,128)S(1)} custom-call(f32[1,64,64]{2,1,0:T(8,128)S(1)} %fusion.2), custom_call_target="InvertDiagBlocksLowerTriangular" | custom-call | tf_op jit(solution)/shard_map/triangular_solve | solution.py:50
  75.8 1.1 copy.24
  76.9 1.4 %convolution_multiply_fusion = f32[2048,64]{0,1:T(8,128)} fusion(f32[2048,64]{0,1:T(8,128)S(1)} %bitcast.43, f32[1,64,64]{1,2,0:T(8,128)S(1)} %custom-call.6), kind=kOutput, calls=%fused_computation.2 | convolution fusion | flops 100794368 | bytes 1064960 | tf_op jit(solution)/shard_map/triangular_solve | solution.py:50
  78.3 2.4 %copy.22 = f32[2048,64]{1,0:T(8,128)} copy(f32[2048,64]{0,1:T(8,128)} %convolution_multiply_fusion) | data formatting | bytes 1048576 | tf_op jit(solution)/shard_map/reshape | solution.py:52
  80.7 0.0 copy-start.2
  80.7 30.1 %gather_fusion.1 = f32[2048,64]{1,0:T(8,128)} fusion(f32[8,256,64]{2,1,0:T(8,128)} %bitcast.39, s32[2048]{0:T(1024)S(1)} %bitcast.38), kind=kCustom, calls=%fused_computation.1 | custom fusion | bytes 1064960 | tf_op jit(solution)/shard_map/jit(take_along_axis)/gather | solution.py:53
  110.7 0.0 copy-done.2
  110.7 2.6 %broadcast_select_fusion = f32[2048,64]{1,0:T(8,128)} fusion(f32[2048,64]{1,0:T(8,128)} %gather_fusion.1, pred[2048]{0:T(1024)(128)(4,1)S(1)} %copy-done.2), kind=kLoop, calls=%fused_computation.7 | loop fusion | flops 131072 | bytes 1050624 | tf_op jit(solution)/shard_map/jit(take_along_axis)/select_n | solution.py:53
  113.3 2.3 %copy.18 = f32[2048,64]{0,1:T(8,128)} copy(f32[2048,64]{1,0:T(8,128)} %broadcast_select_fusion) | data formatting | bytes 1048576 | tf_op jit(solution)/shard_map/jit(take_along_axis)/select_n | solution.py:53
  (5 shorter events, 0.1 us)
Async XLA Ops:
  0.0 15.1 %copy-start = (bf16[8,3,256,256]{3,2,1,0:T(8,128)(2,1)S(1)}, bf16[8,3,256,256]{3,2,1,0:T(8,128)(2,1)}, u32[]{:S(2)}) copy-start(bf16[8,3,256,256]{3,2,1,0:T(8,128)(2,1)} %param.5) | copy-start | bytes 9437188
  2.6 10.8 %collective-permute-start = (bf16[512,64]{0,1:T(8,128)(2,1)}, bf16[512,64]{0,1:T(8,128)(2,1)S(1)}, u32[]{:S(2)}, u32[]{:S(2)}) collective-permute-start(bf16[512,64]{0,1:T(8,128)(2,1)} %get-tuple-element.5), channel_id=1, source_target_pairs={{0,1},{1,2},{2,3},{3,4},{4,5},{5,6},{6,7},{7,8},{8,9},{9,10},{10,1... | collective-permute-start | bytes 196616 | tf_op jit(solution)/shard_map/ppermute | solution.py:19
  5.0 8.4 %collective-permute-start.1 = (bf16[512,64]{0,1:T(8,128)(2,1)}, bf16[512,64]{0,1:T(8,128)(2,1)S(1)}, u32[]{:S(2)}, u32[]{:S(2)}) collective-permute-start(bf16[512,64]{0,1:T(8,128)(2,1)} %get-tuple-element.6), channel_id=1, source_target_pairs={{1,0},{2,1},{3,2},{4,3},{5,4},{6,5},{7,6},{8,7},{9,8},{10,9},{11,1... | collective-permute-start | bytes 196616 | tf_op jit(solution)/shard_map/ppermute | solution.py:21
  17.3 0.8 copy-start.1
  80.7 30.1 %copy-start.2 = (pred[2048]{0:T(1024)(128)(4,1)S(1)}, pred[2048]{0:T(1024)(128)(4,1)}, u32[]{:S(2)}) copy-start(pred[2048]{0:T(1024)(128)(4,1)} %broadcast_in_dim.17) | copy-start | bytes 6148
where the time goes:
time: 116 us
  blocking collectives  44.8 us (39%)
  local copies, waits for them, and re-layouts  41.7 us (36%)
  other arithmetic  21.2 us (18%)
  matrix products  4.18 us (4%)
  starting transfers between devices  3.64 us (3%)
    psum x1, blocking collectives, body(): gram_whole = lax.psum(gram_local, ('rows', 'sub'))  44.8 us
    gather x1, local copies, waits for them, and re-layouts, body(): targets = jnp.take_along_axis(clustered, reorder[:, :, None], axis=1)  30.1 us
    another operation x3, other arithmetic, body(): lower_factor = jnp.linalg.cholesky(gram_whole)  6.6 us
    another operation x2, other arithmetic, body(): lax.linalg.triangular_solve(lower_factor, image_rows.T, left_side=True, l...  5.59 us
    select_n x1, other arithmetic, body(): targets = jnp.take_along_axis(clustered, reorder[:, :, None], axis=1)  2.55 us
    reshape x1, local copies, waits for them, and re-layouts, body(): clustered = (solved.T * math.sqrt(total_items)).reshape(count, block, -1)  2.41 us
    ppermute x1, starting transfers between devices, with_halo(): lax.ppermute(tail, axis, [(i, (i + 1) % count) for i in range(ends)])  2.35 us
    select_n x1, local copies, waits for them, and re-layouts, body(): targets = jnp.take_along_axis(clustered, reorder[:, :, None], axis=1)  2.34 us
  transfers between devices with their start and end apart: 2, of which 0 were waited for; matrix products, arithmetic and copies ran while one was open for 6% of the time, Pallas kernels for 0%

commit v1 on v0

v1 whole, which is shorter than its diff:
```python
import functools
import math

import jax
import jax.numpy as jnp
from jax import lax
from jax.experimental import pallas as pl
from jax.experimental.pallas import tpu as pltpu
from jax.sharding import PartitionSpec as P

REACH = 2
AXES = ("rows", "sub")
LANES = 128
VMEM = pl.BlockSpec(memory_space=pltpu.VMEM)
SMEM = pl.BlockSpec(memory_space=pltpu.SMEM)


def rank_dot(a, b, contract):
    return lax.dot_general(a, b, ((contract[:1], contract[1:]), ((), ())), preferred_element_type=jnp.float32)


def scaled_piece(basis_ref, degrees_ref, piece):
    root = lax.rsqrt(degrees_ref[pl.ds(piece, 1), :].astype(jnp.float32))
    columns = pl.ds(pl.multiple_of(piece * LANES, LANES), LANES)
    return (root * basis_ref[:, columns].astype(jnp.float32)).astype(jnp.bfloat16)


def edges_kernel(width, place_ref, basis_ref, degrees_ref, near_ref, far_ref):
    pieces = width // LANES
    last = basis_ref.shape[1] // LANES - pieces
    odd = place_ref[0] % 2
    for i in range(pieces):
        near_ref[:, i * LANES:(i + 1) * LANES] = scaled_piece(basis_ref, degrees_ref, (1 - odd) * last + i)
        far_ref[:, i * LANES:(i + 1) * LANES] = scaled_piece(basis_ref, degrees_ref, odd * last + i)


def image_kernel(
    count, block, place_ref, columns_ref, basis_ref, degrees_ref, near_ref, far_ref, affinity_ref, image_ref, gram_ref, extended
):
    step = pl.program_id(0)
    per_block = block // LANES

    @pl.when(step == 0)
    def _():
        gram_ref[...] = jnp.zeros_like(gram_ref)
        for piece in range(count * per_block):
            b, c = divmod(piece, per_block)
            extended[REACH + b, :, c * LANES:(c + 1) * LANES] = scaled_piece(basis_ref, degrees_ref, piece)
        odd = place_ref[0] % 2
        near_at, far_at = (1 - odd) * (count + REACH), odd * (count + REACH)
        for b in range(REACH):
            extended[near_at + b] = near_ref[:, b * block:(b + 1) * block]
            extended[far_at + b] = far_ref[:, b * block:(b + 1) * block]

    first = place_ref[0] * count - REACH
    total = jnp.zeros((basis_ref.shape[0], block), jnp.float32)
    for slot in range(affinity_ref.shape[1]):
        picked = extended[columns_ref[step, slot] - first]
        total += rank_dot(picked, affinity_ref[0, slot], (1, 1))
    root = [
        lax.rsqrt(degrees_ref[pl.ds(step * per_block + c, 1), :].astype(jnp.float32)) for c in range(per_block)
    ]
    image = total * jnp.concatenate(root, axis=1)
    image_ref[...] = image
    gram_ref[...] += lax.dot_general(
        image, image, (((1,), (1,)), ((), ())), precision=lax.Precision.HIGHEST, preferred_element_type=jnp.float32
    )


def reorder_kernel(count, block, image_ref, reorder_ref, placed_ref):
    rank = image_ref.shape[0]
    source = lax.broadcasted_iota(jnp.int32, (block, block), 0)
    for b in range(count):
        columns = slice(b * block, (b + 1) * block)
        image = image_ref[:, columns]
        high = image.astype(jnp.bfloat16)
        low = (image - high.astype(jnp.float32)).astype(jnp.bfloat16)
        chosen = jnp.where(source == reorder_ref[b:b + 1, :], 1.0, 0.0).astype(jnp.bfloat16)
        moved = rank_dot(jnp.concatenate([high, low], axis=0), chosen, (1, 0))
        placed_ref[:, columns] = moved.astype(jnp.bfloat16)


def inverse_factor(gram):
    rank = gram.shape[0]
    rows = lax.broadcasted_iota(jnp.int32, (rank, rank), 0)
    columns = lax.broadcasted_iota(jnp.int32, (rank, rank), 1)
    state = jnp.concatenate([gram, jnp.where(rows == columns, 1.0, 0.0)], axis=1)
    below = lax.broadcasted_iota(jnp.int32, state.shape, 0)
    for k in range(rank):
        pivot = 1.0 / state[k:k + 1, k:k + 1]
        row = state[k:k + 1, :] * pivot
        state = jnp.where(below > k, state - state[:, k:k + 1] * row, state)
    diagonal = jnp.sum(jnp.where(rows == columns, state[:, :rank], 0.0), axis=1, keepdims=True)
    return lax.rsqrt(diagonal) * state[:, rank:]


def targets_kernel(total_items, gram_ref, placed_ref, targets_ref):
    rank = gram_ref.shape[0]
    inverse = inverse_factor(gram_ref[...]) * math.sqrt(total_items)
    high = inverse.astype(jnp.bfloat16)
    low = (inverse - high.astype(jnp.float32)).astype(jnp.bfloat16)
    left = jnp.concatenate([high, high, low], axis=1)
    right = jnp.concatenate([placed_ref[...], placed_ref[:rank, :]], axis=0)
    targets_ref[...] = rank_dot(left, right, (1, 0))


def body(mesh_size, affinity, old_basis, degrees, column_blocks, reorder):
    count, slots, block, _ = affinity.shape
    items, rank = old_basis.shape
    width = REACH * block
    basis = old_basis.T
    degree_rows = degrees.reshape(items // LANES, LANES)
    place = lax.axis_index(AXES).astype(jnp.int32).reshape(1)

    edge = jax.ShapeDtypeStruct((rank, width), jnp.bfloat16)
    near, far = pl.pallas_call(
        functools.partial(edges_kernel, width),
        out_shape=(edge, edge),
        in_specs=[SMEM, VMEM, VMEM],
        out_specs=(VMEM, VMEM),
    )(place, basis, degree_rows)
    near = lax.ppermute(near, AXES, [(i, i ^ 1) for i in range(mesh_size) if i ^ 1 < mesh_size])
    crossing = range(1, mesh_size - 1, 2)
    far = lax.ppermute(far, AXES, [(i, i + 1) for i in crossing] + [(i + 1, i) for i in crossing])

    whole = lambda shape: pl.BlockSpec(shape, lambda b: (0,) * len(shape))
    image, gram = pl.pallas_call(
        functools.partial(image_kernel, count, block),
        grid=(count,),
        out_shape=(jax.ShapeDtypeStruct((rank, items), jnp.float32), jax.ShapeDtypeStruct((rank, rank), jnp.float32)),
        in_specs=[
            SMEM,
            SMEM,
            whole((rank, items)),
            whole(degree_rows.shape),
            whole((rank, width)),
            whole((rank, width)),
            pl.BlockSpec((1, slots, block, block), lambda b: (b, 0, 0, 0)),
        ],
        out_specs=(pl.BlockSpec((rank, block), lambda b: (0, b)), whole((rank, rank))),
        scratch_shapes=[pltpu.VMEM((count + 2 * REACH, rank, block), jnp.bfloat16)],
    )(place, column_blocks, basis, degree_rows, near, far, affinity)

    if mesh_size & (mesh_size - 1):
        gram = lax.psum(gram, AXES)
    else:
        step = 1
        while step < mesh_size:
            mask = step | 1
            gram = gram + lax.ppermute(gram, AXES, [(i, i ^ mask) for i in range(mesh_size)])
            step *= 2

    placed = pl.pallas_call(
        functools.partial(reorder_kernel, count, block),
        out_shape=jax.ShapeDtypeStruct((2 * rank, items), jnp.bfloat16),
        in_specs=[VMEM, VMEM],
        out_specs=VMEM,
        cost_estimate=pl.CostEstimate(flops=4 * rank * items * block, bytes_accessed=8 * rank * items, transcendentals=0),
    )(image, reorder)

    targets = pl.pallas_call(
        functools.partial(targets_kernel, items * mesh_size),
        out_shape=jax.ShapeDtypeStruct((rank, items), jnp.float32),
        in_specs=[VMEM, VMEM],
        out_specs=VMEM,
    )(gram, placed)
    return targets.T


def solution(mesh):
    placed = (
        P(AXES, None, None, None),
        P(AXES, None),
        P(AXES),
        P(AXES, None),
        P(AXES, None),
    )
    mesh_size = mesh.shape["rows"] * mesh.shape["sub"]
    return jax.shard_map(
        functools.partial(body, mesh_size), mesh=mesh, in_specs=placed, out_specs=P(AXES, None), check_vma=False
    )
```

time: 116 us -> 44.2 us (0.38)
  blocking collectives: 44.8 us -> 0 us
  local copies, waits for them, and re-layouts: 41.7 us -> 2.58 us
  other arithmetic: 21.2 us -> 1.39 us
  Pallas kernels: 0 us -> 18.8 us
  starting transfers between devices: 3.64 us -> 15.1 us
  waiting for transfers between devices: 0.01 us -> 5.88 us
  matrix products: 4.18 us -> 0 us
    psum x1 -> x0, blocking collectives: 44.8 us -> none  [body(): gram_whole = lax.psum(gram_local, ('rows', 'sub'))]
    gather x2 -> x0, local copies, waits for them, and re-layouts: 31.7 us -> none  [the longest x1 30.1 us: body(): targets = jnp.take_along_axis(clustered, reorder[:, :, None], axis=1)]
    pallas_call x0 -> x4, Pallas kernels: none -> 18.8 us  [the longest x1 7.57 us: body(): pl.pallas_call(functools.partial(targets_kernel, items * mesh_size), out_...]
    another operation x5 -> x0, other arithmetic: 12.2 us -> none  [the longest x3 6.6 us: body(): lower_factor = jnp.linalg.cholesky(gram_whole)]
    ppermute x2 -> x7, starting transfers between devices: 3.64 us -> 15.1 us  [the longest x5 14 us: body(): lax.ppermute(gram, AXES, [(i, i ^ mask) for i in range(mesh_size)])]
    ppermute x2 -> x7, waiting for transfers between devices: 0.01 us -> 5.88 us  [the longest x5 5.87 us: body(): lax.ppermute(gram, AXES, [(i, i ^ mask) for i in range(mesh_size)])]
    select_n x2 -> x0, other arithmetic: 3.24 us -> none  [the longest x1 2.55 us: body(): targets = jnp.take_along_axis(clustered, reorder[:, :, None], axis=1)]
    dot_general x2 -> x0, matrix products: 2.76 us -> none  [the longest x1 2.2 us: body(): jnp.einsum('bkij,bkjr->bir', affinity, fetched, preferred_element_type=jn...]
  transfers between devices with their start and end apart: 2 -> 7, of which waited for: 0 -> 4; matrix products, arithmetic and copies ran while one was open for 6% -> 3% of each run, Pallas kernels for 0% -> 5%
where the time goes in v1:
time: 44.2 us; the launch traced here: 43.8 us
  Pallas kernels  18.8 us (43%)
  starting transfers between devices  15.1 us (34%)
  waiting for transfers between devices  5.88 us (13%)
  local copies, waits for them, and re-layouts  2.58 us (6%)
  other arithmetic  1.39 us (3%)
    ppermute x5, starting transfers between devices, body(): lax.ppermute(gram, AXES, [(i, i ^ mask) for i in range(mesh_size)])  14 us
    pallas_call x1, Pallas kernels, body(): pl.pallas_call(functools.partial(targets_kernel, items * mesh_size), out_...  7.57 us
    pallas_call x1, Pallas kernels, body(): pl.pallas_call(functools.partial(image_kernel, count, block), grid=(count...  7.45 us
    ppermute x5, waiting for transfers between devices, body(): lax.ppermute(gram, AXES, [(i, i ^ mask) for i in range(mesh_size)])  5.87 us
    unnamed x5, local copies, waits for them, and re-layouts  2.58 us
    pallas_call x1, Pallas kernels, body(): pl.pallas_call(functools.partial(reorder_kernel, count, block), out_shape...  2.2 us
    pallas_call x1, Pallas kernels, body(): pl.pallas_call(functools.partial(edges_kernel, width), out_shape=(edge, e...  1.63 us
    add x5, other arithmetic, body(): gram + lax.ppermute(gram, AXES, [(i, i ^ mask) for i in range(mesh_size)])  1.39 us
  transfers between devices with their start and end apart: 7, of which 4 were waited for; matrix products, arithmetic and copies ran while one was open for 3% of the time, Pallas kernels for 5%

profile of v1, /device:TPU:0, one launch (start us, length us, event | category | flops | bytes accessed | tf_op | source)
XLA Modules:
  0.0 43.8 jit_solution(3881549920480251527)
XLA Ops:
  0.0 1.6 %shard_map.55 = (bf16[64,512]{1,0:T(8,128)(2,1)}, bf16[64,512]{1,0:T(8,128)(2,1)}) custom-call(s32[1]{0:T(128)} %bitcast.place_ref, bf16[64,2048]{1,0:T(8,128)(2,1)} %bitcast.4, s32[16,128]{1,0:T(8,128)} %bitcast.6), custom_call_target="tpu_custom_call" | custom-call | tf_op jit(solution)/shard_map/pallas_call | solution.py:116
  1.6 0.5 %collective-permute-start = (bf16[64,512]{1,0:T(8,128)(2,1)}, bf16[64,512]{1,0:T(8,128)(2,1)S(1)}, u32[]{:S(2)}, u32[]{:S(2)}) collective-permute-start(bf16[64,512]{1,0:T(8,128)(2,1)} %get-tuple-element.9), channel_id=1, source_target_pairs={{0,1},{1,0},{2,3},{3,2},{4,5},{5,4},{6,7},{7,6},{8,9},{9,8},{10,11... | collective-permute-start | bytes 196616 | tf_op jit(solution)/shard_map/ppermute | solution.py:122
  2.1 0.7 %collective-permute-start.1 = (bf16[64,512]{1,0:T(8,128)(2,1)}, bf16[64,512]{1,0:T(8,128)(2,1)S(1)}, u32[]{:S(2)}, u32[]{:S(2)}) collective-permute-start(bf16[64,512]{1,0:T(8,128)(2,1)} %get-tuple-element.10), channel_id=1, source_target_pairs={{1,2},{3,4},{5,6},{7,8},{9,10},{11,12},{13,14},{15,16},{17,18},{19... | collective-permute-start | bytes 196616 | tf_op jit(solution)/shard_map/ppermute | solution.py:124
  2.7 1.3 %copy.6.columns_ref = s32[8,3]{1,0:T(8,128)} copy(s32[8,3]{0,1:T(4,128)} %param.8) | data formatting | bytes 192 | tf_op args[3]
  4.1 0.0 collective-permute-done.near_ref
  4.1 0.0 copy-start
  4.1 0.0 collective-permute-done.1.far_ref
  4.1 0.6 %copy-done = bf16[64,512]{1,0:T(8,128)(2,1)} copy-done((bf16[64,512]{1,0:T(8,128)(2,1)}, bf16[64,512]{1,0:T(8,128)(2,1)S(1)}, u32[]{:S(2)}) %copy-start) | copy-done | bytes 65560
  4.7 0.0 copy-start.1
  4.7 0.6 %copy-done.1 = bf16[64,512]{1,0:T(8,128)(2,1)} copy-done((bf16[64,512]{1,0:T(8,128)(2,1)}, bf16[64,512]{1,0:T(8,128)(2,1)S(1)}, u32[]{:S(2)}) %copy-start.1) | copy-done | bytes 65560
  5.3 7.5 %shard_map.56 = (f32[64,2048]{1,0:T(8,128)}, f32[64,64]{1,0:T(8,128)}) custom-call(s32[1]{0:T(128)} %bitcast.place_ref, s32[8,3]{1,0:T(8,128)} %copy.6.columns_ref, bf16[64,2048]{1,0:T(8,128)(2,1)} %bitcast.5, s32[16,128]{1,0:T(8,128)} %bitcast.7, bf16[64,512]{1,0:T(8,128)(2,1)} %copy-done, bf16[64,512]{1,0:T(8,128)(2,1)} %copy-done.1, ...), custom_call_target="tpu_custom_call" | custom-call | tf_op jit(solution)/shard_map/pallas_call | solution.py:127
  12.8 4.0 %collective-permute-start.2 = (f32[64,64]{1,0:T(8,128)}, f32[64,64]{1,0:T(8,128)S(1)}, u32[]{:S(2)}, u32[]{:S(2)}) collective-permute-start(f32[64,64]{1,0:T(8,128)} %get-tuple-element.11), channel_id=1, source_target_pairs={{0,1},{1,0},{2,3},{3,2},{4,5},{5,4},{6,7},{7,6},{8,9},{9,8},{10,11... | collective-permute-start | bytes 49160 | tf_op jit(solution)/shard_map/ppermute | solution.py:150
  16.8 1.1 %collective-permute-done.2 = f32[64,64]{1,0:T(8,128)S(1)} collective-permute-done((f32[64,64]{1,0:T(8,128)}, f32[64,64]{1,0:T(8,128)S(1)}, u32[]{:S(2)}, u32[]{:S(2)}) %collective-permute-start.2) | collective-permute-done | bytes 16416 | tf_op jit(solution)/shard_map/ppermute | solution.py:150
  17.9 0.8 %add.19 = f32[64,64]{1,0:T(8,128)S(1)} add(f32[64,64]{1,0:T(8,128)} %get-tuple-element.11, f32[64,64]{1,0:T(8,128)S(1)} %collective-permute-done.2) | non-fusion elementwise | flops 4096 | bytes 49152 | tf_op jit(solution)/shard_map/add | solution.py:150
  18.6 3.0 %collective-permute-start.3 = (f32[64,64]{1,0:T(8,128)S(1)}, f32[64,64]{1,0:T(8,128)S(1)}, u32[]{:S(2)}, u32[]{:S(2)}) collective-permute-start(f32[64,64]{1,0:T(8,128)S(1)} %add.19), channel_id=1, source_target_pairs={{0,3},{1,2},{2,1},{3,0},{4,7},{5,6},{6,5},{7,4},{8,11},{9,10},{10,... | collective-permute-start | bytes 49160 | tf_op jit(solution)/shard_map/ppermute | solution.py:150
  21.7 1.6 %collective-permute-done.3 = f32[64,64]{1,0:T(8,128)S(1)} collective-permute-done((f32[64,64]{1,0:T(8,128)S(1)}, f32[64,64]{1,0:T(8,128)S(1)}, u32[]{:S(2)}, u32[]{:S(2)}) %collective-permute-start.3) | collective-permute-done | bytes 16416 | tf_op jit(solution)/shard_map/ppermute | solution.py:150
  23.3 2.1 %collective-permute-start.4 = (f32[64,64]{1,0:T(8,128)S(1)}, f32[64,64]{1,0:T(8,128)S(1)}, u32[]{:S(2)}, u32[]{:S(2)}) collective-permute-start(f32[64,64]{1,0:T(8,128)S(1)} %add.20), channel_id=1, source_target_pairs={{0,5},{1,4},{2,7},{3,6},{4,1},{5,0},{6,3},{7,2},{8,13},{9,12},{10,... | collective-permute-start | bytes 49160 | tf_op jit(solution)/shard_map/ppermute | solution.py:150
  25.4 1.6 %collective-permute-done.4 = f32[64,64]{1,0:T(8,128)S(1)} collective-permute-done((f32[64,64]{1,0:T(8,128)S(1)}, f32[64,64]{1,0:T(8,128)S(1)}, u32[]{:S(2)}, u32[]{:S(2)}) %collective-permute-start.4) | collective-permute-done | bytes 16416 | tf_op jit(solution)/shard_map/ppermute | solution.py:150
  27.0 2.1 %collective-permute-start.5 = (f32[64,64]{1,0:T(8,128)S(1)}, f32[64,64]{1,0:T(8,128)S(1)}, u32[]{:S(2)}, u32[]{:S(2)}) collective-permute-start(f32[64,64]{1,0:T(8,128)S(1)} %add.21), channel_id=1, source_target_pairs={{0,9},{1,8},{2,11},{3,10},{4,13},{5,12},{6,15},{7,14},{8,1},{9,0},... | collective-permute-start | bytes 49160 | tf_op jit(solution)/shard_map/ppermute | solution.py:150
  29.1 1.6 %collective-permute-done.5 = f32[64,64]{1,0:T(8,128)S(1)} collective-permute-done((f32[64,64]{1,0:T(8,128)S(1)}, f32[64,64]{1,0:T(8,128)S(1)}, u32[]{:S(2)}, u32[]{:S(2)}) %collective-permute-start.5) | collective-permute-done | bytes 16416 | tf_op jit(solution)/shard_map/ppermute | solution.py:150
  30.7 2.7 %collective-permute-start.6 = (f32[64,64]{1,0:T(8,128)S(1)}, f32[64,64]{1,0:T(8,128)S(1)}, u32[]{:S(2)}, u32[]{:S(2)}) collective-permute-start(f32[64,64]{1,0:T(8,128)S(1)} %add.22), channel_id=1, source_target_pairs={{0,17},{1,16},{2,19},{3,18},{4,21},{5,20},{6,23},{7,22},{8,25},{9,... | collective-permute-start | bytes 49160 | tf_op jit(solution)/shard_map/ppermute | solution.py:150
  33.4 2.2 %shard_map.57.placed_ref = bf16[128,2048]{1,0:T(8,128)(2,1)} custom-call(f32[64,2048]{1,0:T(8,128)} %get-tuple-element.12.image_ref, s32[8,256]{1,0:T(8,128)} %reorder_ref.1), custom_call_target="tpu_custom_call" | custom-call | flops 134217728 | bytes 1048576 | tf_op jit(solution)/shard_map/pallas_call | solution.py:153
  35.6 0.0 collective-permute-done.6
  35.6 0.6 %add.23.gram_ref = f32[64,64]{1,0:T(8,128)} add(f32[64,64]{1,0:T(8,128)S(1)} %add.22, f32[64,64]{1,0:T(8,128)S(1)} %collective-permute-done.6) | non-fusion elementwise | flops 4096 | bytes 49152 | tf_op jit(solution)/shard_map/add | solution.py:150
  36.2 7.6 %shard_map.58 = f32[64,2048]{1,0:T(8,128)} custom-call(f32[64,64]{1,0:T(8,128)} %add.23.gram_ref, bf16[128,2048]{1,0:T(8,128)(2,1)} %shard_map.57.placed_ref), custom_call_target="tpu_custom_call" | custom-call | tf_op jit(solution)/shard_map/pallas_call | solution.py:161
  (3 shorter events, 0.0 us)
Async XLA Ops:
  1.6 2.5 %collective-permute-start = (bf16[64,512]{1,0:T(8,128)(2,1)}, bf16[64,512]{1,0:T(8,128)(2,1)S(1)}, u32[]{:S(2)}, u32[]{:S(2)}) collective-permute-start(bf16[64,512]{1,0:T(8,128)(2,1)} %get-tuple-element.9), channel_id=1, source_target_pairs={{0,1},{1,0},{2,3},{3,2},{4,5},{5,4},{6,7},{7,6},{8,9},{9,8},{10,11... | collective-permute-start | bytes 196616 | tf_op jit(solution)/shard_map/ppermute | solution.py:122
  2.1 2.0 %collective-permute-start.1 = (bf16[64,512]{1,0:T(8,128)(2,1)}, bf16[64,512]{1,0:T(8,128)(2,1)S(1)}, u32[]{:S(2)}, u32[]{:S(2)}) collective-permute-start(bf16[64,512]{1,0:T(8,128)(2,1)} %get-tuple-element.10), channel_id=1, source_target_pairs={{1,2},{3,4},{5,6},{7,8},{9,10},{11,12},{13,14},{15,16},{17,18},{19... | collective-permute-start | bytes 196616 | tf_op jit(solution)/shard_map/ppermute | solution.py:124
  4.1 0.6 %copy-start = (bf16[64,512]{1,0:T(8,128)(2,1)}, bf16[64,512]{1,0:T(8,128)(2,1)S(1)}, u32[]{:S(2)}) copy-start(bf16[64,512]{1,0:T(8,128)(2,1)S(1)} %collective-permute-done.near_ref) | copy-start | bytes 196612
  4.7 0.6 %copy-start.1 = (bf16[64,512]{1,0:T(8,128)(2,1)}, bf16[64,512]{1,0:T(8,128)(2,1)S(1)}, u32[]{:S(2)}) copy-start(bf16[64,512]{1,0:T(8,128)(2,1)S(1)} %collective-permute-done.1.far_ref) | copy-start | bytes 196612
  12.8 5.1 %collective-permute-start.2 = (f32[64,64]{1,0:T(8,128)}, f32[64,64]{1,0:T(8,128)S(1)}, u32[]{:S(2)}, u32[]{:S(2)}) collective-permute-start(f32[64,64]{1,0:T(8,128)} %get-tuple-element.11), channel_id=1, source_target_pairs={{0,1},{1,0},{2,3},{3,2},{4,5},{5,4},{6,7},{7,6},{8,9},{9,8},{10,11... | collective-permute-start | bytes 49160 | tf_op jit(solution)/shard_map/ppermute | solution.py:150
  18.6 4.7 %collective-permute-start.3 = (f32[64,64]{1,0:T(8,128)S(1)}, f32[64,64]{1,0:T(8,128)S(1)}, u32[]{:S(2)}, u32[]{:S(2)}) collective-permute-start(f32[64,64]{1,0:T(8,128)S(1)} %add.19), channel_id=1, source_target_pairs={{0,3},{1,2},{2,1},{3,0},{4,7},{5,6},{6,5},{7,4},{8,11},{9,10},{10,... | collective-permute-start | bytes 49160 | tf_op jit(solution)/shard_map/ppermute | solution.py:150
  23.3 3.7 %collective-permute-start.4 = (f32[64,64]{1,0:T(8,128)S(1)}, f32[64,64]{1,0:T(8,128)S(1)}, u32[]{:S(2)}, u32[]{:S(2)}) collective-permute-start(f32[64,64]{1,0:T(8,128)S(1)} %add.20), channel_id=1, source_target_pairs={{0,5},{1,4},{2,7},{3,6},{4,1},{5,0},{6,3},{7,2},{8,13},{9,12},{10,... | collective-permute-start | bytes 49160 | tf_op jit(solution)/shard_map/ppermute | solution.py:150
  27.0 3.7 %collective-permute-start.5 = (f32[64,64]{1,0:T(8,128)S(1)}, f32[64,64]{1,0:T(8,128)S(1)}, u32[]{:S(2)}, u32[]{:S(2)}) collective-permute-start(f32[64,64]{1,0:T(8,128)S(1)} %add.21), channel_id=1, source_target_pairs={{0,9},{1,8},{2,11},{3,10},{4,13},{5,12},{6,15},{7,14},{8,1},{9,0},... | collective-permute-start | bytes 49160 | tf_op jit(solution)/shard_map/ppermute | solution.py:150
  30.7 4.9 %collective-permute-start.6 = (f32[64,64]{1,0:T(8,128)S(1)}, f32[64,64]{1,0:T(8,128)S(1)}, u32[]{:S(2)}, u32[]{:S(2)}) collective-permute-start(f32[64,64]{1,0:T(8,128)S(1)} %add.22), channel_id=1, source_target_pairs={{0,17},{1,16},{2,19},{3,18},{4,21},{5,20},{6,23},{7,22},{8,25},{9,... | collective-permute-start | bytes 49160 | tf_op jit(solution)/shard_map/ppermute | solution.py:150

commit v2 on v1

v2 whole, which is shorter than its diff:
```python
import functools
import math

import jax
import jax.numpy as jnp
from jax import lax
from jax.experimental import pallas as pl
from jax.experimental.pallas import tpu as pltpu
from jax.sharding import PartitionSpec as P

REACH = 2
AXES = ("rows", "sub")
SUBLANES, LANES = 8, 128
VMEM = pl.BlockSpec(memory_space=pltpu.VMEM)
SMEM = pl.BlockSpec(memory_space=pltpu.SMEM)
HBM = pl.BlockSpec(memory_space=pltpu.HBM)
PARAMS = pltpu.CompilerParams(vmem_limit_bytes=16 << 20)


def in_vmem(x):
    return pltpu.with_memory_space_constraint(x, pltpu.VMEM)


def in_hbm(x):
    return pltpu.with_memory_space_constraint(x, pltpu.HBM)


def rank_dot(a, b, contract, precision=None):
    return lax.dot_general(
        a, b, ((contract[:1], contract[1:]), ((), ())), precision=precision, preferred_element_type=jnp.float32
    )


def gram_of(image):
    return rank_dot(image, image, (1, 1), lax.Precision.HIGHEST)


def inverse_root(degrees_ref, piece):
    return lax.rsqrt(degrees_ref[pl.ds(piece, 1), :].astype(jnp.float32))


def block_root(degrees_ref, b, block):
    pieces = block // LANES
    return jnp.concatenate([inverse_root(degrees_ref, b * pieces + c) for c in range(pieces)], axis=1)


def scaled(degrees_ref, piece, basis):
    return (inverse_root(degrees_ref, piece) * basis.astype(jnp.float32)).astype(jnp.bfloat16)


def edges_kernel(width, place_ref, basis_hbm, degrees_hbm, near_ref, far_ref, ends, degrees_ref, sems):
    items = basis_hbm.shape[1]
    pieces, last = width // LANES, (items - width) // LANES
    copies = [
        pltpu.make_async_copy(degrees_hbm, degrees_ref, sems.at[0]),
        pltpu.make_async_copy(basis_hbm.at[:, :width], ends.at[0], sems.at[1]),
        pltpu.make_async_copy(basis_hbm.at[:, items - width:], ends.at[1], sems.at[2]),
    ]
    for copy in copies:
        copy.start()
    odd = place_ref[0] % 2 == 1
    for copy in copies:
        copy.wait()
    for i in range(pieces):
        columns = slice(i * LANES, (i + 1) * LANES)
        head = scaled(degrees_ref, i, ends[0, :, columns])
        tail = scaled(degrees_ref, last + i, ends[1, :, columns])
        near_ref[:, columns] = jnp.where(odd, head, tail)
        far_ref[:, columns] = jnp.where(odd, tail, head)


def own_kernel(
    count, block, edges, place_ref, columns_hbm, basis_hbm, degrees_hbm, affinity_ref, partial_ref, gram_ref,
    columns_ref, degrees_ref, extended, basis_ref, sems
):
    pieces = block // LANES
    small = [
        pltpu.make_async_copy(columns_hbm, columns_ref, sems.at[0]),
        pltpu.make_async_copy(degrees_hbm, degrees_ref, sems.at[1]),
        pltpu.make_async_copy(basis_hbm, basis_ref, sems.at[2]),
    ]
    for copy in small:
        copy.start()
    for b in range(REACH):
        extended[b] = jnp.zeros_like(extended[b])
        extended[count + REACH + b] = jnp.zeros_like(extended[b])
    for copy in small:
        copy.wait()
    for piece in range(count * pieces):
        b, c = divmod(piece, pieces)
        extended[REACH + b, :, c * LANES:(c + 1) * LANES] = scaled(
            degrees_ref, piece, basis_ref[:, piece * LANES:(piece + 1) * LANES]
        )
    first = place_ref[0] * count - REACH
    inner = []
    for b in range(count):
        total = rank_dot(extended[REACH + b], affinity_ref[b, 0], (1, 1))
        for slot in range(1, affinity_ref.shape[1]):
            total += rank_dot(extended[columns_ref[slot, b] - first], affinity_ref[b, slot], (1, 1))
        if b not in edges:
            total *= block_root(degrees_ref, b, block)
            inner.append(total)
        partial_ref[:, b * block:(b + 1) * block] = total
    if inner:
        gram_ref[...] = gram_of(jnp.concatenate(inner, axis=1))
    else:
        gram_ref[...] = jnp.zeros_like(gram_ref)


def halo_kernel(
    count, block, edges, place_ref, columns_ref, degrees_ref, near_ref, far_ref, affinity_ref, partial_ref, inner_ref,
    image_ref, gram_ref, halo
):
    odd = place_ref[0] % 2
    for b in range(REACH):
        halo[(1 - odd) * REACH + b] = near_ref[:, b * block:(b + 1) * block]
        halo[odd * REACH + b] = far_ref[:, b * block:(b + 1) * block]
    halo[2 * REACH] = jnp.zeros_like(halo[0])
    first = place_ref[0] * count - REACH
    images = []
    for at, b in enumerate(edges):
        total = partial_ref[:, b * block:(b + 1) * block]
        for slot in range(1, affinity_ref.shape[1]):
            index = columns_ref[slot, b] - first
            index = jnp.where(index < REACH, index, jnp.where(index < REACH + count, 2 * REACH, index - count))
            total += rank_dot(halo[index], affinity_ref[b, slot], (1, 1))
        images.append(total * block_root(degrees_ref, b, block))
        image_ref[:, at * block:(at + 1) * block] = images[-1]
    gram_ref[...] = inner_ref[...] + gram_of(jnp.concatenate(images, axis=1))


def reorder_kernel(count, block, edges, inner_ref, outer_ref, reorder_ref, placed_ref):
    source = lax.broadcasted_iota(jnp.int32, (block, block), 0)
    for b in range(count):
        at = edges.index(b) if b in edges else b
        image = (outer_ref if b in edges else inner_ref)[:, at * block:(at + 1) * block]
        high = image.astype(jnp.bfloat16)
        low = (image - high.astype(jnp.float32)).astype(jnp.bfloat16)
        chosen = jnp.where(source == reorder_ref[b:b + 1, :], 1.0, 0.0).astype(jnp.bfloat16)
        moved = rank_dot(jnp.concatenate([high, low], axis=0), chosen, (1, 0))
        placed_ref[:, b * block:(b + 1) * block] = moved.astype(jnp.bfloat16)


def wide(x):
    return jnp.broadcast_to(x, (SUBLANES, LANES))


def inverse_factor(gram):
    rank = gram.shape[0]
    panels = rank // SUBLANES
    rows = lax.broadcasted_iota(jnp.int32, (rank, rank), 0)
    columns = lax.broadcasted_iota(jnp.int32, (rank, rank), 1)
    state = jnp.concatenate([gram, jnp.where(rows == columns, 1.0, 0.0)], axis=1)
    state = [state[SUBLANES * q:SUBLANES * (q + 1)] for q in range(panels)]
    sublane = lax.broadcasted_iota(jnp.int32, (SUBLANES, LANES), 0)
    span = range(SUBLANES)
    out = []
    for p in range(panels):
        spread = [[wide(state[q][:, SUBLANES * p + j:SUBLANES * p + j + 1]) for j in span] for q in range(p, panels)]
        pivot = [[wide(spread[0][j][i:i + 1, :]) for j in range(i + 1)] for i in span]
        old = [wide(state[p][i:i + 1, :]) for i in span]
        inverse, unit, new = [], [], []
        for i in span:
            inverse.append(1.0 / pivot[i][i])
            factor = [pivot[i][m] * inverse[m] for m in range(i)]
            line = []
            for m in range(i):
                entry = factor[m]
                for k in range(m + 1, i):
                    entry = entry + factor[k] * unit[k][m]
                line.append(-entry)
            unit.append(line)
            row = old[i]
            for m in range(i):
                row = row + line[m] * old[m]
            new.append(row)
            for k in range(i + 1, SUBLANES):
                weight = pivot[k][i] * inverse[i]
                for z in range(k, SUBLANES):
                    pivot[z][k] = pivot[z][k] - pivot[z][i] * weight
        if p + 1 < panels:
            divided = [new[i] * inverse[i] for i in span]
            update = []
            for m in span:
                line = divided[m]
                for i in range(m + 1, SUBLANES):
                    line = line + unit[i][m] * divided[i]
                update.append(line)
            for q in range(p + 1, panels):
                terms = [spread[q - p][m] * update[m] for m in span]
                while len(terms) > 1:
                    terms = [terms[a] + terms[a + 1] for a in range(0, len(terms), 2)]
                state[q] = state[q] - terms[0]
        panel = new[0] * lax.rsqrt(pivot[0][0])
        for i in range(1, SUBLANES):
            panel = jnp.where(sublane == i, new[i] * lax.rsqrt(pivot[i][i]), panel)
        out.append(panel)
    return jnp.concatenate(out, axis=0)[:, rank:]


def targets_kernel(total_items, parts, *refs):
    placed_ref, targets_ref = refs[parts:]
    gram = refs[0][...]
    for part in refs[1:parts]:
        gram = gram + part[...]
    rank = gram.shape[0]
    inverse = inverse_factor(gram) * math.sqrt(total_items)
    high = inverse.astype(jnp.bfloat16)
    low = (inverse - high.astype(jnp.float32)).astype(jnp.bfloat16)
    left = jnp.concatenate([high, high, low], axis=1)
    right = jnp.concatenate([placed_ref[...], placed_ref[:rank, :]], axis=0)
    targets_ref[...] = rank_dot(left, right, (1, 0))


def gram_parts(gram, mesh_size):
    if mesh_size & (mesh_size - 1):
        return [lax.psum(gram, AXES)]
    parts, step = [gram], 1
    while step < mesh_size:
        gram = sum(parts[1:], parts[0])
        parts = [gram, lax.ppermute(gram, AXES, [(i, i ^ (step | 1)) for i in range(mesh_size)])]
        step *= 2
    return parts


def body(mesh_size, affinity, old_basis, degrees, column_blocks, reorder):
    count, slots, block, _ = affinity.shape
    items, rank = old_basis.shape
    width = REACH * block
    edges = [b for b in range(count) if b < REACH or b >= count - REACH]
    affinity = in_vmem(affinity)
    basis = old_basis.T
    degree_rows = degrees.reshape(items // LANES, LANES)
    columns = column_blocks.T
    place = lax.axis_index(AXES).astype(jnp.int32).reshape(1)
    square = pltpu.VMEM((rank, rank), jnp.float32)

    near, far = pl.pallas_call(
        functools.partial(edges_kernel, width),
        out_shape=(pltpu.VMEM((rank, width), jnp.bfloat16),) * 2,
        in_specs=[SMEM, HBM, HBM],
        out_specs=(VMEM, VMEM),
        scratch_shapes=[
            pltpu.VMEM((2, rank, width), jnp.bfloat16),
            pltpu.VMEM(degree_rows.shape, jnp.int32),
            pltpu.SemaphoreType.DMA((3,)),
        ],
        compiler_params=PARAMS,
        cost_estimate=pl.CostEstimate(flops=1000 * affinity.size, bytes_accessed=40 * affinity.size, transcendentals=0),
        name="edges",
    )(place, in_hbm(basis), in_hbm(degree_rows))
    near = lax.ppermute(near, AXES, [(i, i ^ 1) for i in range(mesh_size) if i ^ 1 < mesh_size])
    crossing = range(1, mesh_size - 1, 2)
    far = lax.ppermute(far, AXES, [(i, i + 1) for i in crossing] + [(i + 1, i) for i in crossing])

    partial, inner, columns, degree_rows = pl.pallas_call(
        functools.partial(own_kernel, count, block, edges),
        out_shape=(
            pltpu.VMEM((rank, items), jnp.float32),
            square,
            pltpu.SMEM(columns.shape, jnp.int32),
            pltpu.VMEM(degree_rows.shape, jnp.int32),
        ),
        in_specs=[SMEM] + [HBM] * 3 + [VMEM],
        out_specs=(VMEM, VMEM, SMEM, VMEM),
        scratch_shapes=[
            pltpu.VMEM((count + 2 * REACH, rank, block), jnp.bfloat16),
            pltpu.VMEM((rank, items), jnp.bfloat16),
            pltpu.SemaphoreType.DMA((3,)),
        ],
        compiler_params=PARAMS,
        cost_estimate=pl.CostEstimate(
            flops=2 * count * slots * block * block * rank, bytes_accessed=0, transcendentals=0
        ),
        name="own",
    )(place, *map(in_hbm, (columns, basis, degree_rows)), affinity)

    outer, gram = pl.pallas_call(
        functools.partial(halo_kernel, count, block, edges),
        out_shape=(pltpu.VMEM((rank, len(edges) * block), jnp.float32), square),
        in_specs=[SMEM, SMEM] + [VMEM] * 6,
        out_specs=(VMEM, VMEM),
        scratch_shapes=[pltpu.VMEM((2 * REACH + 1, rank, block), jnp.bfloat16)],
        compiler_params=PARAMS,
        name="halo",
    )(place, columns, *map(in_vmem, (degree_rows, near, far)), affinity, *map(in_vmem, (partial, inner)))

    placed = pl.pallas_call(
        functools.partial(reorder_kernel, count, block, edges),
        out_shape=pltpu.VMEM((2 * rank, items), jnp.bfloat16),
        in_specs=[VMEM] * 3,
        out_specs=VMEM,
        compiler_params=PARAMS,
        cost_estimate=pl.CostEstimate(flops=4 * rank * items * block, bytes_accessed=0, transcendentals=0),
        name="reorder",
    )(in_vmem(partial), in_vmem(outer), in_vmem(reorder))

    parts = gram_parts(gram, mesh_size)
    targets = pl.pallas_call(
        functools.partial(targets_kernel, items * mesh_size, len(parts)),
        out_shape=jax.ShapeDtypeStruct((rank, items), jnp.float32),
        in_specs=[VMEM] * (len(parts) + 1),
        out_specs=VMEM,
        compiler_params=PARAMS,
        name="targets",
    )(*map(in_vmem, parts), in_vmem(placed))
    return targets.T


def solution(mesh):
    placed = (
        P(AXES, None, None, None),
        P(AXES, None),
        P(AXES),
        P(AXES, None),
        P(AXES, None),
    )
    mesh_size = mesh.shape["rows"] * mesh.shape["sub"]
    return jax.shard_map(
        functools.partial(body, mesh_size), mesh=mesh, in_specs=placed, out_specs=P(AXES, None), check_vma=False
    )
```

time: 44.2 us -> 29.6 us (0.67)
  Pallas kernels: 18.8 us -> 7.79 us
  local copies, waits for them, and re-layouts: 2.58 us -> 0.01 us
  other arithmetic: 1.39 us -> 0.02 us
  waiting for transfers between devices: 5.88 us -> 6.89 us
    pallas_call x4 -> x5, Pallas kernels: 18.8 us -> 7.79 us  [the longest x1 3.32 us: body(): pl.pallas_call(functools.partial(targets_kernel, items * mesh_size, len(p...]
    unnamed x5 -> x4, local copies, waits for them, and re-layouts: 2.58 us -> 0.01 us
    add x5 -> x4, other arithmetic: 1.39 us -> 0.02 us  [gram_parts(): gram = sum(parts[1:], parts[0])]
    ppermute x5, waiting for transfers between devices: 5.87 us -> 6.89 us  [gram_parts(): lax.ppermute(gram, AXES, [(i, i ^ (step | 1)) for i in range(mesh_size)])]
    ppermute x5, starting transfers between devices: 14 us -> 13.5 us  [gram_parts(): lax.ppermute(gram, AXES, [(i, i ^ (step | 1)) for i in range(mesh_size)])]
  transfers between devices with their start and end apart: 7 -> 7, of which waited for: 4 -> 5; matrix products, arithmetic and copies ran while one was open for 3% -> 0% of each run, Pallas kernels for 5% -> 9%
where the time goes in v2:
time: 29.6 us; the launch traced here: 29.4 us
  starting transfers between devices  14.7 us (50%)
  Pallas kernels  7.79 us (26%)
  waiting for transfers between devices  6.89 us (23%)
    ppermute x5, starting transfers between devices, gram_parts(): lax.ppermute(gram, AXES, [(i, i ^ (step | 1)) for i in range(mesh_size)])  13.5 us
    ppermute x5, waiting for transfers between devices, gram_parts(): lax.ppermute(gram, AXES, [(i, i ^ (step | 1)) for i in range(mesh_size)])  6.89 us
    pallas_call x1, Pallas kernels, body(): pl.pallas_call(functools.partial(targets_kernel, items * mesh_size, len(p...  3.32 us
    pallas_call x1, Pallas kernels, body(): pl.pallas_call(functools.partial(own_kernel, count, block, edges), out_sh...  2.3 us
    pallas_call x1, Pallas kernels, body(): pl.pallas_call(functools.partial(edges_kernel, width), out_shape=(pltpu.V...  1.11 us
    pallas_call x1, Pallas kernels, body(): pl.pallas_call(functools.partial(halo_kernel, count, block, edges), out_s...  0.71 us
    ppermute x1, starting transfers between devices, body(): lax.ppermute(far, AXES, [(i, i + 1) for i in crossing] + [(i + 1, i) for...  0.65 us
  transfers between devices with their start and end apart: 7, of which 5 were waited for; matrix products, arithmetic and copies ran while one was open for 0% of the time, Pallas kernels for 9%

profile of v2, /device:TPU:0, one launch (start us, length us, event | category | flops | bytes accessed | tf_op | source)
XLA Modules:
  0.0 29.4 jit_solution(16348485107562236591)
XLA Ops:
  0.0 0.0 copy-start
  0.0 1.1 %edges.1 = (bf16[64,512]{1,0:T(8,128)(2,1)S(1)}, bf16[64,512]{1,0:T(8,128)(2,1)S(1)}) custom-call(s32[1]{0:T(128)} %bitcast.place_ref, bf16[64,2048]{1,0:T(8,128)(2,1)} %bitcast.5, s32[16,128]{1,0:T(8,128)} %bitcast.7), custom_call_target="tpu_custom_call" | custom-call | flops 1572864000 | bytes 62914560 | tf_op jit(solution)/shard_map/edges/pallas_call | solution.py:238
  1.1 0.5 %collective-permute-start = (bf16[64,512]{1,0:T(8,128)(2,1)S(1)}, bf16[64,512]{1,0:T(8,128)(2,1)S(1)}, u32[]{:S(2)}, u32[]{:S(2)}) collective-permute-start(bf16[64,512]{1,0:T(8,128)(2,1)S(1)} %get-tuple-element.15), channel_id=1, source_target_pairs={{0,1},{1,0},{2,3},{3,2},{4,5},{5,4},{6,7},{7,6},{8,9},{9,8},{10,11... | collective-permute-start | bytes 196616 | tf_op jit(solution)/shard_map/ppermute | solution.py:252
  1.6 0.7 %collective-permute-start.1 = (bf16[64,512]{1,0:T(8,128)(2,1)S(1)}, bf16[64,512]{1,0:T(8,128)(2,1)S(1)}, u32[]{:S(2)}, u32[]{:S(2)}) collective-permute-start(bf16[64,512]{1,0:T(8,128)(2,1)S(1)} %get-tuple-element.16), channel_id=1, source_target_pairs={{1,2},{3,4},{5,6},{7,8},{9,10},{11,12},{13,14},{15,16},{17,18},{19... | collective-permute-start | bytes 196616 | tf_op jit(solution)/shard_map/ppermute | solution.py:254
  2.3 0.0 copy-done
  2.3 0.0 copy-start.1
  2.3 2.3 %own.1 = (f32[64,2048]{1,0:T(8,128)S(1)}, f32[64,64]{1,0:T(8,128)S(1)}, s32[3,8]{1,0:T(4,128)S(4)}, s32[16,128]{1,0:T(8,128)S(1)}) custom-call(s32[1]{0:T(128)} %bitcast.place_ref, s32[3,8]{1,0:T(4,128)} %bitcast.9, bf16[64,2048]{1,0:T(8,128)(2,1)} %bitcast.6, s32[16,128]{1,0:T(8,128)} %bitcast.8, bf16[8,3,256,256]{3,2,1,0:T(8,128)(2,1)S(1)} %copy-done), custom_call_target="tpu_custom_call" | custom-call | flops 201326592 | tf_op jit(solution)/shard_map/own/pallas_call | solution.py:256
  4.6 0.0 collective-permute-done.near_ref
  4.6 0.0 collective-permute-done.1.far_ref
  4.6 0.7 %halo.1 = (f32[64,1024]{1,0:T(8,128)S(1)}, f32[64,64]{1,0:T(8,128)S(1)}) custom-call(s32[1]{0:T(128)} %bitcast.place_ref, s32[3,8]{1,0:T(4,128)S(4)} %get-tuple-element.13.columns_ref, s32[16,128]{1,0:T(8,128)S(1)} %get-tuple-element.14.degrees_ref, bf16[64,512]{1,0:T(8,128)(2,1)S(1)} %collective-permute-done.near_ref, ...), custom_call_target="tpu_custom_call" | custom-call | tf_op jit(solution)/shard_map/halo/pallas_call | solution.py:278
  5.4 3.9 %collective-permute-start.2 = (f32[64,64]{1,0:T(8,128)S(1)}, f32[64,64]{1,0:T(8,128)S(1)}, u32[]{:S(2)}, u32[]{:S(2)}) collective-permute-start(f32[64,64]{1,0:T(8,128)S(1)} %get-tuple-element.19), channel_id=1, source_target_pairs={{0,1},{1,0},{2,3},{3,2},{4,5},{5,4},{6,7},{7,6},{8,9},{9,8},{10,11... | collective-permute-start | bytes 49160 | tf_op jit(solution)/shard_map/ppermute | solution.py:221
  9.3 0.9 %collective-permute-done.2 = f32[64,64]{1,0:T(8,128)S(1)} collective-permute-done((f32[64,64]{1,0:T(8,128)S(1)}, f32[64,64]{1,0:T(8,128)S(1)}, u32[]{:S(2)}, u32[]{:S(2)}) %collective-permute-start.2) | collective-permute-done | bytes 16416 | tf_op jit(solution)/shard_map/ppermute | solution.py:221
  10.2 2.6 %collective-permute-start.3 = (f32[64,64]{1,0:T(8,128)S(1)}, f32[64,64]{1,0:T(8,128)S(1)}, u32[]{:S(2)}, u32[]{:S(2)}) collective-permute-start(f32[64,64]{1,0:T(8,128)S(1)} %add.16), channel_id=1, source_target_pairs={{0,3},{1,2},{2,1},{3,0},{4,7},{5,6},{6,5},{7,4},{8,11},{9,10},{10,... | collective-permute-start | bytes 49160 | tf_op jit(solution)/shard_map/ppermute | solution.py:221
  12.8 1.6 %collective-permute-done.3 = f32[64,64]{1,0:T(8,128)S(1)} collective-permute-done((f32[64,64]{1,0:T(8,128)S(1)}, f32[64,64]{1,0:T(8,128)S(1)}, u32[]{:S(2)}, u32[]{:S(2)}) %collective-permute-start.3) | collective-permute-done | bytes 16416 | tf_op jit(solution)/shard_map/ppermute | solution.py:221
  14.4 2.1 %collective-permute-start.4 = (f32[64,64]{1,0:T(8,128)S(1)}, f32[64,64]{1,0:T(8,128)S(1)}, u32[]{:S(2)}, u32[]{:S(2)}) collective-permute-start(f32[64,64]{1,0:T(8,128)S(1)} %add.17), channel_id=1, source_target_pairs={{0,5},{1,4},{2,7},{3,6},{4,1},{5,0},{6,3},{7,2},{8,13},{9,12},{10,... | collective-permute-start | bytes 49160 | tf_op jit(solution)/shard_map/ppermute | solution.py:221
  16.5 1.6 %collective-permute-done.4 = f32[64,64]{1,0:T(8,128)S(1)} collective-permute-done((f32[64,64]{1,0:T(8,128)S(1)}, f32[64,64]{1,0:T(8,128)S(1)}, u32[]{:S(2)}, u32[]{:S(2)}) %collective-permute-start.4) | collective-permute-done | bytes 16416 | tf_op jit(solution)/shard_map/ppermute | solution.py:221
  18.1 2.1 %collective-permute-start.5 = (f32[64,64]{1,0:T(8,128)S(1)}, f32[64,64]{1,0:T(8,128)S(1)}, u32[]{:S(2)}, u32[]{:S(2)}) collective-permute-start(f32[64,64]{1,0:T(8,128)S(1)} %add.18), channel_id=1, source_target_pairs={{0,9},{1,8},{2,11},{3,10},{4,13},{5,12},{6,15},{7,14},{8,1},{9,0},... | collective-permute-start | bytes 49160 | tf_op jit(solution)/shard_map/ppermute | solution.py:221
  20.2 1.6 %collective-permute-done.5 = f32[64,64]{1,0:T(8,128)S(1)} collective-permute-done((f32[64,64]{1,0:T(8,128)S(1)}, f32[64,64]{1,0:T(8,128)S(1)}, u32[]{:S(2)}, u32[]{:S(2)}) %collective-permute-start.5) | collective-permute-done | bytes 16416 | tf_op jit(solution)/shard_map/ppermute | solution.py:221
  21.8 2.8 %collective-permute-start.6 = (f32[64,64]{1,0:T(8,128)S(1)}, f32[64,64]{1,0:T(8,128)S(1)}, u32[]{:S(2)}, u32[]{:S(2)}) collective-permute-start(f32[64,64]{1,0:T(8,128)S(1)} %add.19.refs_0_), channel_id=1, source_target_pairs={{0,17},{1,16},{2,19},{3,18},{4,21},{5,20},{6,23},{7,22},{8,25},{9,... | collective-permute-start | bytes 49160 | tf_op jit(solution)/shard_map/ppermute | solution.py:221
  24.5 0.0 copy-done.1
  24.5 0.4 %reorder.1.refs_2_ = bf16[128,2048]{1,0:T(8,128)(2,1)S(1)} custom-call(f32[64,2048]{1,0:T(8,128)S(1)} %get-tuple-element.17.partial_ref.inner_ref, f32[64,1024]{1,0:T(8,128)S(1)} %get-tuple-element.20.outer_ref, s32[8,256]{1,0:T(8,128)S(1)} %copy-done.1), custom_call_target="tpu_custom_call" | custom-call | flops 134217728 | tf_op jit(solution)/shard_map/reorder/pallas_call | solution.py:288
  24.9 1.2 %collective-permute-done.6.refs_1_ = f32[64,64]{1,0:T(8,128)S(1)} collective-permute-done((f32[64,64]{1,0:T(8,128)S(1)}, f32[64,64]{1,0:T(8,128)S(1)}, u32[]{:S(2)}, u32[]{:S(2)}) %collective-permute-start.6) | collective-permute-done | bytes 16416 | tf_op jit(solution)/shard_map/ppermute | solution.py:221
  26.1 3.3 %targets.1 = f32[64,2048]{1,0:T(8,128)} custom-call(f32[64,64]{1,0:T(8,128)S(1)} %add.19.refs_0_, f32[64,64]{1,0:T(8,128)S(1)} %collective-permute-done.6.refs_1_, bf16[128,2048]{1,0:T(8,128)(2,1)S(1)} %reorder.1.refs_2_), custom_call_target="tpu_custom_call" | custom-call | tf_op jit(solution)/shard_map/targets/pallas_call | solution.py:299
  (4 shorter events, 0.0 us)
Async XLA Ops:
  0.0 2.3 %copy-start = (bf16[8,3,256,256]{3,2,1,0:T(8,128)(2,1)S(1)}, bf16[8,3,256,256]{3,2,1,0:T(8,128)(2,1)}, u32[]{:S(2)}) copy-start(bf16[8,3,256,256]{3,2,1,0:T(8,128)(2,1)} %affinity_ref.3) | copy-start | bytes 9437188
  1.1 3.5 %collective-permute-start = (bf16[64,512]{1,0:T(8,128)(2,1)S(1)}, bf16[64,512]{1,0:T(8,128)(2,1)S(1)}, u32[]{:S(2)}, u32[]{:S(2)}) collective-permute-start(bf16[64,512]{1,0:T(8,128)(2,1)S(1)} %get-tuple-element.15), channel_id=1, source_target_pairs={{0,1},{1,0},{2,3},{3,2},{4,5},{5,4},{6,7},{7,6},{8,9},{9,8},{10,11... | collective-permute-start | bytes 196616 | tf_op jit(solution)/shard_map/ppermute | solution.py:252
  1.6 3.0 %collective-permute-start.1 = (bf16[64,512]{1,0:T(8,128)(2,1)S(1)}, bf16[64,512]{1,0:T(8,128)(2,1)S(1)}, u32[]{:S(2)}, u32[]{:S(2)}) collective-permute-start(bf16[64,512]{1,0:T(8,128)(2,1)S(1)} %get-tuple-element.16), channel_id=1, source_target_pairs={{1,2},{3,4},{5,6},{7,8},{9,10},{11,12},{13,14},{15,16},{17,18},{19... | collective-permute-start | bytes 196616 | tf_op jit(solution)/shard_map/ppermute | solution.py:254
  2.3 22.2 %copy-start.1 = (s32[8,256]{1,0:T(8,128)S(1)}, s32[8,256]{1,0:T(8,128)}, u32[]{:S(2)}) copy-start(s32[8,256]{1,0:T(8,128)} %reorder_ref.1) | copy-start | bytes 24580
  5.4 4.8 %collective-permute-start.2 = (f32[64,64]{1,0:T(8,128)S(1)}, f32[64,64]{1,0:T(8,128)S(1)}, u32[]{:S(2)}, u32[]{:S(2)}) collective-permute-start(f32[64,64]{1,0:T(8,128)S(1)} %get-tuple-element.19), channel_id=1, source_target_pairs={{0,1},{1,0},{2,3},{3,2},{4,5},{5,4},{6,7},{7,6},{8,9},{9,8},{10,11... | collective-permute-start | bytes 49160 | tf_op jit(solution)/shard_map/ppermute | solution.py:221
  10.2 4.2 %collective-permute-start.3 = (f32[64,64]{1,0:T(8,128)S(1)}, f32[64,64]{1,0:T(8,128)S(1)}, u32[]{:S(2)}, u32[]{:S(2)}) collective-permute-start(f32[64,64]{1,0:T(8,128)S(1)} %add.16), channel_id=1, source_target_pairs={{0,3},{1,2},{2,1},{3,0},{4,7},{5,6},{6,5},{7,4},{8,11},{9,10},{10,... | collective-permute-start | bytes 49160 | tf_op jit(solution)/shard_map/ppermute | solution.py:221
  14.4 3.7 %collective-permute-start.4 = (f32[64,64]{1,0:T(8,128)S(1)}, f32[64,64]{1,0:T(8,128)S(1)}, u32[]{:S(2)}, u32[]{:S(2)}) collective-permute-start(f32[64,64]{1,0:T(8,128)S(1)} %add.17), channel_id=1, source_target_pairs={{0,5},{1,4},{2,7},{3,6},{4,1},{5,0},{6,3},{7,2},{8,13},{9,12},{10,... | collective-permute-start | bytes 49160 | tf_op jit(solution)/shard_map/ppermute | solution.py:221
  18.1 3.7 %collective-permute-start.5 = (f32[64,64]{1,0:T(8,128)S(1)}, f32[64,64]{1,0:T(8,128)S(1)}, u32[]{:S(2)}, u32[]{:S(2)}) collective-permute-start(f32[64,64]{1,0:T(8,128)S(1)} %add.18), channel_id=1, source_target_pairs={{0,9},{1,8},{2,11},{3,10},{4,13},{5,12},{6,15},{7,14},{8,1},{9,0},... | collective-permute-start | bytes 49160 | tf_op jit(solution)/shard_map/ppermute | solution.py:221
  21.8 4.4 %collective-permute-start.6 = (f32[64,64]{1,0:T(8,128)S(1)}, f32[64,64]{1,0:T(8,128)S(1)}, u32[]{:S(2)}, u32[]{:S(2)}) collective-permute-start(f32[64,64]{1,0:T(8,128)S(1)} %add.19.refs_0_), channel_id=1, source_target_pairs={{0,17},{1,16},{2,19},{3,18},{4,21},{5,20},{6,23},{7,22},{8,25},{9,... | collective-permute-start | bytes 49160 | tf_op jit(solution)/shard_map/ppermute | solution.py:221

commit v3 on v2

v3 whole, which is shorter than its diff:
```python
import functools
import math

import jax
import jax.numpy as jnp
from jax import lax
from jax.experimental import pallas as pl
from jax.experimental.pallas import tpu as pltpu
from jax.sharding import PartitionSpec as P

REACH = 2
AXES = ("rows", "sub")
SUBLANES, LANES = 8, 128
CHUNKS = 4
VMEM = pl.BlockSpec(memory_space=pltpu.VMEM)
SMEM = pl.BlockSpec(memory_space=pltpu.SMEM)
HBM = pl.BlockSpec(memory_space=pltpu.HBM)
PARAMS = pltpu.CompilerParams(vmem_limit_bytes=16 << 20)


def in_vmem(x):
    return pltpu.with_memory_space_constraint(x, pltpu.VMEM)


def in_hbm(x):
    return pltpu.with_memory_space_constraint(x, pltpu.HBM)


def rank_dot(a, b, contract, precision=None):
    return lax.dot_general(
        a, b, ((contract[:1], contract[1:]), ((), ())), precision=precision, preferred_element_type=jnp.float32
    )


def gram_of(image):
    return rank_dot(image, image, (1, 1), lax.Precision.HIGHEST)


def inverse_root(degrees_ref, piece):
    return lax.rsqrt(degrees_ref[pl.ds(piece, 1), :].astype(jnp.float32))


def block_root(degrees_ref, b, block):
    pieces = block // LANES
    return jnp.concatenate([inverse_root(degrees_ref, b * pieces + c) for c in range(pieces)], axis=1)


def scaled_piece(basis_ref, degrees_ref, piece):
    columns = slice(piece * LANES, (piece + 1) * LANES)
    if not isinstance(piece, int):
        columns = pl.ds(pl.multiple_of(piece * LANES, LANES), LANES)
    return (inverse_root(degrees_ref, piece) * basis_ref[:, columns].astype(jnp.float32)).astype(jnp.bfloat16)


def edges_kernel(
    width, place_ref, columns_hbm, basis_hbm, degrees_hbm, far_ref, columns_ref, basis_ref, degrees_ref, sems
):
    pieces, last = width // LANES, (basis_ref.shape[1] - width) // LANES
    copies = [
        pltpu.make_async_copy(degrees_hbm, degrees_ref, sems.at[0]),
        pltpu.make_async_copy(basis_hbm, basis_ref, sems.at[1]),
        pltpu.make_async_copy(columns_hbm, columns_ref, sems.at[2]),
    ]
    for copy in copies:
        copy.start()
    odd = place_ref[0] % 2
    for copy in copies:
        copy.wait()
    for i in range(pieces):
        far_ref[:, i * LANES:(i + 1) * LANES] = scaled_piece(basis_ref, degrees_ref, odd * last + i)


def own_kernel(
    count, block, edges, place_ref, columns_ref, basis_ref, degrees_ref, affinity_ref, near_ref, partial_ref, gram_ref,
    extended
):
    pieces = block // LANES
    for b in range(REACH):
        extended[b] = jnp.zeros_like(extended[b])
        extended[count + REACH + b] = jnp.zeros_like(extended[b])
    for piece in range(count * pieces):
        b, c = divmod(piece, pieces)
        extended[REACH + b, :, c * LANES:(c + 1) * LANES] = scaled_piece(basis_ref, degrees_ref, piece)
    odd = place_ref[0] % 2
    for b in range(REACH):
        near_ref[:, b * block:(b + 1) * block] = extended[REACH + (1 - odd) * (count - REACH) + b]
    first = place_ref[0] * count - REACH
    inner = []
    for b in range(count):
        total = rank_dot(extended[REACH + b], affinity_ref[b, 0], (1, 1))
        for slot in range(1, affinity_ref.shape[1]):
            total += rank_dot(extended[columns_ref[slot, b] - first], affinity_ref[b, slot], (1, 1))
        if b not in edges:
            total *= block_root(degrees_ref, b, block)
            inner.append(total)
        partial_ref[:, b * block:(b + 1) * block] = total
    if inner:
        gram_ref[...] = gram_of(jnp.concatenate(inner, axis=1))
    else:
        gram_ref[...] = jnp.zeros_like(gram_ref)


def halo_kernel(
    count, block, edges, place_ref, columns_ref, degrees_ref, near_ref, far_ref, affinity_ref, partial_ref, inner_ref,
    image_ref, gram_ref, halo
):
    odd = place_ref[0] % 2
    for b in range(REACH):
        halo[(1 - odd) * REACH + b] = near_ref[:, b * block:(b + 1) * block]
        halo[odd * REACH + b] = far_ref[:, b * block:(b + 1) * block]
    halo[2 * REACH] = jnp.zeros_like(halo[0])
    first = place_ref[0] * count - REACH
    images = []
    for at, b in enumerate(edges):
        total = partial_ref[:, b * block:(b + 1) * block]
        for slot in range(1, affinity_ref.shape[1]):
            index = columns_ref[slot, b] - first
            index = jnp.where(index < REACH, index, jnp.where(index < REACH + count, 2 * REACH, index - count))
            total += rank_dot(halo[index], affinity_ref[b, slot], (1, 1))
        images.append(total * block_root(degrees_ref, b, block))
        image_ref[:, at * block:(at + 1) * block] = images[-1]
    gram_ref[...] = inner_ref[...] + gram_of(jnp.concatenate(images, axis=1))


def reorder_kernel(count, block, edges, inner_ref, outer_ref, reorder_ref, placed_ref):
    source = lax.broadcasted_iota(jnp.int32, (block, block), 0)
    for b in range(count):
        at = edges.index(b) if b in edges else b
        image = (outer_ref if b in edges else inner_ref)[:, at * block:(at + 1) * block]
        high = image.astype(jnp.bfloat16)
        low = (image - high.astype(jnp.float32)).astype(jnp.bfloat16)
        chosen = jnp.where(source == reorder_ref[b:b + 1, :], 1.0, 0.0).astype(jnp.bfloat16)
        moved = rank_dot(jnp.concatenate([high, low], axis=0), chosen, (1, 0))
        moved = moved.astype(jnp.bfloat16)
        rank = image.shape[0]
        placed_ref[:2 * rank, b * block:(b + 1) * block] = moved
        placed_ref[2 * rank:, b * block:(b + 1) * block] = moved[:rank]


def along_lanes(x, column):
    return jnp.broadcast_to(x[:, column:column + 1], (SUBLANES, LANES))


def along_sublanes(x, row):
    return jnp.broadcast_to(x[row:row + 1, :], (SUBLANES, LANES))


def inverse_factor(gram):
    rank = gram.shape[0]
    tiles, per = rank // SUBLANES, 2
    size = per * SUBLANES
    rows = lax.broadcasted_iota(jnp.int32, (rank, rank), 0)
    columns = lax.broadcasted_iota(jnp.int32, (rank, rank), 1)
    state = jnp.concatenate([gram, jnp.where(rows == columns, 1.0, 0.0)], axis=1)
    state = [state[SUBLANES * t:SUBLANES * (t + 1)] for t in range(tiles)]
    sublane = lax.broadcasted_iota(jnp.int32, (SUBLANES, LANES), 0)
    for top in range(0, tiles, per):
        at = top * SUBLANES
        live = [{t: along_lanes(state[t], at + j) for t in range(top, tiles)} for j in range(size)]
        diagonal = {}
        pivot = along_sublanes(live[0][top], 0)
        for i in range(size):
            tile, s = top + i // SUBLANES, i % SUBLANES
            inverse = 1.0 / pivot
            diagonal[tile] = jnp.where(sublane == s, pivot, diagonal[tile]) if s else pivot
            ahead = {j: along_sublanes(live[j][tile], s) for j in range(i + 1, size)}
            if ahead:
                tile_next, s_next = top + (i + 1) // SUBLANES, (i + 1) % SUBLANES
                pivot = along_sublanes(live[i + 1][tile_next], s_next) - along_sublanes(
                    live[i][tile_next], s_next
                ) * (ahead[i + 1] * inverse)
            row = along_sublanes(state[tile], s)
            for t in range(tile, tiles):
                column = live[i][t] * inverse
                for j in ahead:
                    live[j][t] = live[j][t] - column * ahead[j]
                if t == tile:
                    column = jnp.where(sublane > s, column, 0.0)
                state[t] = state[t] - column * row
        for t in range(top, top + per):
            state[t] = state[t] * lax.rsqrt(diagonal[t])
    return jnp.concatenate(state, axis=0)[:, rank:]


def targets_kernel(total_items, parts, *refs):
    placed_ref, targets_hbm, targets_ref, sems = refs[parts:]
    gram = refs[0][...]
    for part in refs[1:parts]:
        gram = gram + part[...]
    inverse = inverse_factor(gram) * math.sqrt(total_items)
    high = inverse.astype(jnp.bfloat16)
    low = (inverse - high.astype(jnp.float32)).astype(jnp.bfloat16)
    left = jnp.concatenate([high, high, low], axis=1)
    chunk = targets_ref.shape[1] // CHUNKS
    copies = []
    for c in range(CHUNKS):
        columns = slice(c * chunk, (c + 1) * chunk)
        targets_ref[:, columns] = rank_dot(left, placed_ref[:, columns], (1, 0))
        copies.append(pltpu.make_async_copy(targets_ref.at[:, columns], targets_hbm.at[:, columns], sems.at[c]))
        copies[-1].start()
    for copy in copies:
        copy.wait()


def gram_parts(gram, mesh_size):
    if mesh_size & (mesh_size - 1):
        return [lax.psum(gram, AXES)]
    bits = [1 << k for k in range(mesh_size.bit_length() - 2, 0, -1)]
    rounds = [[1]] + [[bit | 1] for bit in bits[:-2]]
    if bits:
        rounds.append([bit | 1 for bit in bits[:-3:-1]] + [sum(bits[-2:])] * (len(bits) > 1))
    parts = [gram]
    for masks in rounds:
        gram = sum(parts[1:], parts[0])
        parts = [gram] + [lax.ppermute(gram, AXES, [(i, i ^ mask) for i in range(mesh_size)]) for mask in masks]
    return parts


def body(mesh_size, affinity, old_basis, degrees, column_blocks, reorder):
    count, slots, block, _ = affinity.shape
    items, rank = old_basis.shape
    width = REACH * block
    edges = [b for b in range(count) if b < REACH or b >= count - REACH]
    affinity = in_vmem(affinity)
    basis = old_basis.T
    degree_rows = degrees.reshape(items // LANES, LANES)
    columns = column_blocks.T
    place = lax.axis_index(AXES).astype(jnp.int32).reshape(1)
    square = pltpu.VMEM((rank, rank), jnp.float32)

    far, columns, basis, degree_rows = pl.pallas_call(
        functools.partial(edges_kernel, width),
        out_shape=(
            pltpu.VMEM((rank, width), jnp.bfloat16),
            pltpu.SMEM(columns.shape, jnp.int32),
            pltpu.VMEM(basis.shape, jnp.bfloat16),
            pltpu.VMEM(degree_rows.shape, jnp.int32),
        ),
        in_specs=[SMEM, HBM, HBM, HBM],
        out_specs=(VMEM, SMEM, VMEM, VMEM),
        scratch_shapes=[pltpu.SemaphoreType.DMA((3,))],
        compiler_params=PARAMS,
        cost_estimate=pl.CostEstimate(flops=1000 * affinity.size, bytes_accessed=40 * affinity.size, transcendentals=0),
        name="edges",
    )(place, *map(in_hbm, (columns, basis, degree_rows)))
    crossing = range(1, mesh_size - 1, 2)
    far = lax.ppermute(far, AXES, [(i, i + 1) for i in crossing] + [(i + 1, i) for i in crossing])

    near, partial, inner = pl.pallas_call(
        functools.partial(own_kernel, count, block, edges),
        out_shape=(
            pltpu.VMEM((rank, width), jnp.bfloat16),
            pltpu.VMEM((rank, items), jnp.float32),
            square,
        ),
        in_specs=[SMEM, SMEM] + [VMEM] * 3,
        out_specs=(VMEM,) * 3,
        scratch_shapes=[pltpu.VMEM((count + 2 * REACH, rank, block), jnp.bfloat16)],
        compiler_params=PARAMS,
        cost_estimate=pl.CostEstimate(
            flops=2 * count * slots * block * block * rank, bytes_accessed=0, transcendentals=0
        ),
        name="own",
    )(place, columns, *map(in_vmem, (basis, degree_rows)), affinity)
    near = lax.ppermute(near, AXES, [(i, i ^ 1) for i in range(mesh_size) if i ^ 1 < mesh_size])

    outer, gram = pl.pallas_call(
        functools.partial(halo_kernel, count, block, edges),
        out_shape=(pltpu.VMEM((rank, len(edges) * block), jnp.float32), square),
        in_specs=[SMEM, SMEM] + [VMEM] * 6,
        out_specs=(VMEM, VMEM),
        scratch_shapes=[pltpu.VMEM((2 * REACH + 1, rank, block), jnp.bfloat16)],
        compiler_params=PARAMS,
        name="halo",
    )(place, columns, *map(in_vmem, (degree_rows, near, far)), affinity, *map(in_vmem, (partial, inner)))

    placed = pl.pallas_call(
        functools.partial(reorder_kernel, count, block, edges),
        out_shape=pltpu.VMEM((3 * rank, items), jnp.bfloat16),
        in_specs=[VMEM] * 3,
        out_specs=VMEM,
        compiler_params=PARAMS,
        cost_estimate=pl.CostEstimate(flops=4 * rank * items * block, bytes_accessed=0, transcendentals=0),
        name="reorder",
    )(in_vmem(partial), in_vmem(outer), in_vmem(reorder))

    parts = gram_parts(gram, mesh_size)
    targets = pl.pallas_call(
        functools.partial(targets_kernel, items * mesh_size, len(parts)),
        out_shape=jax.ShapeDtypeStruct((rank, items), jnp.float32),
        in_specs=[VMEM] * (len(parts) + 1),
        out_specs=HBM,
        scratch_shapes=[pltpu.VMEM((rank, items), jnp.float32), pltpu.SemaphoreType.DMA((CHUNKS,))],
        compiler_params=PARAMS,
        name="targets",
    )(*map(in_vmem, parts), in_vmem(placed))
    return targets.T


def solution(mesh):
    placed = (
        P(AXES, None, None, None),
        P(AXES, None),
        P(AXES),
        P(AXES, None),
        P(AXES, None),
    )
    mesh_size = mesh.shape["rows"] * mesh.shape["sub"]
    return jax.shard_map(
        functools.partial(body, mesh_size), mesh=mesh, in_specs=placed, out_specs=P(AXES, None), check_vma=False
    )
```

time: 29.6 us -> 27.5 us (0.929)
  Pallas kernels: 7.79 us -> 5.95 us
  starting transfers between devices: 14.7 us -> 14.1 us
    ppermute x5 -> x6, starting transfers between devices: 13.5 us -> 9.18 us  [gram_parts(): lax.ppermute(gram, AXES, [(i, i ^ mask) for i in range(mesh_size)])]
    ppermute x1, starting transfers between devices: 0.52 us -> 4.26 us  [body(): lax.ppermute(near, AXES, [(i, i ^ 1) for i in range(mesh_size) if i ^ 1 <...]
    pallas_call x1, Pallas kernels: 2.3 us -> 1.3 us  [body(): pl.pallas_call(functools.partial(own_kernel, count, block, edges), out_sh...]
    pallas_call x1, Pallas kernels: 3.32 us -> 2.42 us  [body(): pl.pallas_call(functools.partial(targets_kernel, items * mesh_size, len(p...]
    ppermute x1, waiting for transfers between devices: 0.01 us -> 0.9 us  [body(): lax.ppermute(near, AXES, [(i, i ^ 1) for i in range(mesh_size) if i ^ 1 <...]
    ppermute x5 -> x6, waiting for transfers between devices: 6.89 us -> 6.25 us  [gram_parts(): lax.ppermute(gram, AXES, [(i, i ^ mask) for i in range(mesh_size)])]
  transfers between devices with their start and end apart: 7 -> 8, of which waited for: 5 -> 6; matrix products, arithmetic and copies ran while one was open for 0% -> 0% of each run, Pallas kernels for 9% -> 6%
where the time goes in v3:
time: 27.5 us; the launch traced here: 27.4 us
  starting transfers between devices  14.1 us (51%)
  waiting for transfers between devices  7.15 us (26%)
  Pallas kernels  5.95 us (22%)
    ppermute x6, starting transfers between devices, gram_parts(): lax.ppermute(gram, AXES, [(i, i ^ mask) for i in range(mesh_size)])  9.18 us
    ppermute x6, waiting for transfers between devices, gram_parts(): lax.ppermute(gram, AXES, [(i, i ^ mask) for i in range(mesh_size)])  6.25 us
    ppermute x1, starting transfers between devices, body(): lax.ppermute(near, AXES, [(i, i ^ 1) for i in range(mesh_size) if i ^ 1 <...  4.26 us
    pallas_call x1, Pallas kernels, body(): pl.pallas_call(functools.partial(targets_kernel, items * mesh_size, len(p...  2.42 us
    pallas_call x1, Pallas kernels, body(): pl.pallas_call(functools.partial(own_kernel, count, block, edges), out_sh...  1.3 us
    pallas_call x1, Pallas kernels, body(): pl.pallas_call(functools.partial(edges_kernel, width), out_shape=(pltpu.V...  1.17 us
    ppermute x1, waiting for transfers between devices, body(): lax.ppermute(near, AXES, [(i, i ^ 1) for i in range(mesh_size) if i ^ 1 <...  0.9 us
    pallas_call x1, Pallas kernels, body(): pl.pallas_call(functools.partial(halo_kernel, count, block, edges), out_s...  0.7 us
  transfers between devices with their start and end apart: 8, of which 6 were waited for; matrix products, arithmetic and copies ran while one was open for 0% of the time, Pallas kernels for 6%

profile of v3, /device:TPU:0, one launch (start us, length us, event | category | flops | bytes accessed | tf_op | source)
XLA Modules:
  0.0 27.4 jit_solution(6471376839445913962)
XLA Ops:
  0.0 0.0 copy-start
  0.0 1.2 %edges.1 = (bf16[64,512]{1,0:T(8,128)(2,1)S(1)}, s32[3,8]{1,0:T(4,128)S(4)}, bf16[64,2048]{1,0:T(8,128)(2,1)S(1)}, s32[16,128]{1,0:T(8,128)S(1)}) custom-call(s32[1]{0:T(128)} %bitcast.place_ref, s32[3,8]{1,0:T(4,128)} %bitcast.7, bf16[64,2048]{1,0:T(8,128)(2,1)} %bitcast.5, s32[16,128]{1,0:T(8,128)} %bitcast.6), custom_call_target="tpu_custom_call" | custom-call | flops 1572864000 | bytes 62914560 | tf_op jit(solution)/shard_map/edges/pallas_call | solution.py:231
  1.2 0.7 %collective-permute-start.1 = (bf16[64,512]{1,0:T(8,128)(2,1)S(1)}, bf16[64,512]{1,0:T(8,128)(2,1)S(1)}, u32[]{:S(2)}, u32[]{:S(2)}) collective-permute-start(bf16[64,512]{1,0:T(8,128)(2,1)S(1)} %get-tuple-element.18), channel_id=1, source_target_pairs={{1,2},{3,4},{5,6},{7,8},{9,10},{11,12},{13,14},{15,16},{17,18},{19... | collective-permute-start | bytes 196616 | tf_op jit(solution)/shard_map/ppermute | solution.py:247
  1.9 0.1 copy-done
  2.0 0.0 copy-start.1
  2.0 1.3 %own.1 = (bf16[64,512]{1,0:T(8,128)(2,1)S(1)}, f32[64,2048]{1,0:T(8,128)S(1)}, f32[64,64]{1,0:T(8,128)S(1)}) custom-call(s32[1]{0:T(128)} %bitcast.place_ref, s32[3,8]{1,0:T(4,128)S(4)} %get-tuple-element.14.columns_ref, bf16[64,2048]{1,0:T(8,128)(2,1)S(1)} %get-tuple-element.16.basis_ref, s32[16,128]{1,0:T(8,128)S(1)} %get-tuple-element.15.degrees_ref, ...), custom_call_target="tpu_custom_call" | custom-call | flops 201326592 | tf_op jit(solution)/shard_map/own/pallas_call | solution.py:249
  3.3 4.3 %collective-permute-start = (bf16[64,512]{1,0:T(8,128)(2,1)S(1)}, bf16[64,512]{1,0:T(8,128)(2,1)S(1)}, u32[]{:S(2)}, u32[]{:S(2)}) collective-permute-start(bf16[64,512]{1,0:T(8,128)(2,1)S(1)} %get-tuple-element.17), channel_id=1, source_target_pairs={{0,1},{1,0},{2,3},{3,2},{4,5},{5,4},{6,7},{7,6},{8,9},{9,8},{10,11... | collective-permute-start | bytes 196616 | tf_op jit(solution)/shard_map/ppermute | solution.py:265
  7.6 0.0 collective-permute-done.1.far_ref
  7.6 0.9 %collective-permute-done.near_ref = bf16[64,512]{1,0:T(8,128)(2,1)S(1)} collective-permute-done((bf16[64,512]{1,0:T(8,128)(2,1)S(1)}, bf16[64,512]{1,0:T(8,128)(2,1)S(1)}, u32[]{:S(2)}, u32[]{:S(2)}) %collective-permute-start) | collective-permute-done | bytes 65568 | tf_op jit(solution)/shard_map/ppermute | solution.py:265
  8.5 0.7 %halo.1 = (f32[64,1024]{1,0:T(8,128)S(1)}, f32[64,64]{1,0:T(8,128)S(1)}) custom-call(s32[1]{0:T(128)} %bitcast.place_ref, s32[3,8]{1,0:T(4,128)S(4)} %get-tuple-element.14.columns_ref, s32[16,128]{1,0:T(8,128)S(1)} %get-tuple-element.15.degrees_ref, bf16[64,512]{1,0:T(8,128)(2,1)S(1)} %collective-permute-done.near_ref, ...), custom_call_target="tpu_custom_call" | custom-call | tf_op jit(solution)/shard_map/halo/pallas_call | solution.py:267
  9.2 0.4 %collective-permute-start.2 = (f32[64,64]{1,0:T(8,128)S(1)}, f32[64,64]{1,0:T(8,128)S(1)}, u32[]{:S(2)}, u32[]{:S(2)}) collective-permute-start(f32[64,64]{1,0:T(8,128)S(1)} %get-tuple-element.21), channel_id=1, source_target_pairs={{0,1},{1,0},{2,3},{3,2},{4,5},{5,4},{6,7},{7,6},{8,9},{9,8},{10,11... | collective-permute-start | bytes 49160 | tf_op jit(solution)/shard_map/ppermute | solution.py:215
  9.6 0.9 %collective-permute-done.2 = f32[64,64]{1,0:T(8,128)S(1)} collective-permute-done((f32[64,64]{1,0:T(8,128)S(1)}, f32[64,64]{1,0:T(8,128)S(1)}, u32[]{:S(2)}, u32[]{:S(2)}) %collective-permute-start.2) | collective-permute-done | bytes 16416 | tf_op jit(solution)/shard_map/ppermute | solution.py:215
  10.4 3.9 %collective-permute-start.3 = (f32[64,64]{1,0:T(8,128)S(1)}, f32[64,64]{1,0:T(8,128)S(1)}, u32[]{:S(2)}, u32[]{:S(2)}) collective-permute-start(f32[64,64]{1,0:T(8,128)S(1)} %add.13), channel_id=1, source_target_pairs={{0,17},{1,16},{2,19},{3,18},{4,21},{5,20},{6,23},{7,22},{8,25},{9,... | collective-permute-start | bytes 49160 | tf_op jit(solution)/shard_map/ppermute | solution.py:215
  14.4 1.6 %collective-permute-done.3 = f32[64,64]{1,0:T(8,128)S(1)} collective-permute-done((f32[64,64]{1,0:T(8,128)S(1)}, f32[64,64]{1,0:T(8,128)S(1)}, u32[]{:S(2)}, u32[]{:S(2)}) %collective-permute-start.3) | collective-permute-done | bytes 16416 | tf_op jit(solution)/shard_map/ppermute | solution.py:215
  16.0 1.6 %collective-permute-start.4 = (f32[64,64]{1,0:T(8,128)S(1)}, f32[64,64]{1,0:T(8,128)S(1)}, u32[]{:S(2)}, u32[]{:S(2)}) collective-permute-start(f32[64,64]{1,0:T(8,128)S(1)} %add.14), channel_id=1, source_target_pairs={{0,9},{1,8},{2,11},{3,10},{4,13},{5,12},{6,15},{7,14},{8,1},{9,0},... | collective-permute-start | bytes 49160 | tf_op jit(solution)/shard_map/ppermute | solution.py:215
  17.6 1.7 %collective-permute-done.4 = f32[64,64]{1,0:T(8,128)S(1)} collective-permute-done((f32[64,64]{1,0:T(8,128)S(1)}, f32[64,64]{1,0:T(8,128)S(1)}, u32[]{:S(2)}, u32[]{:S(2)}) %collective-permute-start.4) | collective-permute-done | bytes 16416 | tf_op jit(solution)/shard_map/ppermute | solution.py:215
  19.3 2.2 %collective-permute-start.7 = (f32[64,64]{1,0:T(8,128)S(1)}, f32[64,64]{1,0:T(8,128)S(1)}, u32[]{:S(2)}, u32[]{:S(2)}) collective-permute-start(f32[64,64]{1,0:T(8,128)S(1)} %add.15.refs_0_), channel_id=1, source_target_pairs={{0,6},{1,7},{2,4},{3,5},{4,2},{5,3},{6,0},{7,1},{8,14},{9,15},{10,... | collective-permute-start | bytes 49160 | tf_op jit(solution)/shard_map/ppermute | solution.py:215
  21.5 0.0 collective-permute-start.6
  21.5 1.0 %collective-permute-start.5 = (f32[64,64]{1,0:T(8,128)S(1)}, f32[64,64]{1,0:T(8,128)S(1)}, u32[]{:S(2)}, u32[]{:S(2)}) collective-permute-start(f32[64,64]{1,0:T(8,128)S(1)} %add.15.refs_0_), channel_id=1, source_target_pairs={{0,3},{1,2},{2,1},{3,0},{4,7},{5,6},{6,5},{7,4},{8,11},{9,10},{10,... | collective-permute-start | bytes 49160 | tf_op jit(solution)/shard_map/ppermute | solution.py:215
  22.5 0.0 copy-done.1
  22.5 0.4 %reorder.1.refs_4_ = bf16[192,2048]{1,0:T(8,128)(2,1)S(1)} custom-call(f32[64,2048]{1,0:T(8,128)S(1)} %get-tuple-element.19.partial_ref.inner_ref, f32[64,1024]{1,0:T(8,128)S(1)} %get-tuple-element.22.outer_ref, s32[8,256]{1,0:T(8,128)S(1)} %copy-done.1), custom_call_target="tpu_custom_call" | custom-call | flops 134217728 | tf_op jit(solution)/shard_map/reorder/pallas_call | solution.py:277
  22.9 1.2 %collective-permute-done.7.refs_3_ = f32[64,64]{1,0:T(8,128)S(1)} collective-permute-done((f32[64,64]{1,0:T(8,128)S(1)}, f32[64,64]{1,0:T(8,128)S(1)}, u32[]{:S(2)}, u32[]{:S(2)}) %collective-permute-start.7) | collective-permute-done | bytes 16416 | tf_op jit(solution)/shard_map/ppermute | solution.py:215
  24.1 0.8 %collective-permute-done.6.refs_2_ = f32[64,64]{1,0:T(8,128)S(1)} collective-permute-done((f32[64,64]{1,0:T(8,128)S(1)}, f32[64,64]{1,0:T(8,128)S(1)}, u32[]{:S(2)}, u32[]{:S(2)}) %collective-permute-start.6) | collective-permute-done | bytes 16416 | tf_op jit(solution)/shard_map/ppermute | solution.py:215
  25.0 0.0 collective-permute-done.5.refs_1_
  25.0 2.4 %targets.1 = f32[64,2048]{1,0:T(8,128)} custom-call(f32[64,64]{1,0:T(8,128)S(1)} %add.15.refs_0_, f32[64,64]{1,0:T(8,128)S(1)} %collective-permute-done.5.refs_1_, f32[64,64]{1,0:T(8,128)S(1)} %collective-permute-done.6.refs_2_, f32[64,64]{1,0:T(8,128)S(1)} %collective-permute-done.7.refs_3_, bf16[192,2048]{1,0:T(8,128)(2,1)S(1)} %reorder.1.refs_4_), custom_call_target="tpu_custom_call" | custom-call | tf_op jit(solution)/shard_map/targets/pallas_call | solution.py:288
  (3 shorter events, 0.0 us)
Async XLA Ops:
  0.0 2.0 %copy-start = (bf16[8,3,256,256]{3,2,1,0:T(8,128)(2,1)S(1)}, bf16[8,3,256,256]{3,2,1,0:T(8,128)(2,1)}, u32[]{:S(2)}) copy-start(bf16[8,3,256,256]{3,2,1,0:T(8,128)(2,1)} %affinity_ref.3) | copy-start | bytes 9437188
  1.2 6.4 %collective-permute-start.1 = (bf16[64,512]{1,0:T(8,128)(2,1)S(1)}, bf16[64,512]{1,0:T(8,128)(2,1)S(1)}, u32[]{:S(2)}, u32[]{:S(2)}) collective-permute-start(bf16[64,512]{1,0:T(8,128)(2,1)S(1)} %get-tuple-element.18), channel_id=1, source_target_pairs={{1,2},{3,4},{5,6},{7,8},{9,10},{11,12},{13,14},{15,16},{17,18},{19... | collective-permute-start | bytes 196616 | tf_op jit(solution)/shard_map/ppermute | solution.py:247
  2.0 20.5 %copy-start.1 = (s32[8,256]{1,0:T(8,128)S(1)}, s32[8,256]{1,0:T(8,128)}, u32[]{:S(2)}) copy-start(s32[8,256]{1,0:T(8,128)} %reorder_ref.1) | copy-start | bytes 24580
  3.3 5.2 %collective-permute-start = (bf16[64,512]{1,0:T(8,128)(2,1)S(1)}, bf16[64,512]{1,0:T(8,128)(2,1)S(1)}, u32[]{:S(2)}, u32[]{:S(2)}) collective-permute-start(bf16[64,512]{1,0:T(8,128)(2,1)S(1)} %get-tuple-element.17), channel_id=1, source_target_pairs={{0,1},{1,0},{2,3},{3,2},{4,5},{5,4},{6,7},{7,6},{8,9},{9,8},{10,11... | collective-permute-start | bytes 196616 | tf_op jit(solution)/shard_map/ppermute | solution.py:265
  9.2 1.3 %collective-permute-start.2 = (f32[64,64]{1,0:T(8,128)S(1)}, f32[64,64]{1,0:T(8,128)S(1)}, u32[]{:S(2)}, u32[]{:S(2)}) collective-permute-start(f32[64,64]{1,0:T(8,128)S(1)} %get-tuple-element.21), channel_id=1, source_target_pairs={{0,1},{1,0},{2,3},{3,2},{4,5},{5,4},{6,7},{7,6},{8,9},{9,8},{10,11... | collective-permute-start | bytes 49160 | tf_op jit(solution)/shard_map/ppermute | solution.py:215
  10.4 5.5 %collective-permute-start.3 = (f32[64,64]{1,0:T(8,128)S(1)}, f32[64,64]{1,0:T(8,128)S(1)}, u32[]{:S(2)}, u32[]{:S(2)}) collective-permute-start(f32[64,64]{1,0:T(8,128)S(1)} %add.13), channel_id=1, source_target_pairs={{0,17},{1,16},{2,19},{3,18},{4,21},{5,20},{6,23},{7,22},{8,25},{9,... | collective-permute-start | bytes 49160 | tf_op jit(solution)/shard_map/ppermute | solution.py:215
  16.0 3.3 %collective-permute-start.4 = (f32[64,64]{1,0:T(8,128)S(1)}, f32[64,64]{1,0:T(8,128)S(1)}, u32[]{:S(2)}, u32[]{:S(2)}) collective-permute-start(f32[64,64]{1,0:T(8,128)S(1)} %add.14), channel_id=1, source_target_pairs={{0,9},{1,8},{2,11},{3,10},{4,13},{5,12},{6,15},{7,14},{8,1},{9,0},... | collective-permute-start | bytes 49160 | tf_op jit(solution)/shard_map/ppermute | solution.py:215
  19.3 4.8 %collective-permute-start.7 = (f32[64,64]{1,0:T(8,128)S(1)}, f32[64,64]{1,0:T(8,128)S(1)}, u32[]{:S(2)}, u32[]{:S(2)}) collective-permute-start(f32[64,64]{1,0:T(8,128)S(1)} %add.15.refs_0_), channel_id=1, source_target_pairs={{0,6},{1,7},{2,4},{3,5},{4,2},{5,3},{6,0},{7,1},{8,14},{9,15},{10,... | collective-permute-start | bytes 49160 | tf_op jit(solution)/shard_map/ppermute | solution.py:215
  21.5 3.4 %collective-permute-start.6 = (f32[64,64]{1,0:T(8,128)S(1)}, f32[64,64]{1,0:T(8,128)S(1)}, u32[]{:S(2)}, u32[]{:S(2)}) collective-permute-start(f32[64,64]{1,0:T(8,128)S(1)} %add.15.refs_0_), channel_id=1, source_target_pairs={{0,5},{1,4},{2,7},{3,6},{4,1},{5,0},{6,3},{7,2},{8,13},{9,12},{10,... | collective-permute-start | bytes 49160 | tf_op jit(solution)/shard_map/ppermute | solution.py:215
  21.5 3.4 %collective-permute-start.5 = (f32[64,64]{1,0:T(8,128)S(1)}, f32[64,64]{1,0:T(8,128)S(1)}, u32[]{:S(2)}, u32[]{:S(2)}) collective-permute-start(f32[64,64]{1,0:T(8,128)S(1)} %add.15.refs_0_), channel_id=1, source_target_pairs={{0,3},{1,2},{2,1},{3,0},{4,7},{5,6},{6,5},{7,4},{8,11},{9,10},{10,... | collective-permute-start | bytes 49160 | tf_op jit(solution)/shard_map/ppermute | solution.py:215

commit v4 on v3

--- a/solution.py
+++ b/solution.py
@@ -101,13 +101,15 @@
 
 
 def halo_kernel(
-    count, block, edges, place_ref, columns_ref, degrees_ref, near_ref, far_ref, affinity_ref, partial_ref, inner_ref,
-    image_ref, gram_ref, halo
+    count, block, edges, late, place_ref, columns_ref, degrees_ref, near_ref, rest_ref, most_ref, affinity_ref, partial_ref,
+    own_gram_ref, image_ref, gram_ref, halo
 ):
     odd = place_ref[0] % 2
+    is_late = (place_ref[0] == late[0]) | (place_ref[0] == late[1])
     for b in range(REACH):
-        halo[(1 - odd) * REACH + b] = near_ref[:, b * block:(b + 1) * block]
-        halo[odd * REACH + b] = far_ref[:, b * block:(b + 1) * block]
+        columns = slice(b * block, (b + 1) * block)
+        halo[(1 - odd) * REACH + b] = near_ref[:, columns]
+        halo[odd * REACH + b] = jnp.where(is_late, rest_ref[:, columns], most_ref[:, columns])
     halo[2 * REACH] = jnp.zeros_like(halo[0])
     first = place_ref[0] * count - REACH
     images = []
@@ -119,7 +121,9 @@
             total += rank_dot(halo[index], affinity_ref[b, slot], (1, 1))
         images.append(total * block_root(degrees_ref, b, block))
         image_ref[:, at * block:(at + 1) * block] = images[-1]
-    gram_ref[...] = inner_ref[...] + gram_of(jnp.concatenate(images, axis=1))
+    gram = own_gram_ref[...] + gram_of(jnp.concatenate(images, axis=1))
+    half = gram.shape[0] // 2
+    gram_ref[...] = jnp.concatenate([gram[:half], gram[half:]], axis=1)
 
 
 def reorder_kernel(count, block, edges, inner_ref, outer_ref, reorder_ref, placed_ref):
@@ -145,13 +149,14 @@
     return jnp.broadcast_to(x[row:row + 1, :], (SUBLANES, LANES))
 
 
-def inverse_factor(gram):
-    rank = gram.shape[0]
+def inverse_factor(folded):
+    rank = folded.shape[1] // 2
     tiles, per = rank // SUBLANES, 2
     size = per * SUBLANES
-    rows = lax.broadcasted_iota(jnp.int32, (rank, rank), 0)
-    columns = lax.broadcasted_iota(jnp.int32, (rank, rank), 1)
-    state = jnp.concatenate([gram, jnp.where(rows == columns, 1.0, 0.0)], axis=1)
+    rows = lax.broadcasted_iota(jnp.int32, (rank, 2 * rank), 0)
+    columns = lax.broadcasted_iota(jnp.int32, (rank, 2 * rank), 1)
+    state = jnp.concatenate([folded, pltpu.roll(folded, rank, 1)], axis=0)
+    state = jnp.where(columns < rank, state, jnp.where(columns - rank == rows, 1.0, 0.0))
     state = [state[SUBLANES * t:SUBLANES * (t + 1)] for t in range(tiles)]
     sublane = lax.broadcasted_iota(jnp.int32, (SUBLANES, LANES), 0)
     for top in range(0, tiles, per):
@@ -216,6 +221,22 @@
     return parts
 
 
+def cycle(*devices):
+    return list(zip(devices, devices[1:] + devices[:1]))
+
+
+def crossing_pairs(mesh_size):
+    n = mesh_size
+    if n % 2 or n < 8:
+        pairs = [pair for i in range(1, n - 1, 2) for pair in cycle(i, i + 1)]
+        return [pairs, pairs]
+    most = [pair for i in range(3, n - 4, 2) for pair in cycle(i, i + 1)]
+    most += cycle(2, 1, 0) + cycle(n - 3, n - 2, n - 1)
+    rest = [pair for i in range(4, n - 4, 2) for pair in cycle(i, i + 1)]
+    rest += cycle(1, 2, 3, 0) + cycle(n - 2, n - 3, n - 4, n - 1)
+    return [rest, most]
+
+
 def body(mesh_size, affinity, old_basis, degrees, column_blocks, reorder):
     count, slots, block, _ = affinity.shape
     items, rank = old_basis.shape
@@ -226,7 +247,7 @@
     degree_rows = degrees.reshape(items // LANES, LANES)
     columns = column_blocks.T
     place = lax.axis_index(AXES).astype(jnp.int32).reshape(1)
-    square = pltpu.VMEM((rank, rank), jnp.float32)
+    folded = pltpu.VMEM((rank // 2, 2 * rank), jnp.float32)
 
     far, columns, basis, degree_rows = pl.pallas_call(
         functools.partial(edges_kernel, width),
@@ -243,15 +264,14 @@
         cost_estimate=pl.CostEstimate(flops=1000 * affinity.size, bytes_accessed=40 * affinity.size, transcendentals=0),
         name="edges",
     )(place, *map(in_hbm, (columns, basis, degree_rows)))
-    crossing = range(1, mesh_size - 1, 2)
-    far = lax.ppermute(far, AXES, [(i, i + 1) for i in crossing] + [(i + 1, i) for i in crossing])
+    distant = [lax.ppermute(far, AXES, pairs) for pairs in crossing_pairs(mesh_size)]
 
     near, partial, inner = pl.pallas_call(
         functools.partial(own_kernel, count, block, edges),
         out_shape=(
             pltpu.VMEM((rank, width), jnp.bfloat16),
             pltpu.VMEM((rank, items), jnp.float32),
-            square,
+            pltpu.VMEM((rank, rank), jnp.float32),
         ),
         in_specs=[SMEM, SMEM] + [VMEM] * 3,
         out_specs=(VMEM,) * 3,
@@ -265,14 +285,14 @@
     near = lax.ppermute(near, AXES, [(i, i ^ 1) for i in range(mesh_size) if i ^ 1 < mesh_size])
 
     outer, gram = pl.pallas_call(
-        functools.partial(halo_kernel, count, block, edges),
-        out_shape=(pltpu.VMEM((rank, len(edges) * block), jnp.float32), square),
-        in_specs=[SMEM, SMEM] + [VMEM] * 6,
+        functools.partial(halo_kernel, count, block, edges, (2, mesh_size - 3)),
+        out_shape=(pltpu.VMEM((rank, len(edges) * block), jnp.float32), folded),
+        in_specs=[SMEM, SMEM] + [VMEM] * 7,
         out_specs=(VMEM, VMEM),
         scratch_shapes=[pltpu.VMEM((2 * REACH + 1, rank, block), jnp.bfloat16)],
         compiler_params=PARAMS,
         name="halo",
-    )(place, columns, *map(in_vmem, (degree_rows, near, far)), affinity, *map(in_vmem, (partial, inner)))
+    )(place, columns, *map(in_vmem, (degree_rows, near, *distant)), affinity, *map(in_vmem, (partial, inner)))
 
     placed = pl.pallas_call(
         functools.partial(reorder_kernel, count, block, edges),

time: 27.5 us -> 25 us (0.909)
  starting transfers between devices: 14.1 us -> 10.4 us
  waiting for transfers between devices: 7.15 us -> 8.4 us
    ppermute x1, starting transfers between devices: 4.26 us -> 0.23 us  [body(): lax.ppermute(near, AXES, [(i, i ^ 1) for i in range(mesh_size) if i ^ 1 <...]
    ppermute x1 -> x2, starting transfers between devices: 0.66 us -> 2.99 us  [body(): lax.ppermute(far, AXES, pairs)]
    ppermute x1 -> x2, waiting for transfers between devices: 0.01 us -> 2.31 us  [body(): lax.ppermute(far, AXES, pairs)]
    ppermute x6, starting transfers between devices: 9.18 us -> 7.21 us  [gram_parts(): lax.ppermute(gram, AXES, [(i, i ^ mask) for i in range(mesh_size)])]
    ppermute x1, waiting for transfers between devices: 0.9 us -> 0.01 us  [body(): lax.ppermute(near, AXES, [(i, i ^ 1) for i in range(mesh_size) if i ^ 1 <...]
  transfers between devices with their start and end apart: 8 -> 9, of which waited for: 6 -> 7; matrix products, arithmetic and copies ran while one was open for 0% -> 0% of each run, Pallas kernels for 6% -> 7%
where the time goes in v4:
time: 25 us; the launch traced here: 24.9 us
  starting transfers between devices  10.4 us (42%)
  waiting for transfers between devices  8.4 us (34%)
  Pallas kernels  5.96 us (24%)
    ppermute x6, starting transfers between devices, gram_parts(): lax.ppermute(gram, AXES, [(i, i ^ mask) for i in range(mesh_size)])  7.21 us
    ppermute x6, waiting for transfers between devices, gram_parts(): lax.ppermute(gram, AXES, [(i, i ^ mask) for i in range(mesh_size)])  6.09 us
    ppermute x2, starting transfers between devices, body(): lax.ppermute(far, AXES, pairs)  2.99 us
    pallas_call x1, Pallas kernels, body(): pl.pallas_call(functools.partial(targets_kernel, items * mesh_size, len(p...  2.35 us
    ppermute x2, waiting for transfers between devices, body(): lax.ppermute(far, AXES, pairs)  2.31 us
    pallas_call x1, Pallas kernels, body(): pl.pallas_call(functools.partial(own_kernel, count, block, edges), out_sh...  1.3 us
    pallas_call x1, Pallas kernels, body(): pl.pallas_call(functools.partial(edges_kernel, width), out_shape=(pltpu.V...  1.17 us
    pallas_call x1, Pallas kernels, body(): pl.pallas_call(functools.partial(halo_kernel, count, block, edges, (2, me...  0.77 us
  transfers between devices with their start and end apart: 9, of which 7 were waited for; matrix products, arithmetic and copies ran while one was open for 0% of the time, Pallas kernels for 7%

profile of v4, /device:TPU:0, one launch (start us, length us, event | category | flops | bytes accessed | tf_op | source)
XLA Modules:
  0.0 24.9 jit_solution(14376798740355216446)
XLA Ops:
  0.0 0.0 copy-start
  0.0 1.2 %edges.1 = (bf16[64,512]{1,0:T(8,128)(2,1)S(1)}, s32[3,8]{1,0:T(4,128)S(4)}, bf16[64,2048]{1,0:T(8,128)(2,1)S(1)}, s32[16,128]{1,0:T(8,128)S(1)}) custom-call(s32[1]{0:T(128)} %bitcast.place_ref, s32[3,8]{1,0:T(4,128)} %bitcast.7, bf16[64,2048]{1,0:T(8,128)(2,1)} %bitcast.5, s32[16,128]{1,0:T(8,128)} %bitcast.6), custom_call_target="tpu_custom_call" | custom-call | flops 1572864000 | bytes 62914560 | tf_op jit(solution)/shard_map/edges/pallas_call | solution.py:252
  1.2 3.0 %collective-permute-start.2 = (bf16[64,512]{1,0:T(8,128)(2,1)S(1)}, bf16[64,512]{1,0:T(8,128)(2,1)S(1)}, u32[]{:S(2)}, u32[]{:S(2)}) collective-permute-start(bf16[64,512]{1,0:T(8,128)(2,1)S(1)} %get-tuple-element.18), channel_id=1, source_target_pairs={{3,4},{4,3},{5,6},{6,5},{7,8},{8,7},{9,10},{10,9},{11,12},{12,11},... | collective-permute-start | bytes 196616 | tf_op jit(solution)/shard_map/ppermute | solution.py:267
  4.2 0.0 collective-permute-start.1
  4.2 0.0 copy-done
  4.2 0.0 copy-start.1
  4.2 1.3 %own.1 = (bf16[64,512]{1,0:T(8,128)(2,1)S(1)}, f32[64,2048]{1,0:T(8,128)S(1)}, f32[64,64]{1,0:T(8,128)S(1)}) custom-call(s32[1]{0:T(128)} %bitcast.place_ref, s32[3,8]{1,0:T(4,128)S(4)} %get-tuple-element.14.columns_ref, bf16[64,2048]{1,0:T(8,128)(2,1)S(1)} %get-tuple-element.16.basis_ref, s32[16,128]{1,0:T(8,128)S(1)} %get-tuple-element.15.degrees_ref, ...), custom_call_target="tpu_custom_call" | custom-call | flops 201326592 | tf_op jit(solution)/shard_map/own/pallas_call | solution.py:269
  5.5 0.2 collective-permute-start
  5.7 0.4 %collective-permute-done.2.most_ref = bf16[64,512]{1,0:T(8,128)(2,1)S(1)} collective-permute-done((bf16[64,512]{1,0:T(8,128)(2,1)S(1)}, bf16[64,512]{1,0:T(8,128)(2,1)S(1)}, u32[]{:S(2)}, u32[]{:S(2)}) %collective-permute-start.2) | collective-permute-done | bytes 65568 | tf_op jit(solution)/shard_map/ppermute | solution.py:267
  6.1 1.9 %collective-permute-done.1.rest_ref = bf16[64,512]{1,0:T(8,128)(2,1)S(1)} collective-permute-done((bf16[64,512]{1,0:T(8,128)(2,1)S(1)}, bf16[64,512]{1,0:T(8,128)(2,1)S(1)}, u32[]{:S(2)}, u32[]{:S(2)}) %collective-permute-start.1) | collective-permute-done | bytes 65568 | tf_op jit(solution)/shard_map/ppermute | solution.py:267
  8.0 0.0 collective-permute-done.near_ref
  8.0 0.8 %halo.1 = (f32[64,1024]{1,0:T(8,128)S(1)}, f32[32,128]{1,0:T(8,128)S(1)}) custom-call(s32[1]{0:T(128)} %bitcast.place_ref, s32[3,8]{1,0:T(4,128)S(4)} %get-tuple-element.14.columns_ref, s32[16,128]{1,0:T(8,128)S(1)} %get-tuple-element.15.degrees_ref, bf16[64,512]{1,0:T(8,128)(2,1)S(1)} %collective-permute-done.near_ref, ...), custom_call_target="tpu_custom_call" | custom-call | tf_op jit(solution)/shard_map/halo/pallas_call | solution.py:287
  8.8 0.0 collective-permute-start.3
  8.8 1.2 %collective-permute-done.3 = f32[32,128]{1,0:T(8,128)S(1)} collective-permute-done((f32[32,128]{1,0:T(8,128)S(1)}, f32[32,128]{1,0:T(8,128)S(1)}, u32[]{:S(2)}, u32[]{:S(2)}) %collective-permute-start.3) | collective-permute-done | bytes 16416 | tf_op jit(solution)/shard_map/ppermute | solution.py:220
  10.0 2.5 %collective-permute-start.4 = (f32[32,128]{1,0:T(8,128)S(1)}, f32[32,128]{1,0:T(8,128)S(1)}, u32[]{:S(2)}, u32[]{:S(2)}) collective-permute-start(f32[32,128]{1,0:T(8,128)S(1)} %add.13), channel_id=1, source_target_pairs={{0,17},{1,16},{2,19},{3,18},{4,21},{5,20},{6,23},{7,22},{8,25},{9,... | collective-permute-start | bytes 49160 | tf_op jit(solution)/shard_map/ppermute | solution.py:220
  12.5 1.6 %collective-permute-done.4 = f32[32,128]{1,0:T(8,128)S(1)} collective-permute-done((f32[32,128]{1,0:T(8,128)S(1)}, f32[32,128]{1,0:T(8,128)S(1)}, u32[]{:S(2)}, u32[]{:S(2)}) %collective-permute-start.4) | collective-permute-done | bytes 16416 | tf_op jit(solution)/shard_map/ppermute | solution.py:220
  14.1 1.5 %collective-permute-start.5 = (f32[32,128]{1,0:T(8,128)S(1)}, f32[32,128]{1,0:T(8,128)S(1)}, u32[]{:S(2)}, u32[]{:S(2)}) collective-permute-start(f32[32,128]{1,0:T(8,128)S(1)} %add.14), channel_id=1, source_target_pairs={{0,9},{1,8},{2,11},{3,10},{4,13},{5,12},{6,15},{7,14},{8,1},{9,0},... | collective-permute-start | bytes 49160 | tf_op jit(solution)/shard_map/ppermute | solution.py:220
  15.6 1.7 %collective-permute-done.5 = f32[32,128]{1,0:T(8,128)S(1)} collective-permute-done((f32[32,128]{1,0:T(8,128)S(1)}, f32[32,128]{1,0:T(8,128)S(1)}, u32[]{:S(2)}, u32[]{:S(2)}) %collective-permute-start.5) | collective-permute-done | bytes 16416 | tf_op jit(solution)/shard_map/ppermute | solution.py:220
  17.2 2.1 %collective-permute-start.8 = (f32[32,128]{1,0:T(8,128)S(1)}, f32[32,128]{1,0:T(8,128)S(1)}, u32[]{:S(2)}, u32[]{:S(2)}) collective-permute-start(f32[32,128]{1,0:T(8,128)S(1)} %add.15.refs_0_), channel_id=1, source_target_pairs={{0,6},{1,7},{2,4},{3,5},{4,2},{5,3},{6,0},{7,1},{8,14},{9,15},{10,... | collective-permute-start | bytes 49160 | tf_op jit(solution)/shard_map/ppermute | solution.py:220
  19.3 0.0 collective-permute-start.7
  19.3 1.1 %collective-permute-start.6 = (f32[32,128]{1,0:T(8,128)S(1)}, f32[32,128]{1,0:T(8,128)S(1)}, u32[]{:S(2)}, u32[]{:S(2)}) collective-permute-start(f32[32,128]{1,0:T(8,128)S(1)} %add.15.refs_0_), channel_id=1, source_target_pairs={{0,3},{1,2},{2,1},{3,0},{4,7},{5,6},{6,5},{7,4},{8,11},{9,10},{10,... | collective-permute-start | bytes 49160 | tf_op jit(solution)/shard_map/ppermute | solution.py:220
  20.5 0.0 copy-done.1
  20.5 0.4 %reorder.1.refs_4_ = bf16[192,2048]{1,0:T(8,128)(2,1)S(1)} custom-call(f32[64,2048]{1,0:T(8,128)S(1)} %get-tuple-element.19.partial_ref.inner_ref, f32[64,1024]{1,0:T(8,128)S(1)} %get-tuple-element.22.outer_ref, s32[8,256]{1,0:T(8,128)S(1)} %copy-done.1), custom_call_target="tpu_custom_call" | custom-call | flops 134217728 | tf_op jit(solution)/shard_map/reorder/pallas_call | solution.py:297
  20.8 1.1 %collective-permute-done.8.refs_3_ = f32[32,128]{1,0:T(8,128)S(1)} collective-permute-done((f32[32,128]{1,0:T(8,128)S(1)}, f32[32,128]{1,0:T(8,128)S(1)}, u32[]{:S(2)}, u32[]{:S(2)}) %collective-permute-start.8) | collective-permute-done | bytes 16416 | tf_op jit(solution)/shard_map/ppermute | solution.py:220
  21.9 0.6 %collective-permute-done.7.refs_2_ = f32[32,128]{1,0:T(8,128)S(1)} collective-permute-done((f32[32,128]{1,0:T(8,128)S(1)}, f32[32,128]{1,0:T(8,128)S(1)}, u32[]{:S(2)}, u32[]{:S(2)}) %collective-permute-start.7) | collective-permute-done | bytes 16416 | tf_op jit(solution)/shard_map/ppermute | solution.py:220
  22.5 0.0 collective-permute-done.6.refs_1_
  22.5 2.4 %targets.1 = f32[64,2048]{1,0:T(8,128)} custom-call(f32[32,128]{1,0:T(8,128)S(1)} %add.15.refs_0_, f32[32,128]{1,0:T(8,128)S(1)} %collective-permute-done.6.refs_1_, f32[32,128]{1,0:T(8,128)S(1)} %collective-permute-done.7.refs_2_, f32[32,128]{1,0:T(8,128)S(1)} %collective-permute-done.8.refs_3_, bf16[192,2048]{1,0:T(8,128)(2,1)S(1)} %reorder.1.refs_4_), custom_call_target="tpu_custom_call" | custom-call | tf_op jit(solution)/shard_map/targets/pallas_call | solution.py:308
  (3 shorter events, 0.0 us)
Async XLA Ops:
  0.0 4.2 %copy-start = (bf16[8,3,256,256]{3,2,1,0:T(8,128)(2,1)S(1)}, bf16[8,3,256,256]{3,2,1,0:T(8,128)(2,1)}, u32[]{:S(2)}) copy-start(bf16[8,3,256,256]{3,2,1,0:T(8,128)(2,1)} %affinity_ref.3) | copy-start | bytes 9437188
  1.2 5.0 %collective-permute-start.2 = (bf16[64,512]{1,0:T(8,128)(2,1)S(1)}, bf16[64,512]{1,0:T(8,128)(2,1)S(1)}, u32[]{:S(2)}, u32[]{:S(2)}) collective-permute-start(bf16[64,512]{1,0:T(8,128)(2,1)S(1)} %get-tuple-element.18), channel_id=1, source_target_pairs={{3,4},{4,3},{5,6},{6,5},{7,8},{8,7},{9,10},{10,9},{11,12},{12,11},... | collective-permute-start | bytes 196616 | tf_op jit(solution)/shard_map/ppermute | solution.py:267
  4.2 3.9 %collective-permute-start.1 = (bf16[64,512]{1,0:T(8,128)(2,1)S(1)}, bf16[64,512]{1,0:T(8,128)(2,1)S(1)}, u32[]{:S(2)}, u32[]{:S(2)}) collective-permute-start(bf16[64,512]{1,0:T(8,128)(2,1)S(1)} %get-tuple-element.18), channel_id=1, source_target_pairs={{4,5},{5,4},{6,7},{7,6},{8,9},{9,8},{10,11},{11,10},{12,13},{13,12... | collective-permute-start | bytes 196616 | tf_op jit(solution)/shard_map/ppermute | solution.py:267
  4.2 16.3 %copy-start.1 = (s32[8,256]{1,0:T(8,128)S(1)}, s32[8,256]{1,0:T(8,128)}, u32[]{:S(2)}) copy-start(s32[8,256]{1,0:T(8,128)} %reorder_ref.1) | copy-start | bytes 24580
  5.5 2.5 %collective-permute-start = (bf16[64,512]{1,0:T(8,128)(2,1)S(1)}, bf16[64,512]{1,0:T(8,128)(2,1)S(1)}, u32[]{:S(2)}, u32[]{:S(2)}) collective-permute-start(bf16[64,512]{1,0:T(8,128)(2,1)S(1)} %get-tuple-element.17), channel_id=1, source_target_pairs={{0,1},{1,0},{2,3},{3,2},{4,5},{5,4},{6,7},{7,6},{8,9},{9,8},{10,11... | collective-permute-start | bytes 196616 | tf_op jit(solution)/shard_map/ppermute | solution.py:285
  8.8 1.2 %collective-permute-start.3 = (f32[32,128]{1,0:T(8,128)S(1)}, f32[32,128]{1,0:T(8,128)S(1)}, u32[]{:S(2)}, u32[]{:S(2)}) collective-permute-start(f32[32,128]{1,0:T(8,128)S(1)} %get-tuple-element.21), channel_id=1, source_target_pairs={{0,1},{1,0},{2,3},{3,2},{4,5},{5,4},{6,7},{7,6},{8,9},{9,8},{10,11... | collective-permute-start | bytes 49160 | tf_op jit(solution)/shard_map/ppermute | solution.py:220
  10.0 4.1 %collective-permute-start.4 = (f32[32,128]{1,0:T(8,128)S(1)}, f32[32,128]{1,0:T(8,128)S(1)}, u32[]{:S(2)}, u32[]{:S(2)}) collective-permute-start(f32[32,128]{1,0:T(8,128)S(1)} %add.13), channel_id=1, source_target_pairs={{0,17},{1,16},{2,19},{3,18},{4,21},{5,20},{6,23},{7,22},{8,25},{9,... | collective-permute-start | bytes 49160 | tf_op jit(solution)/shard_map/ppermute | solution.py:220
  14.1 3.2 %collective-permute-start.5 = (f32[32,128]{1,0:T(8,128)S(1)}, f32[32,128]{1,0:T(8,128)S(1)}, u32[]{:S(2)}, u32[]{:S(2)}) collective-permute-start(f32[32,128]{1,0:T(8,128)S(1)} %add.14), channel_id=1, source_target_pairs={{0,9},{1,8},{2,11},{3,10},{4,13},{5,12},{6,15},{7,14},{8,1},{9,0},... | collective-permute-start | bytes 49160 | tf_op jit(solution)/shard_map/ppermute | solution.py:220
  17.2 4.6 %collective-permute-start.8 = (f32[32,128]{1,0:T(8,128)S(1)}, f32[32,128]{1,0:T(8,128)S(1)}, u32[]{:S(2)}, u32[]{:S(2)}) collective-permute-start(f32[32,128]{1,0:T(8,128)S(1)} %add.15.refs_0_), channel_id=1, source_target_pairs={{0,6},{1,7},{2,4},{3,5},{4,2},{5,3},{6,0},{7,1},{8,14},{9,15},{10,... | collective-permute-start | bytes 49160 | tf_op jit(solution)/shard_map/ppermute | solution.py:220
  19.3 3.2 %collective-permute-start.7 = (f32[32,128]{1,0:T(8,128)S(1)}, f32[32,128]{1,0:T(8,128)S(1)}, u32[]{:S(2)}, u32[]{:S(2)}) collective-permute-start(f32[32,128]{1,0:T(8,128)S(1)} %add.15.refs_0_), channel_id=1, source_target_pairs={{0,5},{1,4},{2,7},{3,6},{4,1},{5,0},{6,3},{7,2},{8,13},{9,12},{10,... | collective-permute-start | bytes 49160 | tf_op jit(solution)/shard_map/ppermute | solution.py:220
  19.3 3.2 %collective-permute-start.6 = (f32[32,128]{1,0:T(8,128)S(1)}, f32[32,128]{1,0:T(8,128)S(1)}, u32[]{:S(2)}, u32[]{:S(2)}) collective-permute-start(f32[32,128]{1,0:T(8,128)S(1)} %add.15.refs_0_), channel_id=1, source_target_pairs={{0,3},{1,2},{2,1},{3,0},{4,7},{5,6},{6,5},{7,4},{8,11},{9,10},{10,... | collective-permute-start | bytes 49160 | tf_op jit(solution)/shard_map/ppermute | solution.py:220

commit v5 on v4

--- a/solution.py
+++ b/solution.py
@@ -32,8 +32,15 @@
     )
 
 
-def gram_of(image):
-    return rank_dot(image, image, (1, 1), lax.Precision.HIGHEST)
+def split(x):
+    high = x.astype(jnp.bfloat16)
+    return jnp.concatenate([high, (x - high.astype(jnp.float32)).astype(jnp.bfloat16)], axis=0)
+
+
+def gram_halves(terms):
+    rank = terms.shape[0] // 2
+    whole = rank_dot(terms, terms, (1, 1))
+    return whole[:rank] + whole[rank:]
 
 
 def inverse_root(degrees_ref, piece):
@@ -45,29 +52,31 @@
     return jnp.concatenate([inverse_root(degrees_ref, b * pieces + c) for c in range(pieces)], axis=1)
 
 
-def scaled_piece(basis_ref, degrees_ref, piece):
-    columns = slice(piece * LANES, (piece + 1) * LANES)
-    if not isinstance(piece, int):
-        columns = pl.ds(pl.multiple_of(piece * LANES, LANES), LANES)
-    return (inverse_root(degrees_ref, piece) * basis_ref[:, columns].astype(jnp.float32)).astype(jnp.bfloat16)
+def scaled(degrees_ref, piece, basis):
+    return (inverse_root(degrees_ref, piece) * basis.astype(jnp.float32)).astype(jnp.bfloat16)
 
 
 def edges_kernel(
-    width, place_ref, columns_hbm, basis_hbm, degrees_hbm, far_ref, columns_ref, basis_ref, degrees_ref, sems
+    width, place_ref, columns_hbm, basis_hbm, degrees_hbm, far_ref, columns_ref, basis_ref, degrees_ref, edge_ref, sems
 ):
-    pieces, last = width // LANES, (basis_ref.shape[1] - width) // LANES
+    odd = place_ref[0] % 2
+    last = basis_hbm.shape[1] - width
+    edge_hbm = basis_hbm.at[:, pl.ds(pl.multiple_of(odd * last, LANES), width)]
     copies = [
-        pltpu.make_async_copy(degrees_hbm, degrees_ref, sems.at[0]),
-        pltpu.make_async_copy(basis_hbm, basis_ref, sems.at[1]),
-        pltpu.make_async_copy(columns_hbm, columns_ref, sems.at[2]),
+        pltpu.make_async_copy(edge_hbm, edge_ref, sems.at[0]),
+        pltpu.make_async_copy(degrees_hbm, degrees_ref, sems.at[1]),
+        pltpu.make_async_copy(basis_hbm, basis_ref, sems.at[2]),
+        pltpu.make_async_copy(columns_hbm, columns_ref, sems.at[3]),
     ]
     for copy in copies:
         copy.start()
-    odd = place_ref[0] % 2
-    for copy in copies:
+    for copy in copies[:2]:
         copy.wait()
-    for i in range(pieces):
-        far_ref[:, i * LANES:(i + 1) * LANES] = scaled_piece(basis_ref, degrees_ref, odd * last + i)
+    for i in range(width // LANES):
+        columns = slice(i * LANES, (i + 1) * LANES)
+        far_ref[:, columns] = scaled(degrees_ref, odd * (last // LANES) + i, edge_ref[:, columns])
+    for copy in copies[2:]:
+        copy.wait()
 
 
 def own_kernel(
@@ -80,7 +89,8 @@
         extended[count + REACH + b] = jnp.zeros_like(extended[b])
     for piece in range(count * pieces):
         b, c = divmod(piece, pieces)
-        extended[REACH + b, :, c * LANES:(c + 1) * LANES] = scaled_piece(basis_ref, degrees_ref, piece)
+        basis = basis_ref[:, piece * LANES:(piece + 1) * LANES]
+        extended[REACH + b, :, c * LANES:(c + 1) * LANES] = scaled(degrees_ref, piece, basis)
     odd = place_ref[0] % 2
     for b in range(REACH):
         near_ref[:, b * block:(b + 1) * block] = extended[REACH + (1 - odd) * (count - REACH) + b]
@@ -92,10 +102,10 @@
             total += rank_dot(extended[columns_ref[slot, b] - first], affinity_ref[b, slot], (1, 1))
         if b not in edges:
             total *= block_root(degrees_ref, b, block)
-            inner.append(total)
+            inner.append(split(total))
         partial_ref[:, b * block:(b + 1) * block] = total
     if inner:
-        gram_ref[...] = gram_of(jnp.concatenate(inner, axis=1))
+        gram_ref[...] = gram_halves(jnp.concatenate(inner, axis=1))
     else:
         gram_ref[...] = jnp.zeros_like(gram_ref)
 
@@ -119,24 +129,25 @@
             index = columns_ref[slot, b] - first
             index = jnp.where(index < REACH, index, jnp.where(index < REACH + count, 2 * REACH, index - count))
             total += rank_dot(halo[index], affinity_ref[b, slot], (1, 1))
-        images.append(total * block_root(degrees_ref, b, block))
+        images.append(split(total * block_root(degrees_ref, b, block)))
         image_ref[:, at * block:(at + 1) * block] = images[-1]
-    gram = own_gram_ref[...] + gram_of(jnp.concatenate(images, axis=1))
-    half = gram.shape[0] // 2
-    gram_ref[...] = jnp.concatenate([gram[:half], gram[half:]], axis=1)
+    halves = own_gram_ref[...] + gram_halves(jnp.concatenate(images, axis=1))
+    rank = halves.shape[0]
+    halves = halves + pltpu.roll(halves, rank, 1)
+    lane = lax.broadcasted_iota(jnp.int32, gram_ref.shape, 1)
+    gram_ref[...] = jnp.where(lane < rank, halves[:rank // 2], halves[rank // 2:])
 
 
 def reorder_kernel(count, block, edges, inner_ref, outer_ref, reorder_ref, placed_ref):
     source = lax.broadcasted_iota(jnp.int32, (block, block), 0)
     for b in range(count):
         at = edges.index(b) if b in edges else b
-        image = (outer_ref if b in edges else inner_ref)[:, at * block:(at + 1) * block]
-        high = image.astype(jnp.bfloat16)
-        low = (image - high.astype(jnp.float32)).astype(jnp.bfloat16)
+        columns = slice(at * block, (at + 1) * block)
+        terms = outer_ref[:, columns] if b in edges else split(inner_ref[:, columns])
         chosen = jnp.where(source == reorder_ref[b:b + 1, :], 1.0, 0.0).astype(jnp.bfloat16)
-        moved = rank_dot(jnp.concatenate([high, low], axis=0), chosen, (1, 0))
+        moved = rank_dot(terms, chosen, (1, 0))
         moved = moved.astype(jnp.bfloat16)
-        rank = image.shape[0]
+        rank = terms.shape[0] // 2
         placed_ref[:2 * rank, b * block:(b + 1) * block] = moved
         placed_ref[2 * rank:, b * block:(b + 1) * block] = moved[:rank]
 
@@ -184,7 +195,7 @@
                 state[t] = state[t] - column * row
         for t in range(top, top + per):
             state[t] = state[t] * lax.rsqrt(diagonal[t])
-    return jnp.concatenate(state, axis=0)[:, rank:]
+    return jnp.concatenate(state, axis=0)
 
 
 def targets_kernel(total_items, parts, *refs):
@@ -192,10 +203,13 @@
     gram = refs[0][...]
     for part in refs[1:parts]:
         gram = gram + part[...]
-    inverse = inverse_factor(gram) * math.sqrt(total_items)
-    high = inverse.astype(jnp.bfloat16)
-    low = (inverse - high.astype(jnp.float32)).astype(jnp.bfloat16)
-    left = jnp.concatenate([high, high, low], axis=1)
+    right = inverse_factor(gram) * math.sqrt(total_items)
+    rank = right.shape[0]
+    left = pltpu.roll(right, rank, 1)
+    lane = lax.broadcasted_iota(jnp.int32, right.shape, 1)
+    high = jnp.where(lane < rank, left, right).astype(jnp.bfloat16)
+    low = (left - left.astype(jnp.bfloat16).astype(jnp.float32)).astype(jnp.bfloat16)
+    left = jnp.concatenate([high, low[:, :rank]], axis=1)
     chunk = targets_ref.shape[1] // CHUNKS
     copies = []
     for c in range(CHUNKS):
@@ -259,7 +273,7 @@
         ),
         in_specs=[SMEM, HBM, HBM, HBM],
         out_specs=(VMEM, SMEM, VMEM, VMEM),
-        scratch_shapes=[pltpu.SemaphoreType.DMA((3,))],
+        scratch_shapes=[pltpu.VMEM((rank, width), jnp.bfloat16), pltpu.SemaphoreType.DMA((4,))],
         compiler_params=PARAMS,
         cost_estimate=pl.CostEstimate(flops=1000 * affinity.size, bytes_accessed=40 * affinity.size, transcendentals=0),
         name="edges",
@@ -271,7 +285,7 @@
         out_shape=(
             pltpu.VMEM((rank, width), jnp.bfloat16),
             pltpu.VMEM((rank, items), jnp.float32),
-            pltpu.VMEM((rank, rank), jnp.float32),
+            pltpu.VMEM((rank, 2 * rank), jnp.float32),
         ),
         in_specs=[SMEM, SMEM] + [VMEM] * 3,
         out_specs=(VMEM,) * 3,
@@ -286,7 +300,7 @@
 
     outer, gram = pl.pallas_call(
         functools.partial(halo_kernel, count, block, edges, (2, mesh_size - 3)),
-        out_shape=(pltpu.VMEM((rank, len(edges) * block), jnp.float32), folded),
+        out_shape=(pltpu.VMEM((2 * rank, len(edges) * block), jnp.bfloat16), folded),
         in_specs=[SMEM, SMEM] + [VMEM] * 7,
         out_specs=(VMEM, VMEM),
         scratch_shapes=[pltpu.VMEM((2 * REACH + 1, rank, block), jnp.bfloat16)],

time: 25 us -> 25 us (level)
  Pallas kernels: 5.96 us -> 5.66 us
  transfers between devices with their start and end apart: 9 -> 9, of which waited for: 7 -> 7; matrix products, arithmetic and copies ran while one was open for 0% -> 0% of each run, Pallas kernels for 7% -> 6%
where the time goes in v5:
time: 25 us; the launch traced here: 24.8 us
  starting transfers between devices  10.5 us (42%)
  waiting for transfers between devices  8.61 us (34%)
  Pallas kernels  5.66 us (23%)
    ppermute x6, starting transfers between devices, gram_parts(): lax.ppermute(gram, AXES, [(i, i ^ mask) for i in range(mesh_size)])  7.27 us
    ppermute x6, waiting for transfers between devices, gram_parts(): lax.ppermute(gram, AXES, [(i, i ^ mask) for i in range(mesh_size)])  6.09 us
    ppermute x2, starting transfers between devices, body(): lax.ppermute(far, AXES, pairs)  2.99 us
    ppermute x2, waiting for transfers between devices, body(): lax.ppermute(far, AXES, pairs)  2.51 us
    pallas_call x1, Pallas kernels, body(): pl.pallas_call(functools.partial(targets_kernel, items * mesh_size, len(p...  2.33 us
    pallas_call x1, Pallas kernels, body(): pl.pallas_call(functools.partial(edges_kernel, width), out_shape=(pltpu.V...  1.19 us
    pallas_call x1, Pallas kernels, body(): pl.pallas_call(functools.partial(own_kernel, count, block, edges), out_sh...  1.1 us
    pallas_call x1, Pallas kernels, body(): pl.pallas_call(functools.partial(halo_kernel, count, block, edges, (2, me...  0.69 us
  transfers between devices with their start and end apart: 9, of which 7 were waited for; matrix products, arithmetic and copies ran while one was open for 0% of the time, Pallas kernels for 6%

profile of v5, /device:TPU:0, one launch (start us, length us, event | category | flops | bytes accessed | tf_op | source)
XLA Modules:
  0.0 24.8 jit_solution(4773855458134850599)
XLA Ops:
  0.0 0.0 copy-start
  0.0 1.2 %edges.1 = (bf16[64,512]{1,0:T(8,128)(2,1)S(1)}, s32[3,8]{1,0:T(4,128)S(4)}, bf16[64,2048]{1,0:T(8,128)(2,1)S(1)}, s32[16,128]{1,0:T(8,128)S(1)}) custom-call(s32[1]{0:T(128)} %bitcast.place_ref, s32[3,8]{1,0:T(4,128)} %bitcast.7, bf16[64,2048]{1,0:T(8,128)(2,1)} %bitcast.5, s32[16,128]{1,0:T(8,128)} %bitcast.6), custom_call_target="tpu_custom_call" | custom-call | flops 1572864000 | bytes 62914560 | tf_op jit(solution)/shard_map/edges/pallas_call | solution.py:266
  1.2 3.0 %collective-permute-start.2 = (bf16[64,512]{1,0:T(8,128)(2,1)S(1)}, bf16[64,512]{1,0:T(8,128)(2,1)S(1)}, u32[]{:S(2)}, u32[]{:S(2)}) collective-permute-start(bf16[64,512]{1,0:T(8,128)(2,1)S(1)} %get-tuple-element.18), channel_id=1, source_target_pairs={{3,4},{4,3},{5,6},{6,5},{7,8},{8,7},{9,10},{10,9},{11,12},{12,11},... | collective-permute-start | bytes 196616 | tf_op jit(solution)/shard_map/ppermute | solution.py:281
  4.2 0.0 collective-permute-start.1
  4.2 0.0 copy-done
  4.2 0.0 copy-start.1
  4.2 1.1 %own.1 = (bf16[64,512]{1,0:T(8,128)(2,1)S(1)}, f32[64,2048]{1,0:T(8,128)S(1)}, f32[64,128]{1,0:T(8,128)S(1)}) custom-call(s32[1]{0:T(128)} %bitcast.place_ref, s32[3,8]{1,0:T(4,128)S(4)} %get-tuple-element.14.columns_ref, bf16[64,2048]{1,0:T(8,128)(2,1)S(1)} %get-tuple-element.16.basis_ref, s32[16,128]{1,0:T(8,128)S(1)} %get-tuple-element.15.degrees_ref, ...), custom_call_target="tpu_custom_call" | custom-call | flops 201326592 | tf_op jit(solution)/shard_map/own/pallas_call | solution.py:283
  5.3 0.2 collective-permute-start
  5.5 0.6 %collective-permute-done.2.most_ref = bf16[64,512]{1,0:T(8,128)(2,1)S(1)} collective-permute-done((bf16[64,512]{1,0:T(8,128)(2,1)S(1)}, bf16[64,512]{1,0:T(8,128)(2,1)S(1)}, u32[]{:S(2)}, u32[]{:S(2)}) %collective-permute-start.2) | collective-permute-done | bytes 65568 | tf_op jit(solution)/shard_map/ppermute | solution.py:281
  6.2 1.9 %collective-permute-done.1.rest_ref = bf16[64,512]{1,0:T(8,128)(2,1)S(1)} collective-permute-done((bf16[64,512]{1,0:T(8,128)(2,1)S(1)}, bf16[64,512]{1,0:T(8,128)(2,1)S(1)}, u32[]{:S(2)}, u32[]{:S(2)}) %collective-permute-start.1) | collective-permute-done | bytes 65568 | tf_op jit(solution)/shard_map/ppermute | solution.py:281
  8.0 0.0 collective-permute-done.near_ref
  8.1 0.7 %halo.1 = (bf16[128,1024]{1,0:T(8,128)(2,1)S(1)}, f32[32,128]{1,0:T(8,128)S(1)}) custom-call(s32[1]{0:T(128)} %bitcast.place_ref, s32[3,8]{1,0:T(4,128)S(4)} %get-tuple-element.14.columns_ref, s32[16,128]{1,0:T(8,128)S(1)} %get-tuple-element.15.degrees_ref, bf16[64,512]{1,0:T(8,128)(2,1)S(1)} %collective-permute-done.near_ref, ...), custom_call_target="tpu_custom_call" | custom-call | tf_op jit(solution)/shard_map/halo/pallas_call | solution.py:301
  8.8 0.1 collective-permute-start.3
  8.8 1.2 %collective-permute-done.3 = f32[32,128]{1,0:T(8,128)S(1)} collective-permute-done((f32[32,128]{1,0:T(8,128)S(1)}, f32[32,128]{1,0:T(8,128)S(1)}, u32[]{:S(2)}, u32[]{:S(2)}) %collective-permute-start.3) | collective-permute-done | bytes 16416 | tf_op jit(solution)/shard_map/ppermute | solution.py:234
  10.0 2.5 %collective-permute-start.4 = (f32[32,128]{1,0:T(8,128)S(1)}, f32[32,128]{1,0:T(8,128)S(1)}, u32[]{:S(2)}, u32[]{:S(2)}) collective-permute-start(f32[32,128]{1,0:T(8,128)S(1)} %add.13), channel_id=1, source_target_pairs={{0,17},{1,16},{2,19},{3,18},{4,21},{5,20},{6,23},{7,22},{8,25},{9,... | collective-permute-start | bytes 49160 | tf_op jit(solution)/shard_map/ppermute | solution.py:234
  12.5 1.6 %collective-permute-done.4 = f32[32,128]{1,0:T(8,128)S(1)} collective-permute-done((f32[32,128]{1,0:T(8,128)S(1)}, f32[32,128]{1,0:T(8,128)S(1)}, u32[]{:S(2)}, u32[]{:S(2)}) %collective-permute-start.4) | collective-permute-done | bytes 16416 | tf_op jit(solution)/shard_map/ppermute | solution.py:234
  14.1 1.5 %collective-permute-start.5 = (f32[32,128]{1,0:T(8,128)S(1)}, f32[32,128]{1,0:T(8,128)S(1)}, u32[]{:S(2)}, u32[]{:S(2)}) collective-permute-start(f32[32,128]{1,0:T(8,128)S(1)} %add.14), channel_id=1, source_target_pairs={{0,9},{1,8},{2,11},{3,10},{4,13},{5,12},{6,15},{7,14},{8,1},{9,0},... | collective-permute-start | bytes 49160 | tf_op jit(solution)/shard_map/ppermute | solution.py:234
  15.6 1.7 %collective-permute-done.5 = f32[32,128]{1,0:T(8,128)S(1)} collective-permute-done((f32[32,128]{1,0:T(8,128)S(1)}, f32[32,128]{1,0:T(8,128)S(1)}, u32[]{:S(2)}, u32[]{:S(2)}) %collective-permute-start.5) | collective-permute-done | bytes 16416 | tf_op jit(solution)/shard_map/ppermute | solution.py:234
  17.2 2.1 %collective-permute-start.8 = (f32[32,128]{1,0:T(8,128)S(1)}, f32[32,128]{1,0:T(8,128)S(1)}, u32[]{:S(2)}, u32[]{:S(2)}) collective-permute-start(f32[32,128]{1,0:T(8,128)S(1)} %add.15.refs_0_), channel_id=1, source_target_pairs={{0,6},{1,7},{2,4},{3,5},{4,2},{5,3},{6,0},{7,1},{8,14},{9,15},{10,... | collective-permute-start | bytes 49160 | tf_op jit(solution)/shard_map/ppermute | solution.py:234
  19.3 0.0 collective-permute-start.7
  19.3 1.1 %collective-permute-start.6 = (f32[32,128]{1,0:T(8,128)S(1)}, f32[32,128]{1,0:T(8,128)S(1)}, u32[]{:S(2)}, u32[]{:S(2)}) collective-permute-start(f32[32,128]{1,0:T(8,128)S(1)} %add.15.refs_0_), channel_id=1, source_target_pairs={{0,3},{1,2},{2,1},{3,0},{4,7},{5,6},{6,5},{7,4},{8,11},{9,10},{10,... | collective-permute-start | bytes 49160 | tf_op jit(solution)/shard_map/ppermute | solution.py:234
  20.5 0.0 copy-done.1
  20.5 0.4 %reorder.1.refs_4_ = bf16[192,2048]{1,0:T(8,128)(2,1)S(1)} custom-call(f32[64,2048]{1,0:T(8,128)S(1)} %get-tuple-element.19.partial_ref.inner_ref, bf16[128,1024]{1,0:T(8,128)(2,1)S(1)} %get-tuple-element.22.outer_ref, s32[8,256]{1,0:T(8,128)S(1)} %copy-done.1), custom_call_target="tpu_custom_call" | custom-call | flops 134217728 | tf_op jit(solution)/shard_map/reorder/pallas_call | solution.py:311
  20.8 1.1 %collective-permute-done.8.refs_3_ = f32[32,128]{1,0:T(8,128)S(1)} collective-permute-done((f32[32,128]{1,0:T(8,128)S(1)}, f32[32,128]{1,0:T(8,128)S(1)}, u32[]{:S(2)}, u32[]{:S(2)}) %collective-permute-start.8) | collective-permute-done | bytes 16416 | tf_op jit(solution)/shard_map/ppermute | solution.py:234
  21.9 0.6 %collective-permute-done.7.refs_2_ = f32[32,128]{1,0:T(8,128)S(1)} collective-permute-done((f32[32,128]{1,0:T(8,128)S(1)}, f32[32,128]{1,0:T(8,128)S(1)}, u32[]{:S(2)}, u32[]{:S(2)}) %collective-permute-start.7) | collective-permute-done | bytes 16416 | tf_op jit(solution)/shard_map/ppermute | solution.py:234
  22.5 0.0 collective-permute-done.6.refs_1_
  22.5 2.3 %targets.1 = f32[64,2048]{1,0:T(8,128)} custom-call(f32[32,128]{1,0:T(8,128)S(1)} %add.15.refs_0_, f32[32,128]{1,0:T(8,128)S(1)} %collective-permute-done.6.refs_1_, f32[32,128]{1,0:T(8,128)S(1)} %collective-permute-done.7.refs_2_, f32[32,128]{1,0:T(8,128)S(1)} %collective-permute-done.8.refs_3_, bf16[192,2048]{1,0:T(8,128)(2,1)S(1)} %reorder.1.refs_4_), custom_call_target="tpu_custom_call" | custom-call | tf_op jit(solution)/shard_map/targets/pallas_call | solution.py:322
  (3 shorter events, 0.0 us)
Async XLA Ops:
  0.0 4.2 %copy-start = (bf16[8,3,256,256]{3,2,1,0:T(8,128)(2,1)S(1)}, bf16[8,3,256,256]{3,2,1,0:T(8,128)(2,1)}, u32[]{:S(2)}) copy-start(bf16[8,3,256,256]{3,2,1,0:T(8,128)(2,1)} %affinity_ref.3) | copy-start | bytes 9437188
  1.2 5.0 %collective-permute-start.2 = (bf16[64,512]{1,0:T(8,128)(2,1)S(1)}, bf16[64,512]{1,0:T(8,128)(2,1)S(1)}, u32[]{:S(2)}, u32[]{:S(2)}) collective-permute-start(bf16[64,512]{1,0:T(8,128)(2,1)S(1)} %get-tuple-element.18), channel_id=1, source_target_pairs={{3,4},{4,3},{5,6},{6,5},{7,8},{8,7},{9,10},{10,9},{11,12},{12,11},... | collective-permute-start | bytes 196616 | tf_op jit(solution)/shard_map/ppermute | solution.py:281
  4.2 3.9 %collective-permute-start.1 = (bf16[64,512]{1,0:T(8,128)(2,1)S(1)}, bf16[64,512]{1,0:T(8,128)(2,1)S(1)}, u32[]{:S(2)}, u32[]{:S(2)}) collective-permute-start(bf16[64,512]{1,0:T(8,128)(2,1)S(1)} %get-tuple-element.18), channel_id=1, source_target_pairs={{4,5},{5,4},{6,7},{7,6},{8,9},{9,8},{10,11},{11,10},{12,13},{13,12... | collective-permute-start | bytes 196616 | tf_op jit(solution)/shard_map/ppermute | solution.py:281
  4.2 16.3 %copy-start.1 = (s32[8,256]{1,0:T(8,128)S(1)}, s32[8,256]{1,0:T(8,128)}, u32[]{:S(2)}) copy-start(s32[8,256]{1,0:T(8,128)} %reorder_ref.1) | copy-start | bytes 24580
  5.3 2.8 %collective-permute-start = (bf16[64,512]{1,0:T(8,128)(2,1)S(1)}, bf16[64,512]{1,0:T(8,128)(2,1)S(1)}, u32[]{:S(2)}, u32[]{:S(2)}) collective-permute-start(bf16[64,512]{1,0:T(8,128)(2,1)S(1)} %get-tuple-element.17), channel_id=1, source_target_pairs={{0,1},{1,0},{2,3},{3,2},{4,5},{5,4},{6,7},{7,6},{8,9},{9,8},{10,11... | collective-permute-start | bytes 196616 | tf_op jit(solution)/shard_map/ppermute | solution.py:299
  8.8 1.2 %collective-permute-start.3 = (f32[32,128]{1,0:T(8,128)S(1)}, f32[32,128]{1,0:T(8,128)S(1)}, u32[]{:S(2)}, u32[]{:S(2)}) collective-permute-start(f32[32,128]{1,0:T(8,128)S(1)} %get-tuple-element.21), channel_id=1, source_target_pairs={{0,1},{1,0},{2,3},{3,2},{4,5},{5,4},{6,7},{7,6},{8,9},{9,8},{10,11... | collective-permute-start | bytes 49160 | tf_op jit(solution)/shard_map/ppermute | solution.py:234
  10.0 4.1 %collective-permute-start.4 = (f32[32,128]{1,0:T(8,128)S(1)}, f32[32,128]{1,0:T(8,128)S(1)}, u32[]{:S(2)}, u32[]{:S(2)}) collective-permute-start(f32[32,128]{1,0:T(8,128)S(1)} %add.13), channel_id=1, source_target_pairs={{0,17},{1,16},{2,19},{3,18},{4,21},{5,20},{6,23},{7,22},{8,25},{9,... | collective-permute-start | bytes 49160 | tf_op jit(solution)/shard_map/ppermute | solution.py:234
  14.1 3.2 %collective-permute-start.5 = (f32[32,128]{1,0:T(8,128)S(1)}, f32[32,128]{1,0:T(8,128)S(1)}, u32[]{:S(2)}, u32[]{:S(2)}) collective-permute-start(f32[32,128]{1,0:T(8,128)S(1)} %add.14), channel_id=1, source_target_pairs={{0,9},{1,8},{2,11},{3,10},{4,13},{5,12},{6,15},{7,14},{8,1},{9,0},... | collective-permute-start | bytes 49160 | tf_op jit(solution)/shard_map/ppermute | solution.py:234
  17.2 4.6 %collective-permute-start.8 = (f32[32,128]{1,0:T(8,128)S(1)}, f32[32,128]{1,0:T(8,128)S(1)}, u32[]{:S(2)}, u32[]{:S(2)}) collective-permute-start(f32[32,128]{1,0:T(8,128)S(1)} %add.15.refs_0_), channel_id=1, source_target_pairs={{0,6},{1,7},{2,4},{3,5},{4,2},{5,3},{6,0},{7,1},{8,14},{9,15},{10,... | collective-permute-start | bytes 49160 | tf_op jit(solution)/shard_map/ppermute | solution.py:234
  19.3 3.2 %collective-permute-start.7 = (f32[32,128]{1,0:T(8,128)S(1)}, f32[32,128]{1,0:T(8,128)S(1)}, u32[]{:S(2)}, u32[]{:S(2)}) collective-permute-start(f32[32,128]{1,0:T(8,128)S(1)} %add.15.refs_0_), channel_id=1, source_target_pairs={{0,5},{1,4},{2,7},{3,6},{4,1},{5,0},{6,3},{7,2},{8,13},{9,12},{10,... | collective-permute-start | bytes 49160 | tf_op jit(solution)/shard_map/ppermute | solution.py:234
  19.3 3.2 %collective-permute-start.6 = (f32[32,128]{1,0:T(8,128)S(1)}, f32[32,128]{1,0:T(8,128)S(1)}, u32[]{:S(2)}, u32[]{:S(2)}) collective-permute-start(f32[32,128]{1,0:T(8,128)S(1)} %add.15.refs_0_), channel_id=1, source_target_pairs={{0,3},{1,2},{2,1},{3,0},{4,7},{5,6},{6,5},{7,4},{8,11},{9,10},{10,... | collective-permute-start | bytes 49160 | tf_op jit(solution)/shard_map/ppermute | solution.py:234

commit v6 on v5

--- a/solution.py
+++ b/solution.py
@@ -79,10 +79,8 @@
         copy.wait()
 
 
-def own_kernel(
-    count, block, edges, place_ref, columns_ref, basis_ref, degrees_ref, affinity_ref, near_ref, partial_ref, gram_ref,
-    extended
-):
+def own_kernel(count, block, edges, place_ref, columns_ref, basis_ref, degrees_ref, affinity_ref, *refs):
+    near_refs, (partial_ref, gram_ref, extended) = refs[:REACH], refs[REACH:]
     pieces = block // LANES
     for b in range(REACH):
         extended[b] = jnp.zeros_like(extended[b])
@@ -93,7 +91,7 @@
         extended[REACH + b, :, c * LANES:(c + 1) * LANES] = scaled(degrees_ref, piece, basis)
     odd = place_ref[0] % 2
     for b in range(REACH):
-        near_ref[:, b * block:(b + 1) * block] = extended[REACH + (1 - odd) * (count - REACH) + b]
+        near_refs[b][...] = extended[REACH + (1 - odd) * (count - REACH) + b]
     first = place_ref[0] * count - REACH
     inner = []
     for b in range(count):
@@ -110,40 +108,63 @@
         gram_ref[...] = jnp.zeros_like(gram_ref)
 
 
-def halo_kernel(
-    count, block, edges, late, place_ref, columns_ref, degrees_ref, near_ref, rest_ref, most_ref, affinity_ref, partial_ref,
-    own_gram_ref, image_ref, gram_ref, halo
+def side_images(count, block, left, place_ref, columns_ref, degrees_ref, affinity_ref, partial_ref, halo):
+    start = jnp.where(left, 0, count - REACH)
+    first = place_ref[0] * count - REACH
+    pieces = block // LANES
+    images = []
+    for b in range(REACH):
+        row = start + b
+        total = partial_ref[:, pl.ds(pl.multiple_of(row * block, block), block)]
+        for slot in range(1, affinity_ref.shape[1]):
+            index = columns_ref[slot, row] - first
+            index = jnp.where(index < REACH, index, jnp.where(index < REACH + count, REACH, index - REACH - count))
+            total += rank_dot(halo[index], affinity_ref[row, slot], (1, 1))
+        root = [inverse_root(degrees_ref, row * pieces + c) for c in range(pieces)]
+        images.append(split(total * jnp.concatenate(root, axis=1)))
+    return jnp.concatenate(images, axis=1)
+
+
+def near_kernel(count, block, place_ref, columns_ref, degrees_ref, *refs):
+    near_refs, (affinity_ref, partial_ref, own_gram_ref, image_ref, gram_ref, halo) = refs[:REACH], refs[REACH:]
+    for b in range(REACH):
+        halo[b] = near_refs[b][...]
+    halo[REACH] = jnp.zeros_like(halo[0])
+    left = place_ref[0] % 2 == 1
+    image = side_images(count, block, left, place_ref, columns_ref, degrees_ref, affinity_ref, partial_ref, halo)
+    image_ref[...] = image
+    gram_ref[...] = own_gram_ref[...] + gram_halves(image)
+
+
+def far_kernel(
+    count, block, late, place_ref, columns_ref, degrees_ref, rest_ref, most_ref, affinity_ref, partial_ref, near_gram_ref,
+    image_ref, gram_ref, halo
 ):
-    odd = place_ref[0] % 2
     is_late = (place_ref[0] == late[0]) | (place_ref[0] == late[1])
     for b in range(REACH):
         columns = slice(b * block, (b + 1) * block)
-        halo[(1 - odd) * REACH + b] = near_ref[:, columns]
-        halo[odd * REACH + b] = jnp.where(is_late, rest_ref[:, columns], most_ref[:, columns])
-    halo[2 * REACH] = jnp.zeros_like(halo[0])
-    first = place_ref[0] * count - REACH
-    images = []
-    for at, b in enumerate(edges):
-        total = partial_ref[:, b * block:(b + 1) * block]
-        for slot in range(1, affinity_ref.shape[1]):
-            index = columns_ref[slot, b] - first
-            index = jnp.where(index < REACH, index, jnp.where(index < REACH + count, 2 * REACH, index - count))
-            total += rank_dot(halo[index], affinity_ref[b, slot], (1, 1))
-        images.append(split(total * block_root(degrees_ref, b, block)))
-        image_ref[:, at * block:(at + 1) * block] = images[-1]
-    halves = own_gram_ref[...] + gram_halves(jnp.concatenate(images, axis=1))
+        halo[b] = jnp.where(is_late, rest_ref[:, columns], most_ref[:, columns])
+    halo[REACH] = jnp.zeros_like(halo[0])
+    left = place_ref[0] % 2 == 0
+    image = side_images(count, block, left, place_ref, columns_ref, degrees_ref, affinity_ref, partial_ref, halo)
+    image_ref[...] = image
+    halves = near_gram_ref[...] + gram_halves(image)
     rank = halves.shape[0]
     halves = halves + pltpu.roll(halves, rank, 1)
     lane = lax.broadcasted_iota(jnp.int32, gram_ref.shape, 1)
     gram_ref[...] = jnp.where(lane < rank, halves[:rank // 2], halves[rank // 2:])
 
 
-def reorder_kernel(count, block, edges, inner_ref, outer_ref, reorder_ref, placed_ref):
+def reorder_kernel(count, block, edges, place_ref, inner_ref, near_ref, far_ref, reorder_ref, placed_ref):
+    odd = place_ref[0] % 2 == 1
     source = lax.broadcasted_iota(jnp.int32, (block, block), 0)
     for b in range(count):
-        at = edges.index(b) if b in edges else b
-        columns = slice(at * block, (at + 1) * block)
-        terms = outer_ref[:, columns] if b in edges else split(inner_ref[:, columns])
+        if b in edges:
+            columns = slice(b % REACH * block, (b % REACH + 1) * block)
+            nearer = odd if b < REACH else ~odd
+            terms = jnp.where(nearer, near_ref[:, columns], far_ref[:, columns])
+        else:
+            terms = split(inner_ref[:, b * block:(b + 1) * block])
         chosen = jnp.where(source == reorder_ref[b:b + 1, :], 1.0, 0.0).astype(jnp.bfloat16)
         moved = rank_dot(terms, chosen, (1, 0))
         moved = moved.astype(jnp.bfloat16)
@@ -224,10 +245,10 @@
 def gram_parts(gram, mesh_size):
     if mesh_size & (mesh_size - 1):
         return [lax.psum(gram, AXES)]
-    bits = [1 << k for k in range(mesh_size.bit_length() - 2, 0, -1)]
-    rounds = [[1]] + [[bit | 1] for bit in bits[:-2]]
+    bits = [1 << k for k in range(1, mesh_size.bit_length() - 1)]
+    rounds = [[1]] + [[bit | 1] for bit in bits[2:]]
     if bits:
-        rounds.append([bit | 1 for bit in bits[:-3:-1]] + [sum(bits[-2:])] * (len(bits) > 1))
+        rounds.append([bit | 1 for bit in bits[1::-1]] + [sum(bits[:2]) | 1] * (len(bits) > 1))
     parts = [gram]
     for masks in rounds:
         gram = sum(parts[1:], parts[0])
@@ -255,6 +276,7 @@
     count, slots, block, _ = affinity.shape
     items, rank = old_basis.shape
     width = REACH * block
+    assert count % REACH == 0 and count >= 2 * REACH
     edges = [b for b in range(count) if b < REACH or b >= count - REACH]
     affinity = in_vmem(affinity)
     basis = old_basis.T
@@ -280,15 +302,15 @@
     )(place, *map(in_hbm, (columns, basis, degree_rows)))
     distant = [lax.ppermute(far, AXES, pairs) for pairs in crossing_pairs(mesh_size)]
 
-    near, partial, inner = pl.pallas_call(
+    *near, partial, inner = pl.pallas_call(
         functools.partial(own_kernel, count, block, edges),
         out_shape=(
-            pltpu.VMEM((rank, width), jnp.bfloat16),
+            *[pltpu.VMEM((rank, block), jnp.bfloat16)] * REACH,
             pltpu.VMEM((rank, items), jnp.float32),
             pltpu.VMEM((rank, 2 * rank), jnp.float32),
         ),
         in_specs=[SMEM, SMEM] + [VMEM] * 3,
-        out_specs=(VMEM,) * 3,
+        out_specs=(VMEM,) * (2 + REACH),
         scratch_shapes=[pltpu.VMEM((count + 2 * REACH, rank, block), jnp.bfloat16)],
         compiler_params=PARAMS,
         cost_estimate=pl.CostEstimate(
@@ -296,27 +318,39 @@
         ),
         name="own",
     )(place, columns, *map(in_vmem, (basis, degree_rows)), affinity)
-    near = lax.ppermute(near, AXES, [(i, i ^ 1) for i in range(mesh_size) if i ^ 1 < mesh_size])
-
-    outer, gram = pl.pallas_call(
-        functools.partial(halo_kernel, count, block, edges, (2, mesh_size - 3)),
-        out_shape=(pltpu.VMEM((2 * rank, len(edges) * block), jnp.bfloat16), folded),
-        in_specs=[SMEM, SMEM] + [VMEM] * 7,
+    near = [lax.ppermute(x, AXES, [(i, i ^ 1) for i in range(mesh_size) if i ^ 1 < mesh_size]) for x in near]
+
+    side = dict(
         out_specs=(VMEM, VMEM),
-        scratch_shapes=[pltpu.VMEM((2 * REACH + 1, rank, block), jnp.bfloat16)],
-        compiler_params=PARAMS,
-        name="halo",
-    )(place, columns, *map(in_vmem, (degree_rows, near, *distant)), affinity, *map(in_vmem, (partial, inner)))
+        scratch_shapes=[pltpu.VMEM((REACH + 1, rank, block), jnp.bfloat16)],
+        compiler_params=PARAMS,
+        cost_estimate=pl.CostEstimate(flops=1, bytes_accessed=1, transcendentals=0),
+    )
+    side_image = pltpu.VMEM((2 * rank, width), jnp.bfloat16)
+    near_image, gram = pl.pallas_call(
+        functools.partial(near_kernel, count, block),
+        out_shape=(side_image, pltpu.VMEM((rank, 2 * rank), jnp.float32)),
+        in_specs=[SMEM, SMEM] + [VMEM] * (4 + REACH),
+        name="near",
+        **side,
+    )(place, columns, *map(in_vmem, (degree_rows, *near)), affinity, *map(in_vmem, (partial, inner)))
+    far_image, gram = pl.pallas_call(
+        functools.partial(far_kernel, count, block, (2, mesh_size - 3)),
+        out_shape=(side_image, folded),
+        in_specs=[SMEM, SMEM] + [VMEM] * 6,
+        name="far",
+        **side,
+    )(place, columns, *map(in_vmem, (degree_rows, *distant)), affinity, *map(in_vmem, (partial, gram)))
 
     placed = pl.pallas_call(
         functools.partial(reorder_kernel, count, block, edges),
         out_shape=pltpu.VMEM((3 * rank, items), jnp.bfloat16),
-        in_specs=[VMEM] * 3,
+        in_specs=[SMEM] + [VMEM] * 4,
         out_specs=VMEM,
         compiler_params=PARAMS,
         cost_estimate=pl.CostEstimate(flops=4 * rank * items * block, bytes_accessed=0, transcendentals=0),
         name="reorder",
-    )(in_vmem(partial), in_vmem(outer), in_vmem(reorder))
+    )(place, *map(in_vmem, (partial, near_image, far_image, reorder)))
 
     parts = gram_parts(gram, mesh_size)
     targets = pl.pallas_call(

time: 25 us -> 24.8 us (level)
  waiting for transfers between devices: 8.61 us -> 7.91 us
  Pallas kernels: 5.66 us -> 5.97 us
    ppermute x2, waiting for transfers between devices: 2.51 us -> 0.82 us  [body(): lax.ppermute(far, AXES, pairs)]
    ppermute x1 -> x2, waiting for transfers between devices: 0.01 us -> 0.87 us  [body(): lax.ppermute(x, AXES, [(i, i ^ 1) for i in range(mesh_size) if i ^ 1 < me...]
    ppermute x1 -> x2, starting transfers between devices: 0.24 us -> 0.58 us  [body(): lax.ppermute(x, AXES, [(i, i ^ 1) for i in range(mesh_size) if i ^ 1 < me...]
    pallas_call x1 -> x2, Pallas kernels: 0.69 us -> 1.01 us  [the longest x1 0.54 us: body(): pl.pallas_call(functools.partial(far_kernel, count, block, (2, mesh_size...]
  transfers between devices with their start and end apart: 9 -> 10, of which waited for: 7 -> 8; matrix products, arithmetic and copies ran while one was open for 0% -> 0% of each run, Pallas kernels for 6% -> 8%
where the time goes in v6:
time: 24.8 us; the launch traced here: 24.6 us
  starting transfers between devices  10.6 us (43%)
  waiting for transfers between devices  7.91 us (32%)
  Pallas kernels  5.97 us (24%)
    ppermute x6, starting transfers between devices, gram_parts(): lax.ppermute(gram, AXES, [(i, i ^ mask) for i in range(mesh_size)])  7.08 us
    ppermute x6, waiting for transfers between devices, gram_parts(): lax.ppermute(gram, AXES, [(i, i ^ mask) for i in range(mesh_size)])  6.23 us
    ppermute x2, starting transfers between devices, body(): lax.ppermute(far, AXES, pairs)  2.99 us
    pallas_call x1, Pallas kernels, body(): pl.pallas_call(functools.partial(targets_kernel, items * mesh_size, len(p...  2.33 us
    pallas_call x1, Pallas kernels, body(): pl.pallas_call(functools.partial(edges_kernel, width), out_shape=(pltpu.V...  1.19 us
    pallas_call x1, Pallas kernels, body(): pl.pallas_call(functools.partial(own_kernel, count, block, edges), out_sh...  1.1 us
    ppermute x2, waiting for transfers between devices, body(): lax.ppermute(x, AXES, [(i, i ^ 1) for i in range(mesh_size) if i ^ 1 < me...  0.87 us
    ppermute x2, waiting for transfers between devices, body(): lax.ppermute(far, AXES, pairs)  0.82 us
  transfers between devices with their start and end apart: 10, of which 8 were waited for; matrix products, arithmetic and copies ran while one was open for 0% of the time, Pallas kernels for 8%

profile of v6, /device:TPU:0, one launch (start us, length us, event | category | flops | bytes accessed | tf_op | source)
XLA Modules:
  0.0 24.6 jit_solution(1650950182392364951)
XLA Ops:
  0.0 0.0 copy-start
  0.0 1.2 %edges.1 = (bf16[64,512]{1,0:T(8,128)(2,1)S(1)}, s32[3,8]{1,0:T(4,128)S(4)}, bf16[64,2048]{1,0:T(8,128)(2,1)S(1)}, s32[16,128]{1,0:T(8,128)S(1)}) custom-call(s32[1]{0:T(128)} %bitcast.place_ref, s32[3,8]{1,0:T(4,128)} %bitcast.7, bf16[64,2048]{1,0:T(8,128)(2,1)} %bitcast.5, s32[16,128]{1,0:T(8,128)} %bitcast.6), custom_call_target="tpu_custom_call" | custom-call | flops 1572864000 | bytes 62914560 | tf_op jit(solution)/shard_map/edges/pallas_call | solution.py:288
  1.2 3.0 %collective-permute-start.1 = (bf16[64,512]{1,0:T(8,128)(2,1)S(1)}, bf16[64,512]{1,0:T(8,128)(2,1)S(1)}, u32[]{:S(2)}, u32[]{:S(2)}) collective-permute-start(bf16[64,512]{1,0:T(8,128)(2,1)S(1)} %get-tuple-element.19), channel_id=1, source_target_pairs={{3,4},{4,3},{5,6},{6,5},{7,8},{8,7},{9,10},{10,9},{11,12},{12,11},... | collective-permute-start | bytes 196616 | tf_op jit(solution)/shard_map/ppermute | solution.py:303
  4.2 0.0 collective-permute-start
  4.2 0.0 copy-done
  4.2 1.1 %own.1 = (bf16[64,256]{1,0:T(8,128)(2,1)S(1)}, bf16[64,256]{1,0:T(8,128)(2,1)S(1)}, f32[64,2048]{1,0:T(8,128)S(1)}, f32[64,128]{1,0:T(8,128)S(1)}) custom-call(s32[1]{0:T(128)} %bitcast.place_ref, s32[3,8]{1,0:T(4,128)S(4)} %get-tuple-element.17.columns_ref, bf16[64,2048]{1,0:T(8,128)(2,1)S(1)} %get-tuple-element.20.basis_ref, ...), custom_call_target="tpu_custom_call" | custom-call | flops 201326592 | tf_op jit(solution)/shard_map/own/pallas_call | solution.py:305
  5.3 0.2 collective-permute-start.2
  5.5 0.3 %collective-permute-start.3 = (bf16[64,256]{1,0:T(8,128)(2,1)S(1)}, bf16[64,256]{1,0:T(8,128)(2,1)S(1)}, u32[]{:S(2)}, u32[]{:S(2)}) collective-permute-start(bf16[64,256]{1,0:T(8,128)(2,1)S(1)} %get-tuple-element.23), channel_id=1, source_target_pairs={{0,1},{1,0},{2,3},{3,2},{4,5},{5,4},{6,7},{7,6},{8,9},{9,8},{10,11... | collective-permute-start | bytes 98312 | tf_op jit(solution)/shard_map/ppermute | solution.py:321
  5.9 0.7 %collective-permute-done.2.refs_0_ = bf16[64,256]{1,0:T(8,128)(2,1)S(1)} collective-permute-done((bf16[64,256]{1,0:T(8,128)(2,1)S(1)}, bf16[64,256]{1,0:T(8,128)(2,1)S(1)}, u32[]{:S(2)}, u32[]{:S(2)}) %collective-permute-start.2) | collective-permute-done | bytes 32800 | tf_op jit(solution)/shard_map/ppermute | solution.py:321
  6.6 0.2 collective-permute-done.3.refs_1_
  6.7 0.0 copy-start.1
  6.7 0.5 %near.1 = (bf16[128,512]{1,0:T(8,128)(2,1)S(1)}, f32[64,128]{1,0:T(8,128)S(1)}) custom-call(s32[1]{0:T(128)} %bitcast.place_ref, s32[3,8]{1,0:T(4,128)S(4)} %get-tuple-element.17.columns_ref, s32[16,128]{1,0:T(8,128)S(1)} %get-tuple-element.18.degrees_ref, bf16[64,256]{1,0:T(8,128)(2,1)S(1)} %collective-permute-done.2.refs_0_, ...), custom_call_target="tpu_custom_call" | custom-call | flops 1 | bytes 1 | tf_op jit(solution)/shard_map/near/pallas_call | solution.py:330
  7.2 0.0 collective-permute-done.1.most_ref
  7.2 0.8 %collective-permute-done.rest_ref = bf16[64,512]{1,0:T(8,128)(2,1)S(1)} collective-permute-done((bf16[64,512]{1,0:T(8,128)(2,1)S(1)}, bf16[64,512]{1,0:T(8,128)(2,1)S(1)}, u32[]{:S(2)}, u32[]{:S(2)}) %collective-permute-start) | collective-permute-done | bytes 65568 | tf_op jit(solution)/shard_map/ppermute | solution.py:303
  8.0 0.5 %far.1 = (bf16[128,512]{1,0:T(8,128)(2,1)S(1)}, f32[32,128]{1,0:T(8,128)S(1)}) custom-call(s32[1]{0:T(128)} %bitcast.place_ref, s32[3,8]{1,0:T(4,128)S(4)} %get-tuple-element.17.columns_ref, s32[16,128]{1,0:T(8,128)S(1)} %get-tuple-element.18.degrees_ref, bf16[64,512]{1,0:T(8,128)(2,1)S(1)} %collective-permute-done.rest_ref, ...), custom_call_target="tpu_custom_call" | custom-call | flops 1 | bytes 1 | tf_op jit(solution)/shard_map/far/pallas_call | solution.py:337
  8.6 0.1 collective-permute-start.4
  8.7 1.2 %collective-permute-done.4 = f32[32,128]{1,0:T(8,128)S(1)} collective-permute-done((f32[32,128]{1,0:T(8,128)S(1)}, f32[32,128]{1,0:T(8,128)S(1)}, u32[]{:S(2)}, u32[]{:S(2)}) %collective-permute-start.4) | collective-permute-done | bytes 16416 | tf_op jit(solution)/shard_map/ppermute | solution.py:255
  9.8 1.5 %collective-permute-start.5 = (f32[32,128]{1,0:T(8,128)S(1)}, f32[32,128]{1,0:T(8,128)S(1)}, u32[]{:S(2)}, u32[]{:S(2)}) collective-permute-start(f32[32,128]{1,0:T(8,128)S(1)} %add.13), channel_id=1, source_target_pairs={{0,9},{1,8},{2,11},{3,10},{4,13},{5,12},{6,15},{7,14},{8,1},{9,0},... | collective-permute-start | bytes 49160 | tf_op jit(solution)/shard_map/ppermute | solution.py:255
  11.3 1.7 %collective-permute-done.5 = f32[32,128]{1,0:T(8,128)S(1)} collective-permute-done((f32[32,128]{1,0:T(8,128)S(1)}, f32[32,128]{1,0:T(8,128)S(1)}, u32[]{:S(2)}, u32[]{:S(2)}) %collective-permute-start.5) | collective-permute-done | bytes 16416 | tf_op jit(solution)/shard_map/ppermute | solution.py:255
  13.0 2.5 %collective-permute-start.6 = (f32[32,128]{1,0:T(8,128)S(1)}, f32[32,128]{1,0:T(8,128)S(1)}, u32[]{:S(2)}, u32[]{:S(2)}) collective-permute-start(f32[32,128]{1,0:T(8,128)S(1)} %add.14), channel_id=1, source_target_pairs={{0,17},{1,16},{2,19},{3,18},{4,21},{5,20},{6,23},{7,22},{8,25},{9,... | collective-permute-start | bytes 49160 | tf_op jit(solution)/shard_map/ppermute | solution.py:255
  15.5 1.6 %collective-permute-done.6 = f32[32,128]{1,0:T(8,128)S(1)} collective-permute-done((f32[32,128]{1,0:T(8,128)S(1)}, f32[32,128]{1,0:T(8,128)S(1)}, u32[]{:S(2)}, u32[]{:S(2)}) %collective-permute-start.6) | collective-permute-done | bytes 16416 | tf_op jit(solution)/shard_map/ppermute | solution.py:255
  17.1 2.0 %collective-permute-start.9 = (f32[32,128]{1,0:T(8,128)S(1)}, f32[32,128]{1,0:T(8,128)S(1)}, u32[]{:S(2)}, u32[]{:S(2)}) collective-permute-start(f32[32,128]{1,0:T(8,128)S(1)} %add.15.refs_0_), channel_id=1, source_target_pairs={{0,7},{1,6},{2,5},{3,4},{4,3},{5,2},{6,1},{7,0},{8,15},{9,14},{10,... | collective-permute-start | bytes 49160 | tf_op jit(solution)/shard_map/ppermute | solution.py:255
  19.1 0.0 collective-permute-start.8
  19.1 1.0 %collective-permute-start.7 = (f32[32,128]{1,0:T(8,128)S(1)}, f32[32,128]{1,0:T(8,128)S(1)}, u32[]{:S(2)}, u32[]{:S(2)}) collective-permute-start(f32[32,128]{1,0:T(8,128)S(1)} %add.15.refs_0_), channel_id=1, source_target_pairs={{0,5},{1,4},{2,7},{3,6},{4,1},{5,0},{6,3},{7,2},{8,13},{9,12},{10,... | collective-permute-start | bytes 49160 | tf_op jit(solution)/shard_map/ppermute | solution.py:255
  20.1 0.0 copy-done.1
  20.1 0.3 %reorder.1.refs_4_ = bf16[192,2048]{1,0:T(8,128)(2,1)S(1)} custom-call(s32[1]{0:T(128)} %bitcast.place_ref, f32[64,2048]{1,0:T(8,128)S(1)} %get-tuple-element.21.refs_3_.partial_ref.inner_ref, bf16[128,512]{1,0:T(8,128)(2,1)S(1)} %get-tuple-element.27.near_ref, bf16[128,512]{1,0:T(8,128)(2,1)S(1)} %get-tuple-element.28.far_ref, s32[8,256]{1,0:T(8,128)S(1)} %copy-done.1), custom_call_target="tpu_custom_call" | custom-call | flops 134217728 | tf_op jit(solution)/shard_map/reorder/pallas_call | solution.py:345
  20.5 0.7 %collective-permute-done.9.refs_3_ = f32[32,128]{1,0:T(8,128)S(1)} collective-permute-done((f32[32,128]{1,0:T(8,128)S(1)}, f32[32,128]{1,0:T(8,128)S(1)}, u32[]{:S(2)}, u32[]{:S(2)}) %collective-permute-start.9) | collective-permute-done | bytes 16416 | tf_op jit(solution)/shard_map/ppermute | solution.py:255
  21.1 1.1 %collective-permute-done.8.refs_2_ = f32[32,128]{1,0:T(8,128)S(1)} collective-permute-done((f32[32,128]{1,0:T(8,128)S(1)}, f32[32,128]{1,0:T(8,128)S(1)}, u32[]{:S(2)}, u32[]{:S(2)}) %collective-permute-start.8) | collective-permute-done | bytes 16416 | tf_op jit(solution)/shard_map/ppermute | solution.py:255
  22.3 0.0 collective-permute-done.7.refs_1_
  22.3 2.3 %targets.1 = f32[64,2048]{1,0:T(8,128)} custom-call(f32[32,128]{1,0:T(8,128)S(1)} %add.15.refs_0_, f32[32,128]{1,0:T(8,128)S(1)} %collective-permute-done.7.refs_1_, f32[32,128]{1,0:T(8,128)S(1)} %collective-permute-done.8.refs_2_, f32[32,128]{1,0:T(8,128)S(1)} %collective-permute-done.9.refs_3_, bf16[192,2048]{1,0:T(8,128)(2,1)S(1)} %reorder.1.refs_4_), custom_call_target="tpu_custom_call" | custom-call | tf_op jit(solution)/shard_map/targets/pallas_call | solution.py:356
  (3 shorter events, 0.0 us)
Async XLA Ops:
  0.0 4.2 %copy-start = (bf16[8,3,256,256]{3,2,1,0:T(8,128)(2,1)S(1)}, bf16[8,3,256,256]{3,2,1,0:T(8,128)(2,1)}, u32[]{:S(2)}) copy-start(bf16[8,3,256,256]{3,2,1,0:T(8,128)(2,1)} %affinity_ref.3) | copy-start | bytes 9437188
  1.2 6.0 %collective-permute-start.1 = (bf16[64,512]{1,0:T(8,128)(2,1)S(1)}, bf16[64,512]{1,0:T(8,128)(2,1)S(1)}, u32[]{:S(2)}, u32[]{:S(2)}) collective-permute-start(bf16[64,512]{1,0:T(8,128)(2,1)S(1)} %get-tuple-element.19), channel_id=1, source_target_pairs={{3,4},{4,3},{5,6},{6,5},{7,8},{8,7},{9,10},{10,9},{11,12},{12,11},... | collective-permute-start | bytes 196616 | tf_op jit(solution)/shard_map/ppermute | solution.py:303
  4.2 3.9 %collective-permute-start = (bf16[64,512]{1,0:T(8,128)(2,1)S(1)}, bf16[64,512]{1,0:T(8,128)(2,1)S(1)}, u32[]{:S(2)}, u32[]{:S(2)}) collective-permute-start(bf16[64,512]{1,0:T(8,128)(2,1)S(1)} %get-tuple-element.19), channel_id=1, source_target_pairs={{4,5},{5,4},{6,7},{7,6},{8,9},{9,8},{10,11},{11,10},{12,13},{13,12... | collective-permute-start | bytes 196616 | tf_op jit(solution)/shard_map/ppermute | solution.py:303
  5.3 1.3 %collective-permute-start.2 = (bf16[64,256]{1,0:T(8,128)(2,1)S(1)}, bf16[64,256]{1,0:T(8,128)(2,1)S(1)}, u32[]{:S(2)}, u32[]{:S(2)}) collective-permute-start(bf16[64,256]{1,0:T(8,128)(2,1)S(1)} %get-tuple-element.22), channel_id=1, source_target_pairs={{0,1},{1,0},{2,3},{3,2},{4,5},{5,4},{6,7},{7,6},{8,9},{9,8},{10,11... | collective-permute-start | bytes 98312 | tf_op jit(solution)/shard_map/ppermute | solution.py:321
  5.5 1.2 %collective-permute-start.3 = (bf16[64,256]{1,0:T(8,128)(2,1)S(1)}, bf16[64,256]{1,0:T(8,128)(2,1)S(1)}, u32[]{:S(2)}, u32[]{:S(2)}) collective-permute-start(bf16[64,256]{1,0:T(8,128)(2,1)S(1)} %get-tuple-element.23), channel_id=1, source_target_pairs={{0,1},{1,0},{2,3},{3,2},{4,5},{5,4},{6,7},{7,6},{8,9},{9,8},{10,11... | collective-permute-start | bytes 98312 | tf_op jit(solution)/shard_map/ppermute | solution.py:321
  6.7 13.4 %copy-start.1 = (s32[8,256]{1,0:T(8,128)S(1)}, s32[8,256]{1,0:T(8,128)}, u32[]{:S(2)}) copy-start(s32[8,256]{1,0:T(8,128)} %reorder_ref.1) | copy-start | bytes 24580
  8.6 1.2 %collective-permute-start.4 = (f32[32,128]{1,0:T(8,128)S(1)}, f32[32,128]{1,0:T(8,128)S(1)}, u32[]{:S(2)}, u32[]{:S(2)}) collective-permute-start(f32[32,128]{1,0:T(8,128)S(1)} %get-tuple-element.26), channel_id=1, source_target_pairs={{0,1},{1,0},{2,3},{3,2},{4,5},{5,4},{6,7},{7,6},{8,9},{9,8},{10,11... | collective-permute-start | bytes 49160 | tf_op jit(solution)/shard_map/ppermute | solution.py:255
  9.8 3.2 %collective-permute-start.5 = (f32[32,128]{1,0:T(8,128)S(1)}, f32[32,128]{1,0:T(8,128)S(1)}, u32[]{:S(2)}, u32[]{:S(2)}) collective-permute-start(f32[32,128]{1,0:T(8,128)S(1)} %add.13), channel_id=1, source_target_pairs={{0,9},{1,8},{2,11},{3,10},{4,13},{5,12},{6,15},{7,14},{8,1},{9,0},... | collective-permute-start | bytes 49160 | tf_op jit(solution)/shard_map/ppermute | solution.py:255
  13.0 4.1 %collective-permute-start.6 = (f32[32,128]{1,0:T(8,128)S(1)}, f32[32,128]{1,0:T(8,128)S(1)}, u32[]{:S(2)}, u32[]{:S(2)}) collective-permute-start(f32[32,128]{1,0:T(8,128)S(1)} %add.14), channel_id=1, source_target_pairs={{0,17},{1,16},{2,19},{3,18},{4,21},{5,20},{6,23},{7,22},{8,25},{9,... | collective-permute-start | bytes 49160 | tf_op jit(solution)/shard_map/ppermute | solution.py:255
  17.1 4.1 %collective-permute-start.9 = (f32[32,128]{1,0:T(8,128)S(1)}, f32[32,128]{1,0:T(8,128)S(1)}, u32[]{:S(2)}, u32[]{:S(2)}) collective-permute-start(f32[32,128]{1,0:T(8,128)S(1)} %add.15.refs_0_), channel_id=1, source_target_pairs={{0,7},{1,6},{2,5},{3,4},{4,3},{5,2},{6,1},{7,0},{8,15},{9,14},{10,... | collective-permute-start | bytes 49160 | tf_op jit(solution)/shard_map/ppermute | solution.py:255
  19.1 3.2 %collective-permute-start.8 = (f32[32,128]{1,0:T(8,128)S(1)}, f32[32,128]{1,0:T(8,128)S(1)}, u32[]{:S(2)}, u32[]{:S(2)}) collective-permute-start(f32[32,128]{1,0:T(8,128)S(1)} %add.15.refs_0_), channel_id=1, source_target_pairs={{0,3},{1,2},{2,1},{3,0},{4,7},{5,6},{6,5},{7,4},{8,11},{9,10},{10,... | collective-permute-start | bytes 49160 | tf_op jit(solution)/shard_map/ppermute | solution.py:255
  19.1 3.2 %collective-permute-start.7 = (f32[32,128]{1,0:T(8,128)S(1)}, f32[32,128]{1,0:T(8,128)S(1)}, u32[]{:S(2)}, u32[]{:S(2)}) collective-permute-start(f32[32,128]{1,0:T(8,128)S(1)} %add.15.refs_0_), channel_id=1, source_target_pairs={{0,5},{1,4},{2,7},{3,6},{4,1},{5,0},{6,3},{7,2},{8,13},{9,12},{10,... | collective-permute-start | bytes 49160 | tf_op jit(solution)/shard_map/ppermute | solution.py:255

commit v7 on v6

--- a/solution.py
+++ b/solution.py
@@ -109,20 +109,29 @@
 
 
 def side_images(count, block, left, place_ref, columns_ref, degrees_ref, affinity_ref, partial_ref, halo):
-    start = jnp.where(left, 0, count - REACH)
     first = place_ref[0] * count - REACH
     pieces = block // LANES
+    slots = affinity_ref.shape[1]
     images = []
-    for b in range(REACH):
-        row = start + b
+    for r in range(REACH):
+        row = jnp.where(left, r, count - 1 - r)
         total = partial_ref[:, pl.ds(pl.multiple_of(row * block, block), block)]
-        for slot in range(1, affinity_ref.shape[1]):
-            index = columns_ref[slot, row] - first
-            index = jnp.where(index < REACH, index, jnp.where(index < REACH + count, REACH, index - REACH - count))
+        named = [columns_ref[slot, row] - first for slot in range(slots)]
+        beyond = [(index < REACH) | (index >= REACH + count) for index in named]
+        picks = [(slot, named[slot], beyond[slot]) for slot in range(1, slots)]
+        if REACH - r == 1:
+            slot, index, outside = picks[0]
+            for other, other_index, other_outside in picks[1:]:
+                slot, index = jnp.where(other_outside, other, slot), jnp.where(other_outside, other_index, index)
+                outside = outside | other_outside
+            picks = [(slot, index, outside)]
+        for slot, index, outside in picks:
+            index = jnp.where(outside, jnp.where(index < REACH, index, index - REACH - count), REACH)
             total += rank_dot(halo[index], affinity_ref[row, slot], (1, 1))
         root = [inverse_root(degrees_ref, row * pieces + c) for c in range(pieces)]
         images.append(split(total * jnp.concatenate(root, axis=1)))
-    return jnp.concatenate(images, axis=1)
+    placed = [jnp.where(left, near, far) for near, far in zip(images, images[::-1])]
+    return jnp.concatenate(images, axis=1), jnp.concatenate(placed, axis=1)
 
 
 def near_kernel(count, block, place_ref, columns_ref, degrees_ref, *refs):
@@ -131,8 +140,8 @@
         halo[b] = near_refs[b][...]
     halo[REACH] = jnp.zeros_like(halo[0])
     left = place_ref[0] % 2 == 1
-    image = side_images(count, block, left, place_ref, columns_ref, degrees_ref, affinity_ref, partial_ref, halo)
-    image_ref[...] = image
+    image, placed = side_images(count, block, left, place_ref, columns_ref, degrees_ref, affinity_ref, partial_ref, halo)
+    image_ref[...] = placed
     gram_ref[...] = own_gram_ref[...] + gram_halves(image)
 
 
@@ -146,8 +155,8 @@
         halo[b] = jnp.where(is_late, rest_ref[:, columns], most_ref[:, columns])
     halo[REACH] = jnp.zeros_like(halo[0])
     left = place_ref[0] % 2 == 0
-    image = side_images(count, block, left, place_ref, columns_ref, degrees_ref, affinity_ref, partial_ref, halo)
-    image_ref[...] = image
+    image, placed = side_images(count, block, left, place_ref, columns_ref, degrees_ref, affinity_ref, partial_ref, halo)
+    image_ref[...] = placed
     halves = near_gram_ref[...] + gram_halves(image)
     rank = halves.shape[0]
     halves = halves + pltpu.roll(halves, rank, 1)

time: 24.8 us -> 24.8 us (level)
  no operation moved by 1% of the time
where the time goes in v7:
time: 24.8 us; the launch traced here: 24.6 us
  starting transfers between devices  10.6 us (43%)
  waiting for transfers between devices  7.9 us (32%)
  Pallas kernels  6 us (24%)
    ppermute x6, starting transfers between devices, gram_parts(): lax.ppermute(gram, AXES, [(i, i ^ mask) for i in range(mesh_size)])  7.08 us
    ppermute x6, waiting for transfers between devices, gram_parts(): lax.ppermute(gram, AXES, [(i, i ^ mask) for i in range(mesh_size)])  6.22 us
    ppermute x2, starting transfers between devices, body(): lax.ppermute(far, AXES, pairs)  2.99 us
    pallas_call x1, Pallas kernels, body(): pl.pallas_call(functools.partial(targets_kernel, items * mesh_size, len(p...  2.33 us
    pallas_call x1, Pallas kernels, body(): pl.pallas_call(functools.partial(edges_kernel, width), out_shape=(pltpu.V...  1.19 us
    pallas_call x1, Pallas kernels, body(): pl.pallas_call(functools.partial(own_kernel, count, block, edges), out_sh...  1.1 us
    ppermute x2, waiting for transfers between devices, body(): lax.ppermute(x, AXES, [(i, i ^ 1) for i in range(mesh_size) if i ^ 1 < me...  0.87 us
    ppermute x2, waiting for transfers between devices, body(): lax.ppermute(far, AXES, pairs)  0.81 us
  transfers between devices with their start and end apart: 10, of which 8 were waited for; matrix products, arithmetic and copies ran while one was open for 0% of the time, Pallas kernels for 8%

profile of v7, /device:TPU:0, one launch (start us, length us, event | category | flops | bytes accessed | tf_op | source)
XLA Modules:
  0.0 24.6 jit_solution(7278866171003357385)
XLA Ops:
  0.0 0.0 copy-start
  0.0 1.2 %edges.1 = (bf16[64,512]{1,0:T(8,128)(2,1)S(1)}, s32[3,8]{1,0:T(4,128)S(4)}, bf16[64,2048]{1,0:T(8,128)(2,1)S(1)}, s32[16,128]{1,0:T(8,128)S(1)}) custom-call(s32[1]{0:T(128)} %bitcast.place_ref, s32[3,8]{1,0:T(4,128)} %bitcast.7, bf16[64,2048]{1,0:T(8,128)(2,1)} %bitcast.5, s32[16,128]{1,0:T(8,128)} %bitcast.6), custom_call_target="tpu_custom_call" | custom-call | flops 1572864000 | bytes 62914560 | tf_op jit(solution)/shard_map/edges/pallas_call | solution.py:297
  1.2 3.0 %collective-permute-start.1 = (bf16[64,512]{1,0:T(8,128)(2,1)S(1)}, bf16[64,512]{1,0:T(8,128)(2,1)S(1)}, u32[]{:S(2)}, u32[]{:S(2)}) collective-permute-start(bf16[64,512]{1,0:T(8,128)(2,1)S(1)} %get-tuple-element.19), channel_id=1, source_target_pairs={{3,4},{4,3},{5,6},{6,5},{7,8},{8,7},{9,10},{10,9},{11,12},{12,11},... | collective-permute-start | bytes 196616 | tf_op jit(solution)/shard_map/ppermute | solution.py:312
  4.2 0.0 collective-permute-start
  4.2 0.0 copy-done
  4.2 1.1 %own.1 = (bf16[64,256]{1,0:T(8,128)(2,1)S(1)}, bf16[64,256]{1,0:T(8,128)(2,1)S(1)}, f32[64,2048]{1,0:T(8,128)S(1)}, f32[64,128]{1,0:T(8,128)S(1)}) custom-call(s32[1]{0:T(128)} %bitcast.place_ref, s32[3,8]{1,0:T(4,128)S(4)} %get-tuple-element.17.columns_ref, bf16[64,2048]{1,0:T(8,128)(2,1)S(1)} %get-tuple-element.20.basis_ref, ...), custom_call_target="tpu_custom_call" | custom-call | flops 201326592 | tf_op jit(solution)/shard_map/own/pallas_call | solution.py:314
  5.3 0.2 collective-permute-start.2
  5.5 0.3 %collective-permute-start.3 = (bf16[64,256]{1,0:T(8,128)(2,1)S(1)}, bf16[64,256]{1,0:T(8,128)(2,1)S(1)}, u32[]{:S(2)}, u32[]{:S(2)}) collective-permute-start(bf16[64,256]{1,0:T(8,128)(2,1)S(1)} %get-tuple-element.23), channel_id=1, source_target_pairs={{0,1},{1,0},{2,3},{3,2},{4,5},{5,4},{6,7},{7,6},{8,9},{9,8},{10,11... | collective-permute-start | bytes 98312 | tf_op jit(solution)/shard_map/ppermute | solution.py:330
  5.9 0.7 %collective-permute-done.2.refs_0_ = bf16[64,256]{1,0:T(8,128)(2,1)S(1)} collective-permute-done((bf16[64,256]{1,0:T(8,128)(2,1)S(1)}, bf16[64,256]{1,0:T(8,128)(2,1)S(1)}, u32[]{:S(2)}, u32[]{:S(2)}) %collective-permute-start.2) | collective-permute-done | bytes 32800 | tf_op jit(solution)/shard_map/ppermute | solution.py:330
  6.6 0.2 collective-permute-done.3.refs_1_
  6.7 0.0 copy-start.1
  6.7 0.5 %near.1 = (bf16[128,512]{1,0:T(8,128)(2,1)S(1)}, f32[64,128]{1,0:T(8,128)S(1)}) custom-call(s32[1]{0:T(128)} %bitcast.place_ref, s32[3,8]{1,0:T(4,128)S(4)} %get-tuple-element.17.columns_ref, s32[16,128]{1,0:T(8,128)S(1)} %get-tuple-element.18.degrees_ref, bf16[64,256]{1,0:T(8,128)(2,1)S(1)} %collective-permute-done.2.refs_0_, ...), custom_call_target="tpu_custom_call" | custom-call | flops 1 | bytes 1 | tf_op jit(solution)/shard_map/near/pallas_call | solution.py:339
  7.2 0.0 collective-permute-done.1.most_ref
  7.2 0.8 %collective-permute-done.rest_ref = bf16[64,512]{1,0:T(8,128)(2,1)S(1)} collective-permute-done((bf16[64,512]{1,0:T(8,128)(2,1)S(1)}, bf16[64,512]{1,0:T(8,128)(2,1)S(1)}, u32[]{:S(2)}, u32[]{:S(2)}) %collective-permute-start) | collective-permute-done | bytes 65568 | tf_op jit(solution)/shard_map/ppermute | solution.py:312
  8.0 0.6 %far.1 = (bf16[128,512]{1,0:T(8,128)(2,1)S(1)}, f32[32,128]{1,0:T(8,128)S(1)}) custom-call(s32[1]{0:T(128)} %bitcast.place_ref, s32[3,8]{1,0:T(4,128)S(4)} %get-tuple-element.17.columns_ref, s32[16,128]{1,0:T(8,128)S(1)} %get-tuple-element.18.degrees_ref, bf16[64,512]{1,0:T(8,128)(2,1)S(1)} %collective-permute-done.rest_ref, ...), custom_call_target="tpu_custom_call" | custom-call | flops 1 | bytes 1 | tf_op jit(solution)/shard_map/far/pallas_call | solution.py:346
  8.6 0.1 collective-permute-start.4
  8.7 1.2 %collective-permute-done.4 = f32[32,128]{1,0:T(8,128)S(1)} collective-permute-done((f32[32,128]{1,0:T(8,128)S(1)}, f32[32,128]{1,0:T(8,128)S(1)}, u32[]{:S(2)}, u32[]{:S(2)}) %collective-permute-start.4) | collective-permute-done | bytes 16416 | tf_op jit(solution)/shard_map/ppermute | solution.py:264
  9.9 1.5 %collective-permute-start.5 = (f32[32,128]{1,0:T(8,128)S(1)}, f32[32,128]{1,0:T(8,128)S(1)}, u32[]{:S(2)}, u32[]{:S(2)}) collective-permute-start(f32[32,128]{1,0:T(8,128)S(1)} %add.13), channel_id=1, source_target_pairs={{0,9},{1,8},{2,11},{3,10},{4,13},{5,12},{6,15},{7,14},{8,1},{9,0},... | collective-permute-start | bytes 49160 | tf_op jit(solution)/shard_map/ppermute | solution.py:264
  11.4 1.7 %collective-permute-done.5 = f32[32,128]{1,0:T(8,128)S(1)} collective-permute-done((f32[32,128]{1,0:T(8,128)S(1)}, f32[32,128]{1,0:T(8,128)S(1)}, u32[]{:S(2)}, u32[]{:S(2)}) %collective-permute-start.5) | collective-permute-done | bytes 16416 | tf_op jit(solution)/shard_map/ppermute | solution.py:264
  13.0 2.5 %collective-permute-start.6 = (f32[32,128]{1,0:T(8,128)S(1)}, f32[32,128]{1,0:T(8,128)S(1)}, u32[]{:S(2)}, u32[]{:S(2)}) collective-permute-start(f32[32,128]{1,0:T(8,128)S(1)} %add.14), channel_id=1, source_target_pairs={{0,17},{1,16},{2,19},{3,18},{4,21},{5,20},{6,23},{7,22},{8,25},{9,... | collective-permute-start | bytes 49160 | tf_op jit(solution)/shard_map/ppermute | solution.py:264
  15.5 1.6 %collective-permute-done.6 = f32[32,128]{1,0:T(8,128)S(1)} collective-permute-done((f32[32,128]{1,0:T(8,128)S(1)}, f32[32,128]{1,0:T(8,128)S(1)}, u32[]{:S(2)}, u32[]{:S(2)}) %collective-permute-start.6) | collective-permute-done | bytes 16416 | tf_op jit(solution)/shard_map/ppermute | solution.py:264
  17.1 2.0 %collective-permute-start.9 = (f32[32,128]{1,0:T(8,128)S(1)}, f32[32,128]{1,0:T(8,128)S(1)}, u32[]{:S(2)}, u32[]{:S(2)}) collective-permute-start(f32[32,128]{1,0:T(8,128)S(1)} %add.15.refs_0_), channel_id=1, source_target_pairs={{0,7},{1,6},{2,5},{3,4},{4,3},{5,2},{6,1},{7,0},{8,15},{9,14},{10,... | collective-permute-start | bytes 49160 | tf_op jit(solution)/shard_map/ppermute | solution.py:264
  19.1 0.0 collective-permute-start.8
  19.1 1.0 %collective-permute-start.7 = (f32[32,128]{1,0:T(8,128)S(1)}, f32[32,128]{1,0:T(8,128)S(1)}, u32[]{:S(2)}, u32[]{:S(2)}) collective-permute-start(f32[32,128]{1,0:T(8,128)S(1)} %add.15.refs_0_), channel_id=1, source_target_pairs={{0,5},{1,4},{2,7},{3,6},{4,1},{5,0},{6,3},{7,2},{8,13},{9,12},{10,... | collective-permute-start | bytes 49160 | tf_op jit(solution)/shard_map/ppermute | solution.py:264
  20.1 0.0 copy-done.1
  20.1 0.4 %reorder.1.refs_4_ = bf16[192,2048]{1,0:T(8,128)(2,1)S(1)} custom-call(s32[1]{0:T(128)} %bitcast.place_ref, f32[64,2048]{1,0:T(8,128)S(1)} %get-tuple-element.21.refs_3_.partial_ref.inner_ref, bf16[128,512]{1,0:T(8,128)(2,1)S(1)} %get-tuple-element.27.near_ref, bf16[128,512]{1,0:T(8,128)(2,1)S(1)} %get-tuple-element.28.far_ref, s32[8,256]{1,0:T(8,128)S(1)} %copy-done.1), custom_call_target="tpu_custom_call" | custom-call | flops 134217728 | tf_op jit(solution)/shard_map/reorder/pallas_call | solution.py:354
  20.5 0.7 %collective-permute-done.9.refs_3_ = f32[32,128]{1,0:T(8,128)S(1)} collective-permute-done((f32[32,128]{1,0:T(8,128)S(1)}, f32[32,128]{1,0:T(8,128)S(1)}, u32[]{:S(2)}, u32[]{:S(2)}) %collective-permute-start.9) | collective-permute-done | bytes 16416 | tf_op jit(solution)/shard_map/ppermute | solution.py:264
  21.2 1.1 %collective-permute-done.8.refs_2_ = f32[32,128]{1,0:T(8,128)S(1)} collective-permute-done((f32[32,128]{1,0:T(8,128)S(1)}, f32[32,128]{1,0:T(8,128)S(1)}, u32[]{:S(2)}, u32[]{:S(2)}) %collective-permute-start.8) | collective-permute-done | bytes 16416 | tf_op jit(solution)/shard_map/ppermute | solution.py:264
  22.3 0.0 collective-permute-done.7.refs_1_
  22.3 2.3 %targets.1 = f32[64,2048]{1,0:T(8,128)} custom-call(f32[32,128]{1,0:T(8,128)S(1)} %add.15.refs_0_, f32[32,128]{1,0:T(8,128)S(1)} %collective-permute-done.7.refs_1_, f32[32,128]{1,0:T(8,128)S(1)} %collective-permute-done.8.refs_2_, f32[32,128]{1,0:T(8,128)S(1)} %collective-permute-done.9.refs_3_, bf16[192,2048]{1,0:T(8,128)(2,1)S(1)} %reorder.1.refs_4_), custom_call_target="tpu_custom_call" | custom-call | tf_op jit(solution)/shard_map/targets/pallas_call | solution.py:365
  (3 shorter events, 0.0 us)
Async XLA Ops:
  0.0 4.2 %copy-start = (bf16[8,3,256,256]{3,2,1,0:T(8,128)(2,1)S(1)}, bf16[8,3,256,256]{3,2,1,0:T(8,128)(2,1)}, u32[]{:S(2)}) copy-start(bf16[8,3,256,256]{3,2,1,0:T(8,128)(2,1)} %affinity_ref.3) | copy-start | bytes 9437188
  1.2 6.0 %collective-permute-start.1 = (bf16[64,512]{1,0:T(8,128)(2,1)S(1)}, bf16[64,512]{1,0:T(8,128)(2,1)S(1)}, u32[]{:S(2)}, u32[]{:S(2)}) collective-permute-start(bf16[64,512]{1,0:T(8,128)(2,1)S(1)} %get-tuple-element.19), channel_id=1, source_target_pairs={{3,4},{4,3},{5,6},{6,5},{7,8},{8,7},{9,10},{10,9},{11,12},{12,11},... | collective-permute-start | bytes 196616 | tf_op jit(solution)/shard_map/ppermute | solution.py:312
  4.2 3.9 %collective-permute-start = (bf16[64,512]{1,0:T(8,128)(2,1)S(1)}, bf16[64,512]{1,0:T(8,128)(2,1)S(1)}, u32[]{:S(2)}, u32[]{:S(2)}) collective-permute-start(bf16[64,512]{1,0:T(8,128)(2,1)S(1)} %get-tuple-element.19), channel_id=1, source_target_pairs={{4,5},{5,4},{6,7},{7,6},{8,9},{9,8},{10,11},{11,10},{12,13},{13,12... | collective-permute-start | bytes 196616 | tf_op jit(solution)/shard_map/ppermute | solution.py:312
  5.3 1.3 %collective-permute-start.2 = (bf16[64,256]{1,0:T(8,128)(2,1)S(1)}, bf16[64,256]{1,0:T(8,128)(2,1)S(1)}, u32[]{:S(2)}, u32[]{:S(2)}) collective-permute-start(bf16[64,256]{1,0:T(8,128)(2,1)S(1)} %get-tuple-element.22), channel_id=1, source_target_pairs={{0,1},{1,0},{2,3},{3,2},{4,5},{5,4},{6,7},{7,6},{8,9},{9,8},{10,11... | collective-permute-start | bytes 98312 | tf_op jit(solution)/shard_map/ppermute | solution.py:330
  5.5 1.2 %collective-permute-start.3 = (bf16[64,256]{1,0:T(8,128)(2,1)S(1)}, bf16[64,256]{1,0:T(8,128)(2,1)S(1)}, u32[]{:S(2)}, u32[]{:S(2)}) collective-permute-start(bf16[64,256]{1,0:T(8,128)(2,1)S(1)} %get-tuple-element.23), channel_id=1, source_target_pairs={{0,1},{1,0},{2,3},{3,2},{4,5},{5,4},{6,7},{7,6},{8,9},{9,8},{10,11... | collective-permute-start | bytes 98312 | tf_op jit(solution)/shard_map/ppermute | solution.py:330
  6.7 13.4 %copy-start.1 = (s32[8,256]{1,0:T(8,128)S(1)}, s32[8,256]{1,0:T(8,128)}, u32[]{:S(2)}) copy-start(s32[8,256]{1,0:T(8,128)} %reorder_ref.1) | copy-start | bytes 24580
  8.6 1.2 %collective-permute-start.4 = (f32[32,128]{1,0:T(8,128)S(1)}, f32[32,128]{1,0:T(8,128)S(1)}, u32[]{:S(2)}, u32[]{:S(2)}) collective-permute-start(f32[32,128]{1,0:T(8,128)S(1)} %get-tuple-element.26), channel_id=1, source_target_pairs={{0,1},{1,0},{2,3},{3,2},{4,5},{5,4},{6,7},{7,6},{8,9},{9,8},{10,11... | collective-permute-start | bytes 49160 | tf_op jit(solution)/shard_map/ppermute | solution.py:264
  9.9 3.2 %collective-permute-start.5 = (f32[32,128]{1,0:T(8,128)S(1)}, f32[32,128]{1,0:T(8,128)S(1)}, u32[]{:S(2)}, u32[]{:S(2)}) collective-permute-start(f32[32,128]{1,0:T(8,128)S(1)} %add.13), channel_id=1, source_target_pairs={{0,9},{1,8},{2,11},{3,10},{4,13},{5,12},{6,15},{7,14},{8,1},{9,0},... | collective-permute-start | bytes 49160 | tf_op jit(solution)/shard_map/ppermute | solution.py:264
  13.0 4.1 %collective-permute-start.6 = (f32[32,128]{1,0:T(8,128)S(1)}, f32[32,128]{1,0:T(8,128)S(1)}, u32[]{:S(2)}, u32[]{:S(2)}) collective-permute-start(f32[32,128]{1,0:T(8,128)S(1)} %add.14), channel_id=1, source_target_pairs={{0,17},{1,16},{2,19},{3,18},{4,21},{5,20},{6,23},{7,22},{8,25},{9,... | collective-permute-start | bytes 49160 | tf_op jit(solution)/shard_map/ppermute | solution.py:264
  17.1 4.1 %collective-permute-start.9 = (f32[32,128]{1,0:T(8,128)S(1)}, f32[32,128]{1,0:T(8,128)S(1)}, u32[]{:S(2)}, u32[]{:S(2)}) collective-permute-start(f32[32,128]{1,0:T(8,128)S(1)} %add.15.refs_0_), channel_id=1, source_target_pairs={{0,7},{1,6},{2,5},{3,4},{4,3},{5,2},{6,1},{7,0},{8,15},{9,14},{10,... | collective-permute-start | bytes 49160 | tf_op jit(solution)/shard_map/ppermute | solution.py:264
  19.1 3.2 %collective-permute-start.8 = (f32[32,128]{1,0:T(8,128)S(1)}, f32[32,128]{1,0:T(8,128)S(1)}, u32[]{:S(2)}, u32[]{:S(2)}) collective-permute-start(f32[32,128]{1,0:T(8,128)S(1)} %add.15.refs_0_), channel_id=1, source_target_pairs={{0,3},{1,2},{2,1},{3,0},{4,7},{5,6},{6,5},{7,4},{8,11},{9,10},{10,... | collective-permute-start | bytes 49160 | tf_op jit(solution)/shard_map/ppermute | solution.py:264
  19.1 3.2 %collective-permute-start.7 = (f32[32,128]{1,0:T(8,128)S(1)}, f32[32,128]{1,0:T(8,128)S(1)}, u32[]{:S(2)}, u32[]{:S(2)}) collective-permute-start(f32[32,128]{1,0:T(8,128)S(1)} %add.15.refs_0_), channel_id=1, source_target_pairs={{0,5},{1,4},{2,7},{3,6},{4,1},{5,0},{6,3},{7,2},{8,13},{9,12},{10,... | collective-permute-start | bytes 49160 | tf_op jit(solution)/shard_map/ppermute | solution.py:264

commit v8 on v7

--- a/solution.py
+++ b/solution.py
@@ -126,8 +126,11 @@
                 outside = outside | other_outside
             picks = [(slot, index, outside)]
         for slot, index, outside in picks:
-            index = jnp.where(outside, jnp.where(index < REACH, index, index - REACH - count), REACH)
-            total += rank_dot(halo[index], affinity_ref[row, slot], (1, 1))
+            index = jnp.where(index < REACH, index, index - REACH - count)
+            picked = jnp.zeros_like(halo[0])
+            for b in range(REACH):
+                picked = jnp.where(outside & (index == b), halo[b], picked)
+            total += rank_dot(picked, affinity_ref[row, slot], (1, 1))
         root = [inverse_root(degrees_ref, row * pieces + c) for c in range(pieces)]
         images.append(split(total * jnp.concatenate(root, axis=1)))
     placed = [jnp.where(left, near, far) for near, far in zip(images, images[::-1])]
@@ -135,10 +138,8 @@
 
 
 def near_kernel(count, block, place_ref, columns_ref, degrees_ref, *refs):
-    near_refs, (affinity_ref, partial_ref, own_gram_ref, image_ref, gram_ref, halo) = refs[:REACH], refs[REACH:]
-    for b in range(REACH):
-        halo[b] = near_refs[b][...]
-    halo[REACH] = jnp.zeros_like(halo[0])
+    near_refs, (affinity_ref, partial_ref, own_gram_ref, image_ref, gram_ref) = refs[:REACH], refs[REACH:]
+    halo = [ref[...] for ref in near_refs]
     left = place_ref[0] % 2 == 1
     image, placed = side_images(count, block, left, place_ref, columns_ref, degrees_ref, affinity_ref, partial_ref, halo)
     image_ref[...] = placed
@@ -147,13 +148,13 @@
 
 def far_kernel(
     count, block, late, place_ref, columns_ref, degrees_ref, rest_ref, most_ref, affinity_ref, partial_ref, near_gram_ref,
-    image_ref, gram_ref, halo
+    image_ref, gram_ref
 ):
     is_late = (place_ref[0] == late[0]) | (place_ref[0] == late[1])
+    halo = []
     for b in range(REACH):
         columns = slice(b * block, (b + 1) * block)
-        halo[b] = jnp.where(is_late, rest_ref[:, columns], most_ref[:, columns])
-    halo[REACH] = jnp.zeros_like(halo[0])
+        halo.append(jnp.where(is_late, rest_ref[:, columns], most_ref[:, columns]))
     left = place_ref[0] % 2 == 0
     image, placed = side_images(count, block, left, place_ref, columns_ref, degrees_ref, affinity_ref, partial_ref, halo)
     image_ref[...] = placed
@@ -331,7 +332,6 @@
 
     side = dict(
         out_specs=(VMEM, VMEM),
-        scratch_shapes=[pltpu.VMEM((REACH + 1, rank, block), jnp.bfloat16)],
         compiler_params=PARAMS,
         cost_estimate=pl.CostEstimate(flops=1, bytes_accessed=1, transcendentals=0),
     )

time: 24.8 us -> 24.8 us (level)
  no operation moved by 1% of the time
where the time goes in v8:
time: 24.8 us; the launch traced here: 24.6 us
  starting transfers between devices  10.6 us (43%)
  waiting for transfers between devices  7.91 us (32%)
  Pallas kernels  5.98 us (24%)
    ppermute x6, starting transfers between devices, gram_parts(): lax.ppermute(gram, AXES, [(i, i ^ mask) for i in range(mesh_size)])  7.08 us
    ppermute x6, waiting for transfers between devices, gram_parts(): lax.ppermute(gram, AXES, [(i, i ^ mask) for i in range(mesh_size)])  6.23 us
    ppermute x2, starting transfers between devices, body(): lax.ppermute(far, AXES, pairs)  2.99 us
    pallas_call x1, Pallas kernels, body(): pl.pallas_call(functools.partial(targets_kernel, items * mesh_size, len(p...  2.33 us
    pallas_call x1, Pallas kernels, body(): pl.pallas_call(functools.partial(edges_kernel, width), out_shape=(pltpu.V...  1.19 us
    pallas_call x1, Pallas kernels, body(): pl.pallas_call(functools.partial(own_kernel, count, block, edges), out_sh...  1.1 us
    ppermute x2, waiting for transfers between devices, body(): lax.ppermute(x, AXES, [(i, i ^ 1) for i in range(mesh_size) if i ^ 1 < me...  0.87 us
    ppermute x2, waiting for transfers between devices, body(): lax.ppermute(far, AXES, pairs)  0.81 us
  transfers between devices with their start and end apart: 10, of which 8 were waited for; matrix products, arithmetic and copies ran while one was open for 0% of the time, Pallas kernels for 8%

profile of v8, /device:TPU:0, one launch (start us, length us, event | category | flops | bytes accessed | tf_op | source)
XLA Modules:
  0.0 24.6 jit_solution(919449430269136657)
XLA Ops:
  0.0 0.0 copy-start
  0.0 1.2 %edges.1 = (bf16[64,512]{1,0:T(8,128)(2,1)S(1)}, s32[3,8]{1,0:T(4,128)S(4)}, bf16[64,2048]{1,0:T(8,128)(2,1)S(1)}, s32[16,128]{1,0:T(8,128)S(1)}) custom-call(s32[1]{0:T(128)} %bitcast.place_ref, s32[3,8]{1,0:T(4,128)} %bitcast.7, bf16[64,2048]{1,0:T(8,128)(2,1)} %bitcast.5, s32[16,128]{1,0:T(8,128)} %bitcast.6), custom_call_target="tpu_custom_call" | custom-call | flops 1572864000 | bytes 62914560 | tf_op jit(solution)/shard_map/edges/pallas_call | solution.py:298
  1.2 3.0 %collective-permute-start.1 = (bf16[64,512]{1,0:T(8,128)(2,1)S(1)}, bf16[64,512]{1,0:T(8,128)(2,1)S(1)}, u32[]{:S(2)}, u32[]{:S(2)}) collective-permute-start(bf16[64,512]{1,0:T(8,128)(2,1)S(1)} %get-tuple-element.19), channel_id=1, source_target_pairs={{3,4},{4,3},{5,6},{6,5},{7,8},{8,7},{9,10},{10,9},{11,12},{12,11},... | collective-permute-start | bytes 196616 | tf_op jit(solution)/shard_map/ppermute | solution.py:313
  4.2 0.0 collective-permute-start
  4.2 0.0 copy-done
  4.2 1.1 %own.1 = (bf16[64,256]{1,0:T(8,128)(2,1)S(1)}, bf16[64,256]{1,0:T(8,128)(2,1)S(1)}, f32[64,2048]{1,0:T(8,128)S(1)}, f32[64,128]{1,0:T(8,128)S(1)}) custom-call(s32[1]{0:T(128)} %bitcast.place_ref, s32[3,8]{1,0:T(4,128)S(4)} %get-tuple-element.17.columns_ref, bf16[64,2048]{1,0:T(8,128)(2,1)S(1)} %get-tuple-element.20.basis_ref, ...), custom_call_target="tpu_custom_call" | custom-call | flops 201326592 | tf_op jit(solution)/shard_map/own/pallas_call | solution.py:315
  5.3 0.2 collective-permute-start.2
  5.5 0.3 %collective-permute-start.3 = (bf16[64,256]{1,0:T(8,128)(2,1)S(1)}, bf16[64,256]{1,0:T(8,128)(2,1)S(1)}, u32[]{:S(2)}, u32[]{:S(2)}) collective-permute-start(bf16[64,256]{1,0:T(8,128)(2,1)S(1)} %get-tuple-element.23), channel_id=1, source_target_pairs={{0,1},{1,0},{2,3},{3,2},{4,5},{5,4},{6,7},{7,6},{8,9},{9,8},{10,11... | collective-permute-start | bytes 98312 | tf_op jit(solution)/shard_map/ppermute | solution.py:331
  5.9 0.7 %collective-permute-done.2.refs_0_ = bf16[64,256]{1,0:T(8,128)(2,1)S(1)} collective-permute-done((bf16[64,256]{1,0:T(8,128)(2,1)S(1)}, bf16[64,256]{1,0:T(8,128)(2,1)S(1)}, u32[]{:S(2)}, u32[]{:S(2)}) %collective-permute-start.2) | collective-permute-done | bytes 32800 | tf_op jit(solution)/shard_map/ppermute | solution.py:331
  6.6 0.2 collective-permute-done.3.refs_1_
  6.7 0.0 copy-start.1
  6.7 0.5 %near.1 = (bf16[128,512]{1,0:T(8,128)(2,1)S(1)}, f32[64,128]{1,0:T(8,128)S(1)}) custom-call(s32[1]{0:T(128)} %bitcast.place_ref, s32[3,8]{1,0:T(4,128)S(4)} %get-tuple-element.17.columns_ref, s32[16,128]{1,0:T(8,128)S(1)} %get-tuple-element.18.degrees_ref, bf16[64,256]{1,0:T(8,128)(2,1)S(1)} %collective-permute-done.2.refs_0_, ...), custom_call_target="tpu_custom_call" | custom-call | flops 1 | bytes 1 | tf_op jit(solution)/shard_map/near/pallas_call | solution.py:339
  7.2 0.0 collective-permute-done.1.most_ref
  7.2 0.8 %collective-permute-done.rest_ref = bf16[64,512]{1,0:T(8,128)(2,1)S(1)} collective-permute-done((bf16[64,512]{1,0:T(8,128)(2,1)S(1)}, bf16[64,512]{1,0:T(8,128)(2,1)S(1)}, u32[]{:S(2)}, u32[]{:S(2)}) %collective-permute-start) | collective-permute-done | bytes 65568 | tf_op jit(solution)/shard_map/ppermute | solution.py:313
  8.0 0.5 %far.1 = (bf16[128,512]{1,0:T(8,128)(2,1)S(1)}, f32[32,128]{1,0:T(8,128)S(1)}) custom-call(s32[1]{0:T(128)} %bitcast.place_ref, s32[3,8]{1,0:T(4,128)S(4)} %get-tuple-element.17.columns_ref, s32[16,128]{1,0:T(8,128)S(1)} %get-tuple-element.18.degrees_ref, bf16[64,512]{1,0:T(8,128)(2,1)S(1)} %collective-permute-done.rest_ref, ...), custom_call_target="tpu_custom_call" | custom-call | flops 1 | bytes 1 | tf_op jit(solution)/shard_map/far/pallas_call | solution.py:346
  8.6 0.1 collective-permute-start.4
  8.7 1.2 %collective-permute-done.4 = f32[32,128]{1,0:T(8,128)S(1)} collective-permute-done((f32[32,128]{1,0:T(8,128)S(1)}, f32[32,128]{1,0:T(8,128)S(1)}, u32[]{:S(2)}, u32[]{:S(2)}) %collective-permute-start.4) | collective-permute-done | bytes 16416 | tf_op jit(solution)/shard_map/ppermute | solution.py:265
  9.9 1.5 %collective-permute-start.5 = (f32[32,128]{1,0:T(8,128)S(1)}, f32[32,128]{1,0:T(8,128)S(1)}, u32[]{:S(2)}, u32[]{:S(2)}) collective-permute-start(f32[32,128]{1,0:T(8,128)S(1)} %add.13), channel_id=1, source_target_pairs={{0,9},{1,8},{2,11},{3,10},{4,13},{5,12},{6,15},{7,14},{8,1},{9,0},... | collective-permute-start | bytes 49160 | tf_op jit(solution)/shard_map/ppermute | solution.py:265
  11.3 1.7 %collective-permute-done.5 = f32[32,128]{1,0:T(8,128)S(1)} collective-permute-done((f32[32,128]{1,0:T(8,128)S(1)}, f32[32,128]{1,0:T(8,128)S(1)}, u32[]{:S(2)}, u32[]{:S(2)}) %collective-permute-start.5) | collective-permute-done | bytes 16416 | tf_op jit(solution)/shard_map/ppermute | solution.py:265
  13.0 2.5 %collective-permute-start.6 = (f32[32,128]{1,0:T(8,128)S(1)}, f32[32,128]{1,0:T(8,128)S(1)}, u32[]{:S(2)}, u32[]{:S(2)}) collective-permute-start(f32[32,128]{1,0:T(8,128)S(1)} %add.14), channel_id=1, source_target_pairs={{0,17},{1,16},{2,19},{3,18},{4,21},{5,20},{6,23},{7,22},{8,25},{9,... | collective-permute-start | bytes 49160 | tf_op jit(solution)/shard_map/ppermute | solution.py:265
  15.5 1.6 %collective-permute-done.6 = f32[32,128]{1,0:T(8,128)S(1)} collective-permute-done((f32[32,128]{1,0:T(8,128)S(1)}, f32[32,128]{1,0:T(8,128)S(1)}, u32[]{:S(2)}, u32[]{:S(2)}) %collective-permute-start.6) | collective-permute-done | bytes 16416 | tf_op jit(solution)/shard_map/ppermute | solution.py:265
  17.1 2.0 %collective-permute-start.9 = (f32[32,128]{1,0:T(8,128)S(1)}, f32[32,128]{1,0:T(8,128)S(1)}, u32[]{:S(2)}, u32[]{:S(2)}) collective-permute-start(f32[32,128]{1,0:T(8,128)S(1)} %add.15.refs_0_), channel_id=1, source_target_pairs={{0,7},{1,6},{2,5},{3,4},{4,3},{5,2},{6,1},{7,0},{8,15},{9,14},{10,... | collective-permute-start | bytes 49160 | tf_op jit(solution)/shard_map/ppermute | solution.py:265
  19.1 0.0 collective-permute-start.8
  19.1 1.0 %collective-permute-start.7 = (f32[32,128]{1,0:T(8,128)S(1)}, f32[32,128]{1,0:T(8,128)S(1)}, u32[]{:S(2)}, u32[]{:S(2)}) collective-permute-start(f32[32,128]{1,0:T(8,128)S(1)} %add.15.refs_0_), channel_id=1, source_target_pairs={{0,5},{1,4},{2,7},{3,6},{4,1},{5,0},{6,3},{7,2},{8,13},{9,12},{10,... | collective-permute-start | bytes 49160 | tf_op jit(solution)/shard_map/ppermute | solution.py:265
  20.1 0.0 copy-done.1
  20.1 0.3 %reorder.1.refs_4_ = bf16[192,2048]{1,0:T(8,128)(2,1)S(1)} custom-call(s32[1]{0:T(128)} %bitcast.place_ref, f32[64,2048]{1,0:T(8,128)S(1)} %get-tuple-element.21.refs_3_.partial_ref.inner_ref, bf16[128,512]{1,0:T(8,128)(2,1)S(1)} %get-tuple-element.27.near_ref, bf16[128,512]{1,0:T(8,128)(2,1)S(1)} %get-tuple-element.28.far_ref, s32[8,256]{1,0:T(8,128)S(1)} %copy-done.1), custom_call_target="tpu_custom_call" | custom-call | flops 134217728 | tf_op jit(solution)/shard_map/reorder/pallas_call | solution.py:354
  20.5 0.7 %collective-permute-done.9.refs_3_ = f32[32,128]{1,0:T(8,128)S(1)} collective-permute-done((f32[32,128]{1,0:T(8,128)S(1)}, f32[32,128]{1,0:T(8,128)S(1)}, u32[]{:S(2)}, u32[]{:S(2)}) %collective-permute-start.9) | collective-permute-done | bytes 16416 | tf_op jit(solution)/shard_map/ppermute | solution.py:265
  21.2 1.1 %collective-permute-done.8.refs_2_ = f32[32,128]{1,0:T(8,128)S(1)} collective-permute-done((f32[32,128]{1,0:T(8,128)S(1)}, f32[32,128]{1,0:T(8,128)S(1)}, u32[]{:S(2)}, u32[]{:S(2)}) %collective-permute-start.8) | collective-permute-done | bytes 16416 | tf_op jit(solution)/shard_map/ppermute | solution.py:265
  22.3 0.0 collective-permute-done.7.refs_1_
  22.3 2.3 %targets.1 = f32[64,2048]{1,0:T(8,128)} custom-call(f32[32,128]{1,0:T(8,128)S(1)} %add.15.refs_0_, f32[32,128]{1,0:T(8,128)S(1)} %collective-permute-done.7.refs_1_, f32[32,128]{1,0:T(8,128)S(1)} %collective-permute-done.8.refs_2_, f32[32,128]{1,0:T(8,128)S(1)} %collective-permute-done.9.refs_3_, bf16[192,2048]{1,0:T(8,128)(2,1)S(1)} %reorder.1.refs_4_), custom_call_target="tpu_custom_call" | custom-call | tf_op jit(solution)/shard_map/targets/pallas_call | solution.py:365
  (3 shorter events, 0.0 us)
Async XLA Ops:
  0.0 4.2 %copy-start = (bf16[8,3,256,256]{3,2,1,0:T(8,128)(2,1)S(1)}, bf16[8,3,256,256]{3,2,1,0:T(8,128)(2,1)}, u32[]{:S(2)}) copy-start(bf16[8,3,256,256]{3,2,1,0:T(8,128)(2,1)} %affinity_ref.3) | copy-start | bytes 9437188
  1.2 6.0 %collective-permute-start.1 = (bf16[64,512]{1,0:T(8,128)(2,1)S(1)}, bf16[64,512]{1,0:T(8,128)(2,1)S(1)}, u32[]{:S(2)}, u32[]{:S(2)}) collective-permute-start(bf16[64,512]{1,0:T(8,128)(2,1)S(1)} %get-tuple-element.19), channel_id=1, source_target_pairs={{3,4},{4,3},{5,6},{6,5},{7,8},{8,7},{9,10},{10,9},{11,12},{12,11},... | collective-permute-start | bytes 196616 | tf_op jit(solution)/shard_map/ppermute | solution.py:313
  4.2 3.9 %collective-permute-start = (bf16[64,512]{1,0:T(8,128)(2,1)S(1)}, bf16[64,512]{1,0:T(8,128)(2,1)S(1)}, u32[]{:S(2)}, u32[]{:S(2)}) collective-permute-start(bf16[64,512]{1,0:T(8,128)(2,1)S(1)} %get-tuple-element.19), channel_id=1, source_target_pairs={{4,5},{5,4},{6,7},{7,6},{8,9},{9,8},{10,11},{11,10},{12,13},{13,12... | collective-permute-start | bytes 196616 | tf_op jit(solution)/shard_map/ppermute | solution.py:313
  5.3 1.3 %collective-permute-start.2 = (bf16[64,256]{1,0:T(8,128)(2,1)S(1)}, bf16[64,256]{1,0:T(8,128)(2,1)S(1)}, u32[]{:S(2)}, u32[]{:S(2)}) collective-permute-start(bf16[64,256]{1,0:T(8,128)(2,1)S(1)} %get-tuple-element.22), channel_id=1, source_target_pairs={{0,1},{1,0},{2,3},{3,2},{4,5},{5,4},{6,7},{7,6},{8,9},{9,8},{10,11... | collective-permute-start | bytes 98312 | tf_op jit(solution)/shard_map/ppermute | solution.py:331
  5.5 1.2 %collective-permute-start.3 = (bf16[64,256]{1,0:T(8,128)(2,1)S(1)}, bf16[64,256]{1,0:T(8,128)(2,1)S(1)}, u32[]{:S(2)}, u32[]{:S(2)}) collective-permute-start(bf16[64,256]{1,0:T(8,128)(2,1)S(1)} %get-tuple-element.23), channel_id=1, source_target_pairs={{0,1},{1,0},{2,3},{3,2},{4,5},{5,4},{6,7},{7,6},{8,9},{9,8},{10,11... | collective-permute-start | bytes 98312 | tf_op jit(solution)/shard_map/ppermute | solution.py:331
  6.7 13.4 %copy-start.1 = (s32[8,256]{1,0:T(8,128)S(1)}, s32[8,256]{1,0:T(8,128)}, u32[]{:S(2)}) copy-start(s32[8,256]{1,0:T(8,128)} %reorder_ref.1) | copy-start | bytes 24580
  8.6 1.2 %collective-permute-start.4 = (f32[32,128]{1,0:T(8,128)S(1)}, f32[32,128]{1,0:T(8,128)S(1)}, u32[]{:S(2)}, u32[]{:S(2)}) collective-permute-start(f32[32,128]{1,0:T(8,128)S(1)} %get-tuple-element.26), channel_id=1, source_target_pairs={{0,1},{1,0},{2,3},{3,2},{4,5},{5,4},{6,7},{7,6},{8,9},{9,8},{10,11... | collective-permute-start | bytes 49160 | tf_op jit(solution)/shard_map/ppermute | solution.py:265
  9.9 3.2 %collective-permute-start.5 = (f32[32,128]{1,0:T(8,128)S(1)}, f32[32,128]{1,0:T(8,128)S(1)}, u32[]{:S(2)}, u32[]{:S(2)}) collective-permute-start(f32[32,128]{1,0:T(8,128)S(1)} %add.13), channel_id=1, source_target_pairs={{0,9},{1,8},{2,11},{3,10},{4,13},{5,12},{6,15},{7,14},{8,1},{9,0},... | collective-permute-start | bytes 49160 | tf_op jit(solution)/shard_map/ppermute | solution.py:265
  13.0 4.1 %collective-permute-start.6 = (f32[32,128]{1,0:T(8,128)S(1)}, f32[32,128]{1,0:T(8,128)S(1)}, u32[]{:S(2)}, u32[]{:S(2)}) collective-permute-start(f32[32,128]{1,0:T(8,128)S(1)} %add.14), channel_id=1, source_target_pairs={{0,17},{1,16},{2,19},{3,18},{4,21},{5,20},{6,23},{7,22},{8,25},{9,... | collective-permute-start | bytes 49160 | tf_op jit(solution)/shard_map/ppermute | solution.py:265
  17.1 4.1 %collective-permute-start.9 = (f32[32,128]{1,0:T(8,128)S(1)}, f32[32,128]{1,0:T(8,128)S(1)}, u32[]{:S(2)}, u32[]{:S(2)}) collective-permute-start(f32[32,128]{1,0:T(8,128)S(1)} %add.15.refs_0_), channel_id=1, source_target_pairs={{0,7},{1,6},{2,5},{3,4},{4,3},{5,2},{6,1},{7,0},{8,15},{9,14},{10,... | collective-permute-start | bytes 49160 | tf_op jit(solution)/shard_map/ppermute | solution.py:265
  19.1 3.2 %collective-permute-start.8 = (f32[32,128]{1,0:T(8,128)S(1)}, f32[32,128]{1,0:T(8,128)S(1)}, u32[]{:S(2)}, u32[]{:S(2)}) collective-permute-start(f32[32,128]{1,0:T(8,128)S(1)} %add.15.refs_0_), channel_id=1, source_target_pairs={{0,3},{1,2},{2,1},{3,0},{4,7},{5,6},{6,5},{7,4},{8,11},{9,10},{10,... | collective-permute-start | bytes 49160 | tf_op jit(solution)/shard_map/ppermute | solution.py:265
  19.1 3.2 %collective-permute-start.7 = (f32[32,128]{1,0:T(8,128)S(1)}, f32[32,128]{1,0:T(8,128)S(1)}, u32[]{:S(2)}, u32[]{:S(2)}) collective-permute-start(f32[32,128]{1,0:T(8,128)S(1)} %add.15.refs_0_), channel_id=1, source_target_pairs={{0,5},{1,4},{2,7},{3,6},{4,1},{5,0},{6,3},{7,2},{8,13},{9,12},{10,... | collective-permute-start | bytes 49160 | tf_op jit(solution)/shard_map/ppermute | solution.py:265
